TPU v7x, 32 devices: a whole 2x2x4 slice. The times are simulated.
32 devices in a mesh: brick: 8 (over y, x, core), kvec: 4 (over z).
Axes of the slice: x: 2, y: 2, z: 4, core: 2. Of those that a mesh axis runs over, the one named last changes fastest.
Arguments:
- features: bfloat16 [8192, 256], P(('brick', 'kvec')), may hold values from -6 to 6
- positions: float32 [3, 8192], P(None, ('brick', 'kvec')), may hold values from 0 to 128, as said below
- neighbours: int32 [8192, 64], P(('brick', 'kvec')), may hold values from 0 to 383, as said below
- counts: int32 [8192], P(('brick', 'kvec')), may hold values from 32 to 64
- w_in: bfloat16 [2, 256, 256], replicated, may hold values from -0.375 to 0.375
- w_out: bfloat16 [2, 256, 256], replicated, may hold values from -0.375 to 0.375
- w_charge: float32 [256], replicated, may hold values from -0.375 to 0.375
- wave: float32 [3, 16384], replicated, may hold values from -3 to 3, as said below
Outputs:
- hidden_state: bfloat16 [8192, 256], P(('brick', 'kvec'))
- potential: float32 [8192], P(('brick', 'kvec'))
- field: float32 [3, 8192], P(None, ('brick', 'kvec'))
Inputs may be any that keep to these rules, and one draw needn't show every extreme that they name: `neighbours`: index e in row i names atom (i // 256) * 256 - 64 + e, which always exists and is never atom i itself; it lies within 64 rows of i. `positions`: atom i has first coordinate in [4 (i // 256), 4 (i // 256) + 4), growing with i; the other two lie in [0, 6]. `wave`: each component's magnitude lies in [0.3, 3].
All inputs are finite; a program needn't handle non-finite values.
Results may differ from a plain program's by a relative error of at most 0.0056.
Values may be sent and summed in bfloat16 or wider, within the bound.
No kernel may reach another device: no remote copies, remote signals or barrier semaphores. Data moves between devices by JAX's collectives and lax.ppermute only.
A program may use at most 192 MiB of HBM per device.

v0:
```python
import math

import jax
import jax.numpy as jnp
from jax import lax
from jax.sharding import PartitionSpec as P

LAYERS = 2
HALO = 64


def padded(x, sides, width):
    for axis, dim in sides:
        devices, length = (lax.axis_size(axis), x.shape[dim])
        up = [(i, (i + 1) % devices) for i in range(devices - 1)]
        down = [(j, i) for i, j in up]
        last = lax.slice_in_dim(x, length - width, length, axis=dim)
        initial = lax.slice_in_dim(x, 0, width, axis=dim)
        before = lax.ppermute(last, axis, up)
        after = lax.ppermute(initial, axis, down)
        x = jnp.concatenate([before, x, after], axis=dim)
    return x


def advance(hidden_block, extended, matrix, w_first, w_second):
    message = jnp.dot(matrix, extended.astype(jnp.float32), precision=lax.Precision.HIGHEST)
    normed = (
        message * lax.rsqrt(jnp.mean(message * message, axis=-1, keepdims=True) + 1e-05)
    ).astype(jnp.bfloat16)
    inner = jax.nn.silu(jnp.dot(normed, w_first, preferred_element_type=jnp.float32)).astype(
        jnp.bfloat16
    )
    update = jnp.dot(inner, w_second, preferred_element_type=jnp.float32)
    return (hidden_block.astype(jnp.float32) + update).astype(jnp.bfloat16)


def adjacency(coords, ext_coords, neighbours, counts):
    own, slots = neighbours.shape
    span = ext_coords.shape[1]
    group = math.gcd(8, slots)
    columns = jnp.arange(span, dtype=jnp.int32)
    offsets = jnp.arange(group, dtype=jnp.int32)

    def accumulate(index, matrix):
        start = index * group
        picked = lax.dynamic_slice_in_dim(neighbours, start, group, 1)
        onehot = (picked[:, :, None] == columns[None, None, :]).astype(jnp.float32)
        near = jnp.einsum("agk,ck->cag", onehot, ext_coords, precision=lax.Precision.HIGHEST)
        diff = near - coords[:, :, None]
        dist = jnp.sum(diff * diff, axis=0)
        live = (start + offsets)[None, :] < counts[:, None]
        weight = jnp.where(live, 1.0 / (1.0 + dist), jnp.zeros_like(dist))
        return matrix + jnp.einsum("agk,ag->ak", onehot, weight, precision=lax.Precision.HIGHEST)

    return lax.fori_loop(0, slots // group, accumulate, jnp.zeros((own, span), jnp.float32))


def phases(coords, tile):
    return (
        coords[0][:, None] * tile[0][None, :]
        + coords[1][:, None] * tile[1][None, :]
        + coords[2][:, None] * tile[2][None, :]
    )


def tile_width(total):
    return math.gcd(2048, total)


def structure(coords, charge, wave):
    total = wave.shape[1]
    width = tile_width(total)
    tiles = wave.reshape(3, total // width, width).transpose(1, 0, 2)

    def single(tile):
        angle = phases(coords, tile)
        cosine = jnp.cos(angle)
        sine = jnp.sin(angle)
        return (
            jnp.sum(charge[:, None] * cosine, axis=0),
            jnp.sum(charge[:, None] * sine, axis=0),
            cosine,
            sine,
        )

    cos_part, sin_part, cos_tiles, sin_tiles = lax.map(single, tiles)
    return (cos_part.reshape(total), sin_part.reshape(total), cos_tiles, sin_tiles)


def response(cos_tiles, sin_tiles, wave, cos_sum, sin_sum, factor):
    total = wave.shape[1]
    width = tile_width(total)
    ksq = jnp.sum(wave * wave, axis=0)
    coef = factor * jnp.exp(-0.1 * ksq) / ksq
    alpha_col = coef * cos_sum
    beta_col = coef * sin_sum
    with_cos = jnp.stack(
        [alpha_col, -wave[0] * beta_col, -wave[1] * beta_col, -wave[2] * beta_col], axis=1
    )
    with_sin = jnp.stack(
        [beta_col, wave[0] * alpha_col, wave[1] * alpha_col, wave[2] * alpha_col], axis=1
    )
    with_cos = with_cos.reshape(total // width, width, 4)
    with_sin = with_sin.reshape(total // width, width, 4)
    result = jnp.einsum("tak,tkc->ca", cos_tiles, with_cos, precision=lax.Precision.HIGHEST)
    result = result + jnp.einsum(
        "tak,tkc->ca", sin_tiles, with_sin, precision=lax.Precision.HIGHEST
    )
    return (result[0], result[1:4])


def per_device(features, positions, neighbours, counts, w_in, w_out, w_charge, wave):
    own = features.shape[0]
    ext_coords = padded(positions, ((("brick", "kvec"), 1),), HALO)
    matrix = adjacency(positions, ext_coords, neighbours, counts)
    hidden = features
    for layer_index in range(LAYERS):
        extended = padded(hidden, ((("brick", "kvec"), 0),), HALO)
        hidden = advance(hidden, extended, matrix, w_in[layer_index], w_out[layer_index])
    charge = jnp.dot(hidden.astype(jnp.float32), w_charge, precision=lax.Precision.HIGHEST)
    total = wave.shape[1]
    atoms_all = own * lax.axis_size("brick") * lax.axis_size("kvec")
    factor = 4.0 / math.sqrt(atoms_all * total)
    cos_part, sin_part, cos_tiles, sin_tiles = structure(positions, charge, wave)
    cos_sum, sin_sum = lax.psum((cos_part, sin_part), ("brick", "kvec"))
    potential, field = response(cos_tiles, sin_tiles, wave, cos_sum, sin_sum, factor)
    return (hidden, potential, field)


def solution(mesh):
    placed = (
        P(("brick", "kvec"), None),
        P(None, ("brick", "kvec")),
        P(("brick", "kvec"), None),
        P(("brick", "kvec")),
        P(),
        P(),
        P(),
        P(),
    )
    return jax.shard_map(
        per_device,
        mesh=mesh,
        in_specs=placed,
        out_specs=(P(("brick", "kvec"), None), P(("brick", "kvec")), P(None, ("brick", "kvec"))),
        check_vma=False,
    )
```

profile of v0, /device:TPU:0, one launch (start us, length us, event | category | flops | bytes accessed | tf_op | source)
XLA Modules:
  0.0 492.7 jit_solution(5917036249849347268)
XLA Ops:
  7.2 0.8 fusion.76
  8.0 4.9 collective-permute-start
  12.9 1.3 collective-permute-start.1
  14.2 0.8 fusion.74
  15.0 4.5 collective-permute-start.2
  19.6 1.3 collective-permute-start.3
  21.7 141.9 %while.31 = (s32[]{:T(128)}, f32[256,384]{1,0:T(8,128)S(1)}, s32[256,64]{0,1:T(8,128)}, s32[256]{0:T(256)}, f32[3,384]{1,0:T(4,128)S(1)}, /*index=5*/f32[3,256]{...) while((s32[]{:T(128)}, f32[256,384]{1,0:T(8,128)S(1)}, s32[256,64]{0,1:T(8,128)}, ...), condition=%wide.region_2.3_spmd.clone, body=%wide.region_0.2_spmd.clone.sunk | while | flops 39542796 | bytes 1794845 | solution.py:55
  21.7 0.8 constant_dynamic-slice_fusion.7
  22.6 14.2 %fusion.94 = f32[256,8,3]{1,2,0:T(4,128)S(1)} fusion(s32[256,8]{1,0:T(8,128)S(1)} %copy.25, f32[3,384]{1,0:T(4,128)S(1)} %get-tuple-element.410), kind=kOutput, calls=%fused_computation.13.clone.1 | convolution fusion | flops 29097984 | bytes 37376 | tf_op jit(solution)/shard_map/while/body/eval_jaxpr/agk,ck->cag/dot_general | solution.py:48
  37.2 2.2 fusion.96
  40.3 14.2 %fusion.94 = f32[256,8,3]{1,2,0:T(4,128)S(1)} fusion(s32[256,8]{1,0:T(8,128)S(1)} %copy.25, f32[3,384]{1,0:T(4,128)S(1)} %get-tuple-element.410), kind=kOutput, calls=%fused_computation.13.clone.1 | convolution fusion | flops 29097984 | bytes 37376 | tf_op jit(solution)/shard_map/while/body/eval_jaxpr/agk,ck->cag/dot_general | solution.py:48
  54.9 2.2 fusion.96
  58.1 14.2 %fusion.94 = f32[256,8,3]{1,2,0:T(4,128)S(1)} fusion(s32[256,8]{1,0:T(8,128)S(1)} %copy.25, f32[3,384]{1,0:T(4,128)S(1)} %get-tuple-element.410), kind=kOutput, calls=%fused_computation.13.clone.1 | convolution fusion | flops 29097984 | bytes 37376 | tf_op jit(solution)/shard_map/while/body/eval_jaxpr/agk,ck->cag/dot_general | solution.py:48
  72.6 2.2 fusion.96
  75.8 14.2 %fusion.94 = f32[256,8,3]{1,2,0:T(4,128)S(1)} fusion(s32[256,8]{1,0:T(8,128)S(1)} %copy.25, f32[3,384]{1,0:T(4,128)S(1)} %get-tuple-element.410), kind=kOutput, calls=%fused_computation.13.clone.1 | convolution fusion | flops 29097984 | bytes 37376 | tf_op jit(solution)/shard_map/while/body/eval_jaxpr/agk,ck->cag/dot_general | solution.py:48
  90.4 2.2 fusion.96
  93.5 14.2 %fusion.94 = f32[256,8,3]{1,2,0:T(4,128)S(1)} fusion(s32[256,8]{1,0:T(8,128)S(1)} %copy.25, f32[3,384]{1,0:T(4,128)S(1)} %get-tuple-element.410), kind=kOutput, calls=%fused_computation.13.clone.1 | convolution fusion | flops 29097984 | bytes 37376 | tf_op jit(solution)/shard_map/while/body/eval_jaxpr/agk,ck->cag/dot_general | solution.py:48
  108.1 2.2 fusion.96
  111.3 14.2 %fusion.94 = f32[256,8,3]{1,2,0:T(4,128)S(1)} fusion(s32[256,8]{1,0:T(8,128)S(1)} %copy.25, f32[3,384]{1,0:T(4,128)S(1)} %get-tuple-element.410), kind=kOutput, calls=%fused_computation.13.clone.1 | convolution fusion | flops 29097984 | bytes 37376 | tf_op jit(solution)/shard_map/while/body/eval_jaxpr/agk,ck->cag/dot_general | solution.py:48
  125.8 2.2 fusion.96
  129.0 14.2 %fusion.94 = f32[256,8,3]{1,2,0:T(4,128)S(1)} fusion(s32[256,8]{1,0:T(8,128)S(1)} %copy.25, f32[3,384]{1,0:T(4,128)S(1)} %get-tuple-element.410), kind=kOutput, calls=%fused_computation.13.clone.1 | convolution fusion | flops 29097984 | bytes 37376 | tf_op jit(solution)/shard_map/while/body/eval_jaxpr/agk,ck->cag/dot_general | solution.py:48
  143.5 2.2 fusion.96
  146.7 14.2 %fusion.94 = f32[256,8,3]{1,2,0:T(4,128)S(1)} fusion(s32[256,8]{1,0:T(8,128)S(1)} %copy.25, f32[3,384]{1,0:T(4,128)S(1)} %get-tuple-element.410), kind=kOutput, calls=%fused_computation.13.clone.1 | convolution fusion | flops 29097984 | bytes 37376 | tf_op jit(solution)/shard_map/while/body/eval_jaxpr/agk,ck->cag/dot_general | solution.py:48
  161.3 2.2 fusion.96
  164.5 4.5 collective-permute-start.4
  169.1 1.5 collective-permute-start.5
  170.7 4.1 collective-permute-done.5
  176.4 143.6 %while.30 = (s32[]{:T(128)}, f32[8,2048]{1,0:T(8,128)S(1)}, f32[8,2048]{1,0:T(8,128)S(1)}, f32[8,256,2048]{2,1,0:T(8,128)}, f32[8,256,2048]{2,1,0:T(8,128)}, /*i...) while((s32[]{:T(128)}, f32[8,2048]{1,0:T(8,128)S(1)}, ...), condition=%wide.region_9.10_spmd, body=%wide.region_6.0_spmd.sunk | while | flops 7335940 | bytes 4355745 | solution.py:86
  176.4 8.3 %multiply_reduce_fusion.6 = (f32[2048]{0:T(1024)S(1)}, f32[2048]{0:T(1024)S(1)}) fusion(f32[2048]{0:T(1024)S(1)} %bitcast.102, f32[256]{0:T(256)S(1)} %bitcast.121, f32[2048]{0:T(1024)S(1)} %bitcast.100, f32[256]{0:T(256)S(1)} %bitcast.123, f32[2048]{0:T(1024)S(1)} %bitcast.98, f32[256]{0:T(256)S(1)} %bitcast.119, f32[256]{0:T(256)S(1)} %get-tuple-element.445), kind=kLoop, calls=%fused_computation.5.clone.1 | loop fusion | flops 4714496 | bytes 45056 | tf_op jit(solution)/shard_map/while/body/eval_jaxpr/reduce_sum | solution.py:81
  185.2 9.2 %sine_dynamic-update-slice_fusion.2 = (f32[8,256,2048]{2,1,0:T(8,128)}, f32[8,256,2048]{2,1,0:T(8,128)}) fusion(f32[8,256,2048]{2,1,0:T(8,128)} %get-tuple-element.432, s32[]{:T(128)} %get-tuple-element.428, f32[2048]{0:T(1024)S(1)} %bitcast.103, f32[256]{0:T(256)S(1)} %bitcast.122, f32[2048]{0:T(1024)S(1)} %bitcast.101, f32[256]{0:T(256)S(1)} %bitcast.124, ...), kind=kLoop, calls=%fused_computation.2.clone.1 | loop fusion | flops 2621440 | bytes 4222464 | tf_op jit(solution)/shard_map/while/body/jit(dynamic_update_index_in_dim)/dynamic_update_slice | solution.py:86
  194.4 8.3 %multiply_reduce_fusion.6 = (f32[2048]{0:T(1024)S(1)}, f32[2048]{0:T(1024)S(1)}) fusion(f32[2048]{0:T(1024)S(1)} %bitcast.102, f32[256]{0:T(256)S(1)} %bitcast.121, f32[2048]{0:T(1024)S(1)} %bitcast.100, f32[256]{0:T(256)S(1)} %bitcast.123, f32[2048]{0:T(1024)S(1)} %bitcast.98, f32[256]{0:T(256)S(1)} %bitcast.119, f32[256]{0:T(256)S(1)} %get-tuple-element.445), kind=kLoop, calls=%fused_computation.5.clone.1 | loop fusion | flops 4714496 | bytes 45056 | tf_op jit(solution)/shard_map/while/body/eval_jaxpr/reduce_sum | solution.py:81
  203.1 9.2 %sine_dynamic-update-slice_fusion.2 = (f32[8,256,2048]{2,1,0:T(8,128)}, f32[8,256,2048]{2,1,0:T(8,128)}) fusion(f32[8,256,2048]{2,1,0:T(8,128)} %get-tuple-element.432, s32[]{:T(128)} %get-tuple-element.428, f32[2048]{0:T(1024)S(1)} %bitcast.103, f32[256]{0:T(256)S(1)} %bitcast.122, f32[2048]{0:T(1024)S(1)} %bitcast.101, f32[256]{0:T(256)S(1)} %bitcast.124, ...), kind=kLoop, calls=%fused_computation.2.clone.1 | loop fusion | flops 2621440 | bytes 4222464 | tf_op jit(solution)/shard_map/while/body/jit(dynamic_update_index_in_dim)/dynamic_update_slice | solution.py:86
  212.3 8.3 %multiply_reduce_fusion.6 = (f32[2048]{0:T(1024)S(1)}, f32[2048]{0:T(1024)S(1)}) fusion(f32[2048]{0:T(1024)S(1)} %bitcast.102, f32[256]{0:T(256)S(1)} %bitcast.121, f32[2048]{0:T(1024)S(1)} %bitcast.100, f32[256]{0:T(256)S(1)} %bitcast.123, f32[2048]{0:T(1024)S(1)} %bitcast.98, f32[256]{0:T(256)S(1)} %bitcast.119, f32[256]{0:T(256)S(1)} %get-tuple-element.445), kind=kLoop, calls=%fused_computation.5.clone.1 | loop fusion | flops 4714496 | bytes 45056 | tf_op jit(solution)/shard_map/while/body/eval_jaxpr/reduce_sum | solution.py:81
  221.0 9.2 %sine_dynamic-update-slice_fusion.2 = (f32[8,256,2048]{2,1,0:T(8,128)}, f32[8,256,2048]{2,1,0:T(8,128)}) fusion(f32[8,256,2048]{2,1,0:T(8,128)} %get-tuple-element.432, s32[]{:T(128)} %get-tuple-element.428, f32[2048]{0:T(1024)S(1)} %bitcast.103, f32[256]{0:T(256)S(1)} %bitcast.122, f32[2048]{0:T(1024)S(1)} %bitcast.101, f32[256]{0:T(256)S(1)} %bitcast.124, ...), kind=kLoop, calls=%fused_computation.2.clone.1 | loop fusion | flops 2621440 | bytes 4222464 | tf_op jit(solution)/shard_map/while/body/jit(dynamic_update_index_in_dim)/dynamic_update_slice | solution.py:86
  230.3 8.3 %multiply_reduce_fusion.6 = (f32[2048]{0:T(1024)S(1)}, f32[2048]{0:T(1024)S(1)}) fusion(f32[2048]{0:T(1024)S(1)} %bitcast.102, f32[256]{0:T(256)S(1)} %bitcast.121, f32[2048]{0:T(1024)S(1)} %bitcast.100, f32[256]{0:T(256)S(1)} %bitcast.123, f32[2048]{0:T(1024)S(1)} %bitcast.98, f32[256]{0:T(256)S(1)} %bitcast.119, f32[256]{0:T(256)S(1)} %get-tuple-element.445), kind=kLoop, calls=%fused_computation.5.clone.1 | loop fusion | flops 4714496 | bytes 45056 | tf_op jit(solution)/shard_map/while/body/eval_jaxpr/reduce_sum | solution.py:81
  239.0 9.2 %sine_dynamic-update-slice_fusion.2 = (f32[8,256,2048]{2,1,0:T(8,128)}, f32[8,256,2048]{2,1,0:T(8,128)}) fusion(f32[8,256,2048]{2,1,0:T(8,128)} %get-tuple-element.432, s32[]{:T(128)} %get-tuple-element.428, f32[2048]{0:T(1024)S(1)} %bitcast.103, f32[256]{0:T(256)S(1)} %bitcast.122, f32[2048]{0:T(1024)S(1)} %bitcast.101, f32[256]{0:T(256)S(1)} %bitcast.124, ...), kind=kLoop, calls=%fused_computation.2.clone.1 | loop fusion | flops 2621440 | bytes 4222464 | tf_op jit(solution)/shard_map/while/body/jit(dynamic_update_index_in_dim)/dynamic_update_slice | solution.py:86
  248.2 8.3 %multiply_reduce_fusion.6 = (f32[2048]{0:T(1024)S(1)}, f32[2048]{0:T(1024)S(1)}) fusion(f32[2048]{0:T(1024)S(1)} %bitcast.102, f32[256]{0:T(256)S(1)} %bitcast.121, f32[2048]{0:T(1024)S(1)} %bitcast.100, f32[256]{0:T(256)S(1)} %bitcast.123, f32[2048]{0:T(1024)S(1)} %bitcast.98, f32[256]{0:T(256)S(1)} %bitcast.119, f32[256]{0:T(256)S(1)} %get-tuple-element.445), kind=kLoop, calls=%fused_computation.5.clone.1 | loop fusion | flops 4714496 | bytes 45056 | tf_op jit(solution)/shard_map/while/body/eval_jaxpr/reduce_sum | solution.py:81
  257.0 9.2 %sine_dynamic-update-slice_fusion.2 = (f32[8,256,2048]{2,1,0:T(8,128)}, f32[8,256,2048]{2,1,0:T(8,128)}) fusion(f32[8,256,2048]{2,1,0:T(8,128)} %get-tuple-element.432, s32[]{:T(128)} %get-tuple-element.428, f32[2048]{0:T(1024)S(1)} %bitcast.103, f32[256]{0:T(256)S(1)} %bitcast.122, f32[2048]{0:T(1024)S(1)} %bitcast.101, f32[256]{0:T(256)S(1)} %bitcast.124, ...), kind=kLoop, calls=%fused_computation.2.clone.1 | loop fusion | flops 2621440 | bytes 4222464 | tf_op jit(solution)/shard_map/while/body/jit(dynamic_update_index_in_dim)/dynamic_update_slice | solution.py:86
  266.2 8.3 %multiply_reduce_fusion.6 = (f32[2048]{0:T(1024)S(1)}, f32[2048]{0:T(1024)S(1)}) fusion(f32[2048]{0:T(1024)S(1)} %bitcast.102, f32[256]{0:T(256)S(1)} %bitcast.121, f32[2048]{0:T(1024)S(1)} %bitcast.100, f32[256]{0:T(256)S(1)} %bitcast.123, f32[2048]{0:T(1024)S(1)} %bitcast.98, f32[256]{0:T(256)S(1)} %bitcast.119, f32[256]{0:T(256)S(1)} %get-tuple-element.445), kind=kLoop, calls=%fused_computation.5.clone.1 | loop fusion | flops 4714496 | bytes 45056 | tf_op jit(solution)/shard_map/while/body/eval_jaxpr/reduce_sum | solution.py:81
  274.9 9.2 %sine_dynamic-update-slice_fusion.2 = (f32[8,256,2048]{2,1,0:T(8,128)}, f32[8,256,2048]{2,1,0:T(8,128)}) fusion(f32[8,256,2048]{2,1,0:T(8,128)} %get-tuple-element.432, s32[]{:T(128)} %get-tuple-element.428, f32[2048]{0:T(1024)S(1)} %bitcast.103, f32[256]{0:T(256)S(1)} %bitcast.122, f32[2048]{0:T(1024)S(1)} %bitcast.101, f32[256]{0:T(256)S(1)} %bitcast.124, ...), kind=kLoop, calls=%fused_computation.2.clone.1 | loop fusion | flops 2621440 | bytes 4222464 | tf_op jit(solution)/shard_map/while/body/jit(dynamic_update_index_in_dim)/dynamic_update_slice | solution.py:86
  284.2 8.3 %multiply_reduce_fusion.6 = (f32[2048]{0:T(1024)S(1)}, f32[2048]{0:T(1024)S(1)}) fusion(f32[2048]{0:T(1024)S(1)} %bitcast.102, f32[256]{0:T(256)S(1)} %bitcast.121, f32[2048]{0:T(1024)S(1)} %bitcast.100, f32[256]{0:T(256)S(1)} %bitcast.123, f32[2048]{0:T(1024)S(1)} %bitcast.98, f32[256]{0:T(256)S(1)} %bitcast.119, f32[256]{0:T(256)S(1)} %get-tuple-element.445), kind=kLoop, calls=%fused_computation.5.clone.1 | loop fusion | flops 4714496 | bytes 45056 | tf_op jit(solution)/shard_map/while/body/eval_jaxpr/reduce_sum | solution.py:81
  292.9 9.2 %sine_dynamic-update-slice_fusion.2 = (f32[8,256,2048]{2,1,0:T(8,128)}, f32[8,256,2048]{2,1,0:T(8,128)}) fusion(f32[8,256,2048]{2,1,0:T(8,128)} %get-tuple-element.432, s32[]{:T(128)} %get-tuple-element.428, f32[2048]{0:T(1024)S(1)} %bitcast.103, f32[256]{0:T(256)S(1)} %bitcast.122, f32[2048]{0:T(1024)S(1)} %bitcast.101, f32[256]{0:T(256)S(1)} %bitcast.124, ...), kind=kLoop, calls=%fused_computation.2.clone.1 | loop fusion | flops 2621440 | bytes 4222464 | tf_op jit(solution)/shard_map/while/body/jit(dynamic_update_index_in_dim)/dynamic_update_slice | solution.py:86
  302.1 8.3 %multiply_reduce_fusion.6 = (f32[2048]{0:T(1024)S(1)}, f32[2048]{0:T(1024)S(1)}) fusion(f32[2048]{0:T(1024)S(1)} %bitcast.102, f32[256]{0:T(256)S(1)} %bitcast.121, f32[2048]{0:T(1024)S(1)} %bitcast.100, f32[256]{0:T(256)S(1)} %bitcast.123, f32[2048]{0:T(1024)S(1)} %bitcast.98, f32[256]{0:T(256)S(1)} %bitcast.119, f32[256]{0:T(256)S(1)} %get-tuple-element.445), kind=kLoop, calls=%fused_computation.5.clone.1 | loop fusion | flops 4714496 | bytes 45056 | tf_op jit(solution)/shard_map/while/body/eval_jaxpr/reduce_sum | solution.py:81
  310.8 9.2 %sine_dynamic-update-slice_fusion.2 = (f32[8,256,2048]{2,1,0:T(8,128)}, f32[8,256,2048]{2,1,0:T(8,128)}) fusion(f32[8,256,2048]{2,1,0:T(8,128)} %get-tuple-element.432, s32[]{:T(128)} %get-tuple-element.428, f32[2048]{0:T(1024)S(1)} %bitcast.103, f32[256]{0:T(256)S(1)} %bitcast.122, f32[2048]{0:T(1024)S(1)} %bitcast.101, f32[256]{0:T(256)S(1)} %bitcast.124, ...), kind=kLoop, calls=%fused_computation.2.clone.1 | loop fusion | flops 2621440 | bytes 4222464 | tf_op jit(solution)/shard_map/while/body/jit(dynamic_update_index_in_dim)/dynamic_update_slice | solution.py:86
  321.5 132.1 %all-reduce.3.cloned.1.call-done = (f32[16384]{0:T(1024)}, f32[16384]{0:T(1024)}) async-done(((f32[16384]{0:T(1024)}, f32[16384]{0:T(1024)}), (f32[16384]{0:T(1024)}, f32[16384]{0:T(1024)})) %all-reduce.3.cloned.1.call-update) | async-done | bytes 131088 | tf_op jit(solution)/shard_map/psum | solution.py:125
  453.6 0.9 fusion.68
  454.5 16.9 %convolution_bitcast_fusion.1 = f32[4,256]{1,0:T(4,128)S(1)} fusion(f32[8,256,2048]{2,1,0:T(8,128)} %get-tuple-element.190, f32[8,2048,1]{1,2,0:T(1,128)S(1)} %bitcast.110, f32[8,2048,1]{1,2,0:T(1,128)S(1)} %bitcast.111, f32[8,2048,1]{1,2,0:T(1,128)S(1)} %bitcast.107, f32[8,2048,1]{1,2,0:T(1,128)S(1)} %bitcast.105), kind=kOutput, calls=%fused_computation.30 | convolution fusion | flops 201523200 | bytes 17043456 | tf_op jit(solution)/shard_map/tak,tkc->ca/dot_general | solution.py:105
  471.5 13.2 %fusion.13 = f32[4,256]{1,0:T(4,128)S(1)} fusion(f32[4,256]{1,0:T(4,128)S(1)} %convolution_bitcast_fusion.1, f32[8,256,2048]{2,1,0:T(8,128)S(1)} %copy-done.1, f32[8,2048,1]{1,2,0:T(1,128)S(1)} %bitcast.109, f32[8,2048,1]{1,2,0:T(1,128)S(1)} %bitcast.108, f32[8,2048,1]{1,2,0:T(1,128)S(1)} %bitcast.106, f32[8,2048,1]{1,2,0:T(1,128)S(1)} %bitcast.104), kind=kOutput, calls=%fused_computation.29 | convolution fusion | flops 201524224 | bytes 17047552 | tf_op jit(solution)/shard_map/tak,tkc->ca/dot_general | solution.py:106
  (171 shorter events, 19.0 us)
Async XLA Ops:
  7.2 168.6 %copy-start = (f32[256]{0:T(256)S(1)}, f32[256]{0:T(256)}, u32[]{:S(2)}) copy-start(f32[256]{0:T(256)} %param.18) | copy-start | bytes 3076
  7.2 446.4 %all-reduce.3.cloned.1.call-start = ((), (), s32[]{:S(2)}) async-start(), calls=%async_computation | async-start | bytes 262144 | tf_op jit(solution)/shard_map/psum | solution.py:125
  8.0 12.9 %collective-permute-start = (f32[3,64]{1,0:T(4,128)S(1)}, f32[3,64]{1,0:T(4,128)S(1)}, u32[]{:S(2)}, u32[]{:S(2)}) collective-permute-start(f32[3,64]{1,0:T(4,128)S(1)} %get-tuple-element.274), channel_id=1, source_target_pairs={{0,1},{1,2},{2,3},{3,4},{4,5},{5,6},{6,7},{7,8},{8,9},{9,10},{10,1... | collective-permute-start | bytes 2312 | tf_op jit(solution)/shard_map/ppermute | solution.py:19
  12.9 8.0 %collective-permute-start.1 = (f32[3,64]{1,0:T(4,128)S(1)}, f32[3,64]{1,0:T(4,128)S(1)}, u32[]{:S(2)}, u32[]{:S(2)}) collective-permute-start(f32[3,64]{1,0:T(4,128)S(1)} %get-tuple-element.275), channel_id=1, source_target_pairs={{1,0},{2,1},{3,2},{4,3},{5,4},{6,5},{7,6},{8,7},{9,8},{10,9},{11,1... | collective-permute-start | bytes 2312 | tf_op jit(solution)/shard_map/ppermute | solution.py:20
  15.0 148.6 %collective-permute-start.2 = (bf16[64,256]{1,0:T(8,128)(2,1)S(1)}, bf16[64,256]{1,0:T(8,128)(2,1)S(1)}, u32[]{:S(2)}, u32[]{:S(2)}) collective-permute-start(bf16[64,256]{1,0:T(8,128)(2,1)S(1)} %get-tuple-element.268), channel_id=1, source_target_pairs={{0,1},{1,2},{2,3},{3,4},{4,5},{5,6},{6,7},{7,8},{8,9},{9,10},{10,1... | collective-permute-start | bytes 98312 | tf_op jit(solution)/shard_map/ppermute | solution.py:19
  19.6 144.0 %collective-permute-start.3 = (bf16[64,256]{1,0:T(8,128)(2,1)S(1)}, bf16[64,256]{1,0:T(8,128)(2,1)S(1)}, u32[]{:S(2)}, u32[]{:S(2)}) collective-permute-start(bf16[64,256]{1,0:T(8,128)(2,1)S(1)} %get-tuple-element.269), channel_id=1, source_target_pairs={{1,0},{2,1},{3,2},{4,3},{5,4},{6,5},{7,6},{8,7},{9,8},{10,9},{11,1... | collective-permute-start | bytes 98312 | tf_op jit(solution)/shard_map/ppermute | solution.py:20
  21.6 142.0 %copy-start.5 = (bf16[256,256]{1,0:T(8,128)(2,1)S(1)}, bf16[256,256]{1,0:T(8,128)(2,1)}, u32[]{:S(2)}) copy-start(bf16[256,256]{1,0:T(8,128)(2,1)} %param.12) | copy-start | bytes 393220
  21.6 142.4 %copy-start.8 = (bf16[2,256,256]{2,1,0:T(8,128)(2,1)S(1)}, bf16[2,256,256]{2,1,0:T(8,128)(2,1)}, u32[]{:S(2)}) copy-start(bf16[2,256,256]{2,1,0:T(8,128)(2,1)} %param.17) | copy-start | bytes 786436
  21.6 142.4 %copy-start.9 = (bf16[2,256,256]{2,1,0:T(8,128)(2,1)S(1)}, bf16[2,256,256]{2,1,0:T(8,128)(2,1)}, u32[]{:S(2)}) copy-start(bf16[2,256,256]{2,1,0:T(8,128)(2,1)} %param.16) | copy-start | bytes 786436
  21.7 15.3 %copy-start.3 = (f32[3,256]{1,0:T(4,128)S(1)}, f32[3,256]{1,0:T(4,128)}, u32[]{:S(2)}) copy-start(f32[3,256]{1,0:T(4,128)} %get-tuple-element.411) | copy-start | bytes 9220 | tf_op jit(solution)/shard_map/while
  21.7 15.3 %copy-start.7 = (s32[256]{0:T(256)S(1)}, s32[256]{0:T(256)}, u32[]{:S(2)}) copy-start(s32[256]{0:T(256)} %get-tuple-element.409) | copy-start | bytes 3076 | tf_op jit(solution)/shard_map/while
  39.5 15.2 %copy-start.3 = (f32[3,256]{1,0:T(4,128)S(1)}, f32[3,256]{1,0:T(4,128)}, u32[]{:S(2)}) copy-start(f32[3,256]{1,0:T(4,128)} %get-tuple-element.411) | copy-start | bytes 9220 | tf_op jit(solution)/shard_map/while
  39.5 15.2 %copy-start.7 = (s32[256]{0:T(256)S(1)}, s32[256]{0:T(256)}, u32[]{:S(2)}) copy-start(s32[256]{0:T(256)} %get-tuple-element.409) | copy-start | bytes 3076 | tf_op jit(solution)/shard_map/while
  57.2 15.2 %copy-start.3 = (f32[3,256]{1,0:T(4,128)S(1)}, f32[3,256]{1,0:T(4,128)}, u32[]{:S(2)}) copy-start(f32[3,256]{1,0:T(4,128)} %get-tuple-element.411) | copy-start | bytes 9220 | tf_op jit(solution)/shard_map/while
  57.2 15.2 %copy-start.7 = (s32[256]{0:T(256)S(1)}, s32[256]{0:T(256)}, u32[]{:S(2)}) copy-start(s32[256]{0:T(256)} %get-tuple-element.409) | copy-start | bytes 3076 | tf_op jit(solution)/shard_map/while
  74.9 15.2 %copy-start.3 = (f32[3,256]{1,0:T(4,128)S(1)}, f32[3,256]{1,0:T(4,128)}, u32[]{:S(2)}) copy-start(f32[3,256]{1,0:T(4,128)} %get-tuple-element.411) | copy-start | bytes 9220 | tf_op jit(solution)/shard_map/while
  74.9 15.2 %copy-start.7 = (s32[256]{0:T(256)S(1)}, s32[256]{0:T(256)}, u32[]{:S(2)}) copy-start(s32[256]{0:T(256)} %get-tuple-element.409) | copy-start | bytes 3076 | tf_op jit(solution)/shard_map/while
  92.7 15.2 %copy-start.3 = (f32[3,256]{1,0:T(4,128)S(1)}, f32[3,256]{1,0:T(4,128)}, u32[]{:S(2)}) copy-start(f32[3,256]{1,0:T(4,128)} %get-tuple-element.411) | copy-start | bytes 9220 | tf_op jit(solution)/shard_map/while
  92.7 15.2 %copy-start.7 = (s32[256]{0:T(256)S(1)}, s32[256]{0:T(256)}, u32[]{:S(2)}) copy-start(s32[256]{0:T(256)} %get-tuple-element.409) | copy-start | bytes 3076 | tf_op jit(solution)/shard_map/while
  110.4 15.2 %copy-start.3 = (f32[3,256]{1,0:T(4,128)S(1)}, f32[3,256]{1,0:T(4,128)}, u32[]{:S(2)}) copy-start(f32[3,256]{1,0:T(4,128)} %get-tuple-element.411) | copy-start | bytes 9220 | tf_op jit(solution)/shard_map/while
  110.4 15.2 %copy-start.7 = (s32[256]{0:T(256)S(1)}, s32[256]{0:T(256)}, u32[]{:S(2)}) copy-start(s32[256]{0:T(256)} %get-tuple-element.409) | copy-start | bytes 3076 | tf_op jit(solution)/shard_map/while
  128.1 15.2 %copy-start.3 = (f32[3,256]{1,0:T(4,128)S(1)}, f32[3,256]{1,0:T(4,128)}, u32[]{:S(2)}) copy-start(f32[3,256]{1,0:T(4,128)} %get-tuple-element.411) | copy-start | bytes 9220 | tf_op jit(solution)/shard_map/while
  128.1 15.2 %copy-start.7 = (s32[256]{0:T(256)S(1)}, s32[256]{0:T(256)}, u32[]{:S(2)}) copy-start(s32[256]{0:T(256)} %get-tuple-element.409) | copy-start | bytes 3076 | tf_op jit(solution)/shard_map/while
  145.8 15.2 %copy-start.3 = (f32[3,256]{1,0:T(4,128)S(1)}, f32[3,256]{1,0:T(4,128)}, u32[]{:S(2)}) copy-start(f32[3,256]{1,0:T(4,128)} %get-tuple-element.411) | copy-start | bytes 9220 | tf_op jit(solution)/shard_map/while
  145.9 15.2 %copy-start.7 = (s32[256]{0:T(256)S(1)}, s32[256]{0:T(256)}, u32[]{:S(2)}) copy-start(s32[256]{0:T(256)} %get-tuple-element.409) | copy-start | bytes 3076 | tf_op jit(solution)/shard_map/while
  163.6 7.0 %copy-start.2 = (f32[3,16384]{1,0:T(4,128)S(1)}, f32[3,16384]{1,0:T(4,128)}, u32[]{:S(2)}) copy-start(f32[3,16384]{1,0:T(4,128)} %param.19) | copy-start | bytes 589828
  164.5 11.5 %copy-start.4 = (f32[3,256]{1,0:T(4,128)S(1)}, f32[3,256]{1,0:T(4,128)}, u32[]{:S(2)}) copy-start(f32[3,256]{1,0:T(4,128)} %get-tuple-element.457) | copy-start | bytes 9220
  164.5 6.2 %collective-permute-start.4 = (bf16[64,256]{1,0:T(8,128)(2,1)S(1)}, bf16[64,256]{1,0:T(8,128)(2,1)S(1)}, u32[]{:S(2)}, u32[]{:S(2)}) collective-permute-start(bf16[64,256]{1,0:T(8,128)(2,1)S(1)} %get-tuple-element.266), channel_id=1, source_target_pairs={{0,1},{1,2},{2,3},{3,4},{4,5},{5,6},{6,7},{7,8},{8,9},{9,10},{10,1... | collective-permute-start | bytes 98312 | tf_op jit(solution)/shard_map/ppermute | solution.py:19
  169.1 5.8 %collective-permute-start.5 = (bf16[64,256]{1,0:T(8,128)(2,1)S(1)}, bf16[64,256]{1,0:T(8,128)(2,1)S(1)}, u32[]{:S(2)}, u32[]{:S(2)}) collective-permute-start(bf16[64,256]{1,0:T(8,128)(2,1)S(1)} %get-tuple-element.267), channel_id=1, source_target_pairs={{1,0},{2,1},{3,2},{4,3},{5,4},{6,5},{7,6},{8,7},{9,8},{10,9},{11,1... | collective-permute-start | bytes 98312 | tf_op jit(solution)/shard_map/ppermute | solution.py:20
  175.7 0.7 copy-start.6
  454.5 17.0 %copy-start.1 = (f32[8,256,2048]{2,1,0:T(8,128)S(1)}, f32[8,256,2048]{2,1,0:T(8,128)}, u32[]{:S(2)}) copy-start(f32[8,256,2048]{2,1,0:T(8,128)} %get-tuple-element.191) | copy-start | bytes 50331652
Sparse Core Ops, SparseCore 0:
  321.4 132.1 all-reduce.2
where the time goes:
time: 494 us; the launch traced here: 493 us
  matrix products  163 us (33%)
  other arithmetic  143 us (29%)
  waiting for transfers between devices  136 us (28%)
  starting transfers between devices  18.1 us (4%)
  local copies, waits for them, and re-layouts  17.2 us (3%)
  between operations  14.3 us (3%)
    psum x1, waiting for transfers between devices, per_device(): cos_sum, sin_sum = lax.psum((cos_part, sin_part), ('brick', 'kvec'))  132 us
    dot_general x8, matrix products, accumulate(): jnp.einsum('agk,ck->cag', onehot, ext_coords, precision=lax.Precision.HIG...  113 us
    dynamic_update_slice x8, other arithmetic, structure(): cos_part, sin_part, cos_tiles, sin_tiles = lax.map(single, tiles)  73.5 us
    reduce_sum x8, other arithmetic, single(): jnp.sum(charge[:, None] * sine, axis=0)  66.3 us
    dot_general x8, matrix products, accumulate(): jnp.einsum('agk,ag->ak', onehot, weight, precision=lax.Precision.HIGHEST)  17.6 us
    dot_general x1, matrix products, response(): jnp.einsum('tak,tkc->ca', cos_tiles, with_cos, precision=lax.Precision.HI...  16.9 us
    ppermute x3, starting transfers between devices, padded(): before = lax.ppermute(last, axis, up)  14 us
    dot_general x1, matrix products, response(): jnp.einsum('tak,tkc->ca', sin_tiles, with_sin, precision=lax.Precision.HI...  13.2 us
  transfers between devices with their start and end apart: 7, of which 2 were waited for; matrix products, arithmetic and copies ran while one was open for 29% of the time, Pallas kernels for 0%

commit v1 on v0

v1 whole, which is shorter than its diff:
```python
import functools
import math

import jax
import jax.numpy as jnp
import numpy as np
from jax import lax
from jax.experimental import pallas as pl
from jax.experimental.pallas import tpu as pltpu
from jax.sharding import PartitionSpec as P

LAYERS = 2
HALO = 64
AXES = ("brick", "kvec")
LANES = 128
F32 = jnp.float32
BF16 = jnp.bfloat16

VMEM = pl.BlockSpec(memory_space=pltpu.VMEM)


def pieces(x):
    first = x.astype(BF16).astype(F32)
    rest = x - first
    second = rest.astype(BF16).astype(F32)
    return first, second, rest - second


def pack_kernel(feat_ref, pos_ref, neigh_ref, counts_ref, first_ref, last_ref):
    own, slots = neigh_ref.shape
    channels = feat_ref.shape[1]
    pos = pos_ref[...]
    count_row = counts_ref[...].astype(F32)
    hi, mid, lo = pieces(pos)
    zero5 = jnp.zeros((5, own), F32)
    stack = jnp.concatenate(
        [jnp.zeros((64, own), F32), hi, count_row, zero5[:4], mid, zero5, lo, zero5]
        + [jnp.zeros((40, own), F32)],
        axis=0,
    )
    columns = stack.T
    rows = lax.broadcasted_iota(jnp.int32, (own, slots), 0)
    slot = lax.broadcasted_iota(jnp.int32, (own, slots), 1).astype(F32)
    delta = (neigh_ref[...] - HALO - rows).astype(F32)
    delta = jnp.where(slot < columns[:, 67:68], delta, jnp.zeros_like(delta))
    wide = jnp.concatenate([delta, jnp.zeros((own, LANES - slots), F32)], axis=1)
    lane = lax.broadcasted_iota(jnp.int32, (own, LANES), 1)
    side = jnp.where(lane < slots, wide, columns).astype(BF16)
    half = own // 2
    for ref, start in ((first_ref, 0), (last_ref, half)):
        ref[:, :channels] = feat_ref[start : start + half, :]
        ref[:, channels:] = side[start : start + half, :]


def make_series():
    nodes = 400
    x = np.cos((np.arange(nodes) + 0.5) * np.pi / nodes)
    s = 0.125 * (x + 1.0)
    r = np.sqrt(s)

    def fitted(values, degree):
        cheb = np.polynomial.chebyshev.Chebyshev.fit(s, values, degree, domain=[0.0, 0.25])
        return [float(v) for v in cheb.convert(kind=np.polynomial.Polynomial).coef]

    root = math.sqrt(2.0)
    half_sine = fitted(root * np.sin(np.pi * r) / r, 3)
    half_cosine = fitted(root * np.cos(np.pi * r), 3)
    return half_sine, half_cosine


HALF_SINE, HALF_COSINE = make_series()


def horner(s, coefs):
    value = coefs[-1] * s + coefs[-2]
    for c in coefs[-3::-1]:
        value = value * s + c
    return value


def trig_kernel(pos_ref, wave_ref, cos_ref, sin_ref, left_ref, *, tile, chunk):
    own = pos_ref.shape[1]
    total = wave_ref.shape[1]
    zero5 = jnp.zeros((5, own), F32)
    a, b, c = (jnp.concatenate([p, zero5], axis=0) for p in pieces(pos_ref[...]))
    left = jnp.concatenate([a, a, b, b, a, c] + [jnp.zeros((80, own), F32)], axis=0)
    left_ref[...] = left.T.astype(BF16)
    tail5 = jnp.zeros((5, tile), F32)
    magic = 12582912.0

    @pl.loop(0, total // tile)
    def _(step):
        span = pl.ds(pl.multiple_of(step * tile, tile), tile)
        turns = wave_ref[:, span] * (0.5 / math.pi)
        u, v, w = (jnp.concatenate([p, tail5], axis=0) for p in pieces(turns))
        right = jnp.concatenate([u, v, u, v, w, u] + [jnp.zeros((80, tile), F32)], axis=0)
        right = right.astype(BF16)
        for start in range(0, own, chunk):
            t = jnp.dot(left_ref[start : start + chunk, :], right, preferred_element_type=F32)
            r = t - ((t + magic) - magic)
            s = r * r
            x = r * horner(s, HALF_SINE)
            y = horner(s, HALF_COSINE)
            cos_ref[start : start + chunk, span] = (1.0 - x * x).astype(BF16)
            sin_ref[start : start + chunk, span] = (x * y).astype(BF16)


def silu(x):
    return x / (1.0 + jnp.exp(-x))


def layer_kernel(
    before_ref, first_ref, last_ref, after_ref, w_in_ref, w_out_ref, w_charge_ref, cos_ref,
    sin_ref, hidden_ref, sums_ref, feat_ref, mid_ref, matrix_ref, *, tile,
):
    parts = (before_ref, first_ref, last_ref, after_ref)
    half, width = before_ref.shape
    channels = w_in_ref.shape[1]
    own = 2 * half
    pad = HALO
    for n, ref in enumerate(parts):
        feat_ref[n * half : (n + 1) * half, :] = ref[:, :channels]
    feat_ref[4 * half :, :] = jnp.zeros((pad, channels), BF16)
    sides = [ref[:, channels:].astype(F32) for ref in parts]
    flipped = [side.T for side in sides]
    rows = [f[64:72] + f[72:80] + f[80:88] for f in flipped]
    ext_rows = jnp.concatenate(rows + [jnp.zeros((8, LANES), F32)], axis=1)
    side_all = jnp.concatenate(sides, axis=0)
    lane = lax.broadcasted_iota(jnp.int32, (HALO, LANES), 1)
    lane_f = lane.astype(F32)
    blocks = (own + 2 * HALO) // HALO
    zeros = jnp.zeros((HALO, LANES), F32)
    for block in range(blocks):
        base = HALO * (block + 1)
        side = side_all[base : base + HALO, :]
        delta = side[:, :64]
        place = jnp.where(delta > 0, delta + 63.0, delta + 64.0)
        place = jnp.where(delta == 0, -1.0, place)
        hist = zeros
        for slot in range(64):
            hist = hist + jnp.where(lane_f == place[:, slot : slot + 1], 1.0, 0.0)
        low = jnp.concatenate([jnp.where(lane < 64, hist, 0.0), zeros], axis=1)
        high = jnp.concatenate([jnp.where(lane < 64, 0.0, hist), zeros], axis=1)
        counted = pltpu.roll(low, 0, 1, stride=1, stride_axis=0) + pltpu.roll(
            high, 1, 1, stride=1, stride_axis=0
        )
        dist = jnp.zeros((HALO, 2 * LANES), F32)
        for c in range(3):
            here = side[:, 64 + c : 65 + c] + side[:, 72 + c : 73 + c] + side[:, 80 + c : 81 + c]
            there = ext_rows[c : c + 1, HALO * block : HALO * block + 2 * LANES]
            diff = there - here
            dist = dist + diff * diff
        weight = counted / (1.0 + dist)
        upper = weight.astype(BF16)
        lower = (weight - upper.astype(F32)).astype(BF16)
        matrix_ref[block, :HALO, :] = upper
        matrix_ref[block, HALO:, :] = lower

    def advance(source_ref, layer, block_ids, row0, residual):
        messages = []
        for block in block_ids:
            start = HALO * (block - row0)
            out = jnp.dot(
                matrix_ref[block],
                source_ref[start : start + 2 * LANES, :],
                preferred_element_type=F32,
            )
            messages.append(out[:HALO] + out[HALO:])
        message = jnp.concatenate(messages, axis=0)
        scale = lax.rsqrt(jnp.mean(message * message, axis=-1, keepdims=True) + 1e-05)
        normed = (message * scale).astype(BF16)
        inner = silu(jnp.dot(normed, w_in_ref[layer], preferred_element_type=F32)).astype(BF16)
        update = jnp.dot(inner, w_out_ref[layer], preferred_element_type=F32)
        return (residual.astype(F32) + update).astype(BF16)

    grown = own + 2 * HALO
    mid_ref[:grown, :] = advance(
        feat_ref, 0, range(blocks), 0, feat_ref[HALO : HALO + grown, :]
    )
    mid_ref[grown:, :] = jnp.zeros((pad, channels), BF16)
    final = advance(mid_ref, 1, range(1, blocks - 1), 1, mid_ref[HALO : HALO + own, :])
    hidden_ref[...] = final
    reader = jnp.concatenate(
        list(pieces(w_charge_ref[...])) + [jnp.zeros((5, channels), F32)], axis=0
    ).astype(BF16)
    read = lax.dot_general(
        reader, final, (((1,), (1,)), ((), ())), preferred_element_type=F32
    )
    charge = read[0:1] + read[1:2] + read[2:3]
    hi, mid, lo = pieces(charge)
    charges = jnp.concatenate([hi, mid, lo, jnp.zeros((5, own), F32)], axis=0).astype(BF16)

    @pl.loop(0, sums_ref.shape[0])
    def _(step):
        span = pl.ds(pl.multiple_of(step * tile, tile), tile)
        for n, ref in enumerate((cos_ref, sin_ref)):
            part = jnp.dot(charges, ref[:, span], preferred_element_type=F32)
            sums_ref[step, n : n + 1, :] = part[0:1] + part[1:2] + part[2:3]


def response_kernel(sums_ref, wave_ref, cos_ref, sin_ref, pot_ref, field_ref, acc_ref, *, tile, factor):
    acc_ref[...] = jnp.zeros_like(acc_ref)
    lead = lax.broadcasted_iota(jnp.int32, (4, tile), 0) == 0
    dims = (((1,), (1,)), ((), ()))

    @pl.loop(0, sums_ref.shape[0])
    def _(step):
        span = pl.ds(pl.multiple_of(step * tile, tile), tile)
        wave = wave_ref[:, span]
        ksq = jnp.sum(wave * wave, axis=0, keepdims=True)
        coef = factor * jnp.exp(-0.1 * ksq) / ksq
        scaled = coef * jnp.concatenate([jnp.ones((1, tile), F32), wave], axis=0)
        sums = sums_ref[step]
        cosine = sums[0:1]
        sine = sums[1:2]
        for ref, top, other in ((cos_ref, cosine, -sine), (sin_ref, sine, cosine)):
            full = scaled * jnp.where(lead, top, other)
            hi = full.astype(BF16).astype(F32)
            both = jnp.concatenate([hi, full - hi], axis=0).astype(BF16)
            acc_ref[...] += lax.dot_general(
                both, ref[:, span], dims, preferred_element_type=F32
            )

    result = acc_ref[:4] + acc_ref[4:]
    pot_ref[...] = result[0:1]
    field_ref[...] = result[1:4]


def shifted(x, step):
    devices = lax.axis_size(AXES)
    pairs = [(i, i + step) for i in range(devices) if 0 <= i + step < devices]
    return lax.ppermute(x, AXES, pairs)


def per_device(features, positions, neighbours, counts, w_in, w_out, w_charge, wave):
    own, channels = features.shape
    total = wave.shape[1]
    devices = lax.axis_size(AXES)
    half = own // 2
    width = channels + LANES
    share = total // devices

    edge = jax.ShapeDtypeStruct((half, width), BF16)
    first, last = pl.pallas_call(
        pack_kernel,
        out_shape=(edge, edge),
        in_specs=[VMEM] * 4,
        out_specs=(VMEM, VMEM),
    )(features, positions, neighbours, counts.reshape(1, own))
    before = shifted(last, 1)
    after = shifted(first, -1)

    table = pltpu.VMEM((own, total), BF16)
    cosine, sine = pl.pallas_call(
        functools.partial(trig_kernel, tile=256, chunk=32),
        out_shape=(table, table),
        in_specs=[VMEM] * 2,
        out_specs=(VMEM, VMEM),
        scratch_shapes=[pltpu.VMEM((own, LANES), BF16)],
        compiler_params=pltpu.CompilerParams(vmem_limit_bytes=16 << 20),
        cost_estimate=pl.CostEstimate(
            flops=own * total * 40, bytes_accessed=4 * own * total, transcendentals=0
        ),
    )(positions, wave)

    hidden, partial = pl.pallas_call(
        functools.partial(layer_kernel, tile=share),
        out_shape=(
            jax.ShapeDtypeStruct((own, channels), BF16),
            jax.ShapeDtypeStruct((devices, 2, share), F32),
        ),
        in_specs=[VMEM] * 9,
        out_specs=(VMEM, VMEM),
        scratch_shapes=[
            pltpu.VMEM((4 * half + HALO, channels), BF16),
            pltpu.VMEM((own + 3 * HALO, channels), BF16),
            pltpu.VMEM((own // HALO + 2, 2 * HALO, 2 * LANES), BF16),
        ],
        compiler_params=pltpu.CompilerParams(vmem_limit_bytes=16 << 20),
    )(before, first, last, after, w_in, w_out, w_charge.reshape(1, channels), cosine, sine)

    swapped = lax.all_to_all(partial, AXES, 0, 0, tiled=True)
    mine = jnp.sum(swapped, axis=0)
    sums = lax.all_gather(mine, AXES)

    factor = 4.0 / math.sqrt(own * devices * total)
    potential, field = pl.pallas_call(
        functools.partial(response_kernel, tile=share, factor=factor),
        out_shape=(
            jax.ShapeDtypeStruct((1, own), F32),
            jax.ShapeDtypeStruct((3, own), F32),
        ),
        in_specs=[VMEM] * 4,
        out_specs=(VMEM, VMEM),
        scratch_shapes=[pltpu.VMEM((8, own), F32)],
        compiler_params=pltpu.CompilerParams(vmem_limit_bytes=16 << 20),
    )(sums, wave, cosine, sine)
    return (hidden, potential.reshape(own), field)


def solution(mesh):
    placed = (
        P(AXES, None),
        P(None, AXES),
        P(AXES, None),
        P(AXES),
        P(),
        P(),
        P(),
        P(),
    )
    return jax.shard_map(
        per_device,
        mesh=mesh,
        in_specs=placed,
        out_specs=(P(AXES, None), P(AXES), P(None, AXES)),
        check_vma=False,
    )
```

time: 494 us -> 148 us (0.30)
  matrix products: 163 us -> 0 us
  other arithmetic: 143 us -> 0.06 us
  waiting for transfers between devices: 136 us -> 0.01 us
  blocking collectives: 0 us -> 80.1 us
  Pallas kernels: 0 us -> 44.9 us
  between operations: 14.3 us -> 0.71 us
  starting transfers between devices: 18.1 us -> 6.21 us
    dot_general x23 -> x0, matrix products: 163 us -> none  [the longest x8 113 us: accumulate(): jnp.einsum('agk,ck->cag', onehot, ext_coords, precision=lax.Precision.HIG...]
    psum x1 -> x0, waiting for transfers between devices: 132 us -> none  [per_device(): cos_sum, sin_sum = lax.psum((cos_part, sin_part), ('brick', 'kvec'))]
    dynamic_update_slice x8 -> x0, other arithmetic: 73.5 us -> none  [structure(): cos_part, sin_part, cos_tiles, sin_tiles = lax.map(single, tiles)]
    reduce_sum x17 -> x1, other arithmetic: 66.6 us -> 0.06 us  [per_device(): mine = jnp.sum(swapped, axis=0)]
    all_gather x0 -> x1, blocking collectives: none -> 65 us  [per_device(): sums = lax.all_gather(mine, AXES)]
    pallas_call x0 -> x4, Pallas kernels: none -> 44.9 us  [the longest x1 21.1 us: per_device(): pl.pallas_call(functools.partial(trig_kernel, tile=256, chunk=32), out_sh...]
    all_to_all x0 -> x1, blocking collectives: none -> 15.1 us  [per_device(): swapped = lax.all_to_all(partial, AXES, 0, 0, tiled=True)]
    unnamed x18 -> x25, local copies, waits for them, and re-layouts: 1.79 us -> 15 us
  transfers between devices with their start and end apart: 7 -> 2, of which waited for: 2 -> 0; matrix products, arithmetic and copies ran while one was open for 29% -> 0% of each run, Pallas kernels for 0% -> 14%
where the time goes in v1:
time: 148 us; the launch traced here: 147 us
  blocking collectives  80.1 us (54%)
  Pallas kernels  44.9 us (30%)
  local copies, waits for them, and re-layouts  15 us (10%)
  starting transfers between devices  6.21 us (4%)
    all_gather x1, blocking collectives, per_device(): sums = lax.all_gather(mine, AXES)  65 us
    pallas_call x1, Pallas kernels, per_device(): pl.pallas_call(functools.partial(trig_kernel, tile=256, chunk=32), out_sh...  21.1 us
    all_to_all x1, blocking collectives, per_device(): swapped = lax.all_to_all(partial, AXES, 0, 0, tiled=True)  15.1 us
    unnamed x25, local copies, waits for them, and re-layouts  15 us
    pallas_call x1, Pallas kernels, per_device(): pl.pallas_call(functools.partial(layer_kernel, tile=share), out_shape=(ja...  13.2 us
    pallas_call x1, Pallas kernels, per_device(): pl.pallas_call(functools.partial(response_kernel, tile=share, factor=fact...  8.74 us
    ppermute x2, starting transfers between devices, shifted(): return lax.ppermute(x, AXES, pairs)  6.21 us
  transfers between devices with their start and end apart: 2, of which 0 were waited for; matrix products, arithmetic and copies ran while one was open for 0% of the time, Pallas kernels for 14%

profile of v1, /device:TPU:0, one launch (start us, length us, event | category | flops | bytes accessed | tf_op | source)
XLA Modules:
  0.0 147.0 jit_solution(1309378146588644032)
XLA Ops:
  0.6 1.6 %copy.12.neigh_ref = s32[256,64]{1,0:T(8,128)} copy(s32[256,64]{0,1:T(8,128)} %param.10) | data formatting | bytes 131072 | tf_op args[2]
  2.2 1.8 %shard_map.103 = (bf16[128,384]{1,0:T(8,128)(2,1)}, bf16[128,384]{1,0:T(8,128)(2,1)}) custom-call(bf16[256,256]{1,0:T(8,128)(2,1)} %feat_ref.1, f32[3,256]{1,0:T(4,128)} %pos_ref.3, s32[256,64]{1,0:T(8,128)} %copy.12.neigh_ref, s32[1,256]{1,0:T(1,128)} %bitcast.6), custom_call_target="tpu_custom_call" | custom-call | tf_op jit(solution)/shard_map/pallas_call | solution.py:244
  4.1 4.9 %collective-permute-start = (bf16[128,384]{1,0:T(8,128)(2,1)}, bf16[128,384]{1,0:T(8,128)(2,1)S(1)}, u32[]{:S(2)}, u32[]{:S(2)}) collective-permute-start(bf16[128,384]{1,0:T(8,128)(2,1)} %get-tuple-element.11.last_ref), channel_id=1, source_target_pairs={{0,1},{1,2},{2,3},{3,4},{4,5},{5,6},{6,7},{7,8},{8,9},{9,10},{10,1... | collective-permute-start | bytes 294920 | tf_op jit(solution)/shard_map/ppermute | solution.py:232
  9.0 1.3 collective-permute-start.1
  10.3 0.0 copy-start.6
  10.3 0.9 copy-done.6
  11.2 0.0 copy-start.10
  11.2 0.7 copy-done.10
  11.9 21.1 %shard_map.104 = (bf16[256,16384]{1,0:T(8,128)(2,1)S(1)}, bf16[256,16384]{1,0:T(8,128)(2,1)S(1)}) custom-call(f32[3,256]{1,0:T(4,128)S(1)} %copy-done.10, f32[3,16384]{1,0:T(4,128)S(1)} %copy-done.6), custom_call_target="tpu_custom_call" | custom-call | flops 167772160 | bytes 16777216 | tf_op jit(solution)/shard_map/pallas_call | solution.py:254
  33.0 0.0 copy-start
  33.0 0.0 copy-start.2
  33.1 0.0 collective-permute-done.before_ref
  33.1 0.0 collective-permute-done.1.after_ref
  33.1 0.0 copy-start.4
  33.1 1.1 copy-done.4
  34.2 0.0 copy-start.5
  34.2 1.2 copy-done.5
  35.4 0.0 copy-start.8
  35.4 1.0 copy-done.8
  36.4 0.0 copy-start.9
  36.4 1.0 copy-done.9
  37.4 0.0 copy-start.11
  37.4 0.7 copy-done.11
  38.1 0.0 copy-start.7
  38.1 13.2 %shard_map.105 = (bf16[256,256]{1,0:T(8,128)(2,1)}, f32[32,2,512]{2,1,0:T(2,128)S(1)}) custom-call(bf16[128,384]{1,0:T(8,128)(2,1)S(1)} %collective-permute-done.before_ref, bf16[128,384]{1,0:T(8,128)(2,1)S(1)} %copy-done.8, bf16[128,384]{1,0:T(8,128)(2,1)S(1)} %copy-done.9, bf16[128,384]{1,0:T(8,128)(2,1)S(1)} %collective-permute-done.1.after_ref, ...), custom_call_target="tpu_custom_call" | custom-call | tf_op jit(solution)/shard_map/pallas_call | solution.py:266
  51.3 0.0 copy-done
  51.3 0.0 copy-done.2
  51.3 15.1 %all_to_all.5 = f32[32,2,512]{2,1,0:T(2,128)S(1)} all-to-all(f32[32,2,512]{2,1,0:T(2,128)S(1)} %get-tuple-element.16), channel_id=1, replica_groups=mesh['brick'=8,'kvec'=4] {'brick','kvec'}, dimensions={0} | all-to-all | bytes 262144 | tf_op jit(solution)/shard_map/all_to_all | solution.py:282
  66.4 0.1 reduce_sum.9
  66.5 65.0 %all-gather.1.sums_ref = f32[32,2,512]{2,1,0:T(2,128)S(1)} all-gather(f32[1,2,512]{2,1,0:T(2,128)S(1)} %bitcast.5), channel_id=2, replica_groups=mesh['brick'=8,'kvec'=4] {'brick','kvec'}, dimensions={0}, use_global_device_ids=true | all-gather | bytes 135168 | tf_op jit(solution)/shard_map/all_gather | solution.py:284
  131.5 0.0 copy-done.7
  131.5 0.0 copy-start.1
  131.5 3.4 %copy-done.1 = bf16[256,16384]{1,0:T(8,128)(2,1)S(1)} copy-done((bf16[256,16384]{1,0:T(8,128)(2,1)S(1)}, bf16[256,16384]{1,0:T(8,128)(2,1)}, u32[]{:S(2)}) %copy-start.1) | copy-done | bytes 8388632
  134.9 0.0 copy-start.3
  134.9 3.4 %copy-done.3 = bf16[256,16384]{1,0:T(8,128)(2,1)S(1)} copy-done((bf16[256,16384]{1,0:T(8,128)(2,1)S(1)}, bf16[256,16384]{1,0:T(8,128)(2,1)}, u32[]{:S(2)}) %copy-start.3) | copy-done | bytes 8388632
  138.3 8.7 %shard_map.106 = (f32[1,256]{1,0:T(1,128)}, f32[3,256]{1,0:T(4,128)}) custom-call(f32[32,2,512]{2,1,0:T(2,128)S(1)} %all-gather.1.sums_ref, f32[3,16384]{1,0:T(4,128)S(1)} %copy-done.7, bf16[256,16384]{1,0:T(8,128)(2,1)S(1)} %copy-done.1, bf16[256,16384]{1,0:T(8,128)(2,1)S(1)} %copy-done.3), custom_call_target="tpu_custom_call" | custom-call | tf_op jit(solution)/shard_map/pallas_call | solution.py:287
Async XLA Ops:
  4.1 29.0 %collective-permute-start = (bf16[128,384]{1,0:T(8,128)(2,1)}, bf16[128,384]{1,0:T(8,128)(2,1)S(1)}, u32[]{:S(2)}, u32[]{:S(2)}) collective-permute-start(bf16[128,384]{1,0:T(8,128)(2,1)} %get-tuple-element.11.last_ref), channel_id=1, source_target_pairs={{0,1},{1,2},{2,3},{3,4},{4,5},{5,6},{6,7},{7,8},{8,9},{9,10},{10,1... | collective-permute-start | bytes 294920 | tf_op jit(solution)/shard_map/ppermute | solution.py:232
  9.0 24.1 %collective-permute-start.1 = (bf16[128,384]{1,0:T(8,128)(2,1)}, bf16[128,384]{1,0:T(8,128)(2,1)S(1)}, u32[]{:S(2)}, u32[]{:S(2)}) collective-permute-start(bf16[128,384]{1,0:T(8,128)(2,1)} %get-tuple-element.12.first_ref), channel_id=1, source_target_pairs={{1,0},{2,1},{3,2},{4,3},{5,4},{6,5},{7,6},{8,7},{9,8},{10,9},{11,1... | collective-permute-start | bytes 294920 | tf_op jit(solution)/shard_map/ppermute | solution.py:232
  10.3 1.0 copy-start.6
  11.2 0.7 copy-start.10
  33.0 18.3 %copy-start = (bf16[256,16384]{1,0:T(8,128)(2,1)}, bf16[256,16384]{1,0:T(8,128)(2,1)S(1)}, u32[]{:S(2)}) copy-start(bf16[256,16384]{1,0:T(8,128)(2,1)S(1)} %get-tuple-element.13.cos_ref) | copy-start | bytes 25165828
  33.0 18.3 %copy-start.2 = (bf16[256,16384]{1,0:T(8,128)(2,1)}, bf16[256,16384]{1,0:T(8,128)(2,1)S(1)}, u32[]{:S(2)}) copy-start(bf16[256,16384]{1,0:T(8,128)(2,1)S(1)} %get-tuple-element.14.sin_ref) | copy-start | bytes 25165828
  33.1 1.1 copy-start.4
  34.2 1.2 copy-start.5
  35.4 1.0 copy-start.8
  36.4 1.0 copy-start.9
  37.4 0.7 copy-start.11
  38.1 93.4 %copy-start.7 = (f32[3,16384]{1,0:T(4,128)S(1)}, f32[3,16384]{1,0:T(4,128)}, u32[]{:S(2)}) copy-start(f32[3,16384]{1,0:T(4,128)} %wave_ref.3) | copy-start | bytes 589828
  131.5 3.4 %copy-start.1 = (bf16[256,16384]{1,0:T(8,128)(2,1)S(1)}, bf16[256,16384]{1,0:T(8,128)(2,1)}, u32[]{:S(2)}) copy-start(bf16[256,16384]{1,0:T(8,128)(2,1)} %copy-done) | copy-start | bytes 25165828
  134.9 3.4 %copy-start.3 = (bf16[256,16384]{1,0:T(8,128)(2,1)S(1)}, bf16[256,16384]{1,0:T(8,128)(2,1)}, u32[]{:S(2)}) copy-start(bf16[256,16384]{1,0:T(8,128)(2,1)} %copy-done.2) | copy-start | bytes 25165828

commit v2 on v1

v2 whole, which is shorter than its diff:
```python
import functools
import math

import jax
import jax.numpy as jnp
import numpy as np
from jax import lax
from jax.experimental import pallas as pl
from jax.experimental.pallas import tpu as pltpu
from jax.sharding import PartitionSpec as P

LAYERS = 2
HALO = 64
AXES = ("brick", "kvec")
LANES = 128
F32 = jnp.float32
BF16 = jnp.bfloat16

VMEM = pl.BlockSpec(memory_space=pltpu.VMEM)
HBM = pl.BlockSpec(memory_space=pltpu.HBM)


def pieces(x):
    first = x.astype(BF16).astype(F32)
    rest = x - first
    second = rest.astype(BF16).astype(F32)
    return first, second, rest - second


def pack_kernel(
    feat_ref, pos_ref, neigh_ref, counts_ref, wave_ref, first_ref, last_ref, waves_ref, sem
):
    slots, own = neigh_ref.shape
    channels = feat_ref.shape[1]
    copy = pltpu.make_async_copy(wave_ref, waves_ref, sem)
    copy.start()
    rows = lax.broadcasted_iota(jnp.int32, (slots, own), 1)
    slot = lax.broadcasted_iota(jnp.int32, (slots, own), 0)
    delta = (neigh_ref[...] - HALO - rows).astype(F32)
    delta = jnp.where(slot < counts_ref[...], delta, 0.0)
    zero5 = jnp.zeros((5, own), F32)
    coords = [jnp.concatenate([p, zero5], axis=0) for p in pieces(pos_ref[...])]
    rest = jnp.zeros((LANES - slots - 24, own), F32)
    extra = jnp.concatenate([delta] + coords + [rest], axis=0).astype(BF16)
    half = own // 2
    for ref, start in ((first_ref, 0), (last_ref, half)):
        ref[:, :channels] = feat_ref[start : start + half, :]
        ref[:, channels:] = extra[:, start : start + half]
    copy.wait()


def make_series():
    nodes = 400
    x = np.cos((np.arange(nodes) + 0.5) * np.pi / nodes)
    s = 0.125 * (x + 1.0)
    r = np.sqrt(s)

    def fitted(values, degree):
        cheb = np.polynomial.chebyshev.Chebyshev.fit(s, values, degree, domain=[0.0, 0.25])
        return [float(v) for v in cheb.convert(kind=np.polynomial.Polynomial).coef]

    root = math.sqrt(2.0)
    half_sine = fitted(root * np.sin(np.pi * r) / r, 3)
    half_cosine = fitted(root * np.cos(np.pi * r), 3)
    return half_sine, half_cosine


HALF_SINE, HALF_COSINE = make_series()


def horner(s, coefs):
    value = coefs[-1] * s + coefs[-2]
    for c in coefs[-3::-1]:
        value = value * s + c
    return value


def trig_kernel(
    pos_ref, wave_ref, w_in_ref, w_out_ref, w_charge_ref, cos_ref, sin_ref, coef_ref, w_in_out,
    w_out_out, w_charge_out, left_ref, even_ref, odd_ref, sems, *, tile, chunk, factor,
):
    own = pos_ref.shape[1]
    total = wave_ref.shape[1]
    copies = [
        pltpu.make_async_copy(source, target, sems.at[n])
        for n, (source, target) in enumerate(
            ((w_in_ref, w_in_out), (w_out_ref, w_out_out), (w_charge_ref, w_charge_out))
        )
    ]
    for copy in copies:
        copy.start()
    zero5 = jnp.zeros((5, own), F32)
    a, b, c = (jnp.concatenate([p, zero5], axis=0) for p in pieces(pos_ref[...]))
    left = jnp.concatenate([a, a, b, b, a, c] + [jnp.zeros((80, own), F32)], axis=0)
    left_ref[...] = left.T.astype(BF16)
    tail5 = jnp.zeros((5, tile), F32)
    magic = 12582912.0
    count = total // tile

    def place(step):
        return pl.ds(pl.multiple_of(step * tile, tile), tile)

    def phase(step, out_ref):
        turns = wave_ref[:, place(step)] * (0.5 / math.pi)
        u, v, w = (jnp.concatenate([p, tail5], axis=0) for p in pieces(turns))
        right = jnp.concatenate([u, v, u, v, w, u] + [jnp.zeros((80, tile), F32)], axis=0)
        out_ref[...] = jnp.dot(left_ref[...], right.astype(BF16), preferred_element_type=F32)

    def evaluate(step, in_ref):
        span = place(step)
        for start in range(0, own, chunk):
            t = in_ref[start : start + chunk, :]
            r = t - ((t + magic) - magic)
            s = r * r
            x = r * horner(s, HALF_SINE)
            y = horner(s, HALF_COSINE)
            cos_ref[start : start + chunk, span] = (1.0 - x * x).astype(BF16)
            sin_ref[start : start + chunk, span] = (x * y).astype(BF16)
        wave = wave_ref[:, span]
        ksq = jnp.sum(wave * wave, axis=0, keepdims=True)
        coef = factor * jnp.exp(-0.1 * ksq) / ksq
        scaled = coef * jnp.concatenate([jnp.ones((1, tile), F32), wave], axis=0)
        coef_ref[:, span] = jnp.concatenate([scaled, scaled], axis=0)

    phase(0, even_ref)

    @pl.loop(0, count // 2)
    def _(pair):
        step = 2 * pair
        phase(step + 1, odd_ref)
        evaluate(step, even_ref)
        phase(jnp.minimum(step + 2, count - 1), even_ref)
        evaluate(step + 1, odd_ref)

    for copy in copies:
        copy.wait()


def silu(x):
    return x / (1.0 + jnp.exp(-x))


def layer_kernel(
    before_ref, first_ref, last_ref, after_ref, w_in_ref, w_out_ref, w_charge_ref, cos_ref,
    sin_ref, hidden_ref, sums_ref, feat_ref, mid_ref, matrix_ref, *, tile,
):
    parts = (before_ref, first_ref, last_ref, after_ref)
    half = before_ref.shape[0]
    channels = w_in_ref.shape[1]
    own = 2 * half
    for n, ref in enumerate(parts):
        feat_ref[n * half : (n + 1) * half, :] = ref[:, :channels]
    feat_ref[4 * half :, :] = jnp.zeros((HALO, channels), BF16)
    extras = [ref[:, channels:].astype(F32) for ref in parts]
    rows = [e[64:72] + e[72:80] + e[80:88] for e in extras]
    ext_rows = jnp.concatenate(rows + [jnp.zeros((8, LANES), F32)], axis=1)
    ext_cols = jnp.concatenate([r.T for r in rows], axis=0)
    lane = lax.broadcasted_iota(jnp.int32, (HALO, LANES), 1)
    deep = lax.broadcasted_iota(jnp.int32, (LANES, LANES), 0).astype(F32)
    deltas = [e[:64] for e in extras]
    ends = jnp.where(lane < HALO, deltas[3], deltas[0])
    hists = []
    for delta in (ends, deltas[1], deltas[2]):
        place = jnp.where(delta > 0, delta + 63.0, delta + 64.0)
        place = jnp.where(delta == 0, -1.0, place)
        hist = jnp.zeros((LANES, LANES), F32)
        for slot in range(64):
            hist = hist + jnp.where(deep == place[slot : slot + 1, :], 1.0, 0.0)
        hists.append(hist.T)
    hist_all = (hists[0][HALO:], hists[1][:HALO], hists[1][HALO:], hists[2][:HALO])
    hist_all = hist_all + (hists[2][HALO:], hists[0][:HALO])
    blocks = (own + 2 * HALO) // HALO
    zeros = jnp.zeros((HALO, LANES), F32)
    for block in range(blocks):
        base = HALO * (block + 1)
        hist = hist_all[block]
        low = jnp.concatenate([jnp.where(lane < 64, hist, 0.0), zeros], axis=1)
        high = jnp.concatenate([jnp.where(lane < 64, 0.0, hist), zeros], axis=1)
        counted = pltpu.roll(low, 0, 1, stride=1, stride_axis=0) + pltpu.roll(
            high, 1, 1, stride=1, stride_axis=0
        )
        dist = jnp.zeros((HALO, 2 * LANES), F32)
        for c in range(3):
            there = ext_rows[c : c + 1, HALO * block : HALO * block + 2 * LANES]
            diff = there - ext_cols[base : base + HALO, c : c + 1]
            dist = dist + diff * diff
        weight = counted / (1.0 + dist)
        upper = weight.astype(BF16)
        lower = (weight - upper.astype(F32)).astype(BF16)
        matrix_ref[block, :HALO, :] = upper
        matrix_ref[block, HALO:, :] = lower

    def advance(source_ref, layer, block_ids, row0, residual):
        messages = []
        for block in block_ids:
            start = HALO * (block - row0)
            out = jnp.dot(
                matrix_ref[block],
                source_ref[start : start + 2 * LANES, :],
                preferred_element_type=F32,
            )
            messages.append(out[:HALO] + out[HALO:])
        message = jnp.concatenate(messages, axis=0)
        scale = lax.rsqrt(jnp.mean(message * message, axis=-1, keepdims=True) + 1e-05)
        normed = (message * scale).astype(BF16)
        inner = silu(jnp.dot(normed, w_in_ref[layer], preferred_element_type=F32)).astype(BF16)
        update = jnp.dot(inner, w_out_ref[layer], preferred_element_type=F32)
        return (residual.astype(F32) + update).astype(BF16)

    grown = own + 2 * HALO
    mid_ref[:grown, :] = advance(
        feat_ref, 0, range(blocks), 0, feat_ref[HALO : HALO + grown, :]
    )
    mid_ref[grown:, :] = jnp.zeros((HALO, channels), BF16)
    final = advance(mid_ref, 1, range(1, blocks - 1), 1, mid_ref[HALO : HALO + own, :])
    hidden_ref[...] = final
    reader = jnp.concatenate(
        list(pieces(w_charge_ref[...])) + [jnp.zeros((5, channels), F32)], axis=0
    ).astype(BF16)
    read = lax.dot_general(
        reader, final, (((1,), (1,)), ((), ())), preferred_element_type=F32
    )
    charge = read[0:1] + read[1:2] + read[2:3]
    hi, mid, lo = pieces(charge)
    charges = jnp.concatenate([hi, mid, lo, jnp.zeros((5, own), F32)], axis=0).astype(BF16)

    share = sums_ref.shape[2]
    per = tile // share

    @pl.loop(0, sums_ref.shape[0] // per)
    def _(step):
        span = pl.ds(pl.multiple_of(step * tile, tile), tile)
        for n, ref in enumerate((cos_ref, sin_ref)):
            part = jnp.dot(charges, ref[:, span], preferred_element_type=F32)
            part = part[0:1] + part[1:2] + part[2:3]
            for q in range(per):
                sums_ref[step * per + q, n : n + 1, :] = part[:, q * share : (q + 1) * share]


def response_kernel(sums_ref, coef_ref, cos_ref, sin_ref, pot_ref, field_ref, acc_ref):
    step = pl.program_id(0)
    per, _, share = sums_ref.shape
    row = lax.broadcasted_iota(jnp.int32, (8, share), 0)
    lead = row % 4 == 0
    upper = row < 4
    dims = (((1,), (1,)), ((), ()))

    @pl.when(step == 0)
    def _():
        acc_ref[...] = jnp.zeros_like(acc_ref)

    factors = ([], [])
    for q in range(per):
        scaled = coef_ref[:, q * share : (q + 1) * share]
        cosine = sums_ref[q, 0:1, :]
        sine = sums_ref[q, 1:2, :]
        for n, (top, other) in enumerate(((cosine, -sine), (sine, cosine))):
            full = scaled * jnp.where(lead, top, other)
            hi = full.astype(BF16).astype(F32)
            factors[n].append(jnp.where(upper, hi, full - hi))
    total = acc_ref[...]
    for n, ref in enumerate((cos_ref, sin_ref)):
        wide = jnp.concatenate(factors[n], axis=1).astype(BF16)
        total = total + lax.dot_general(wide, ref[...], dims, preferred_element_type=F32)
    acc_ref[...] = total

    @pl.when(step == pl.num_programs(0) - 1)
    def _():
        result = acc_ref[:4] + acc_ref[4:]
        pot_ref[...] = result[0:1]
        field_ref[...] = result[1:4]


def shifted(x, step):
    devices = lax.axis_size(AXES)
    pairs = [(i, i + step) for i in range(devices) if 0 <= i + step < devices]
    return lax.ppermute(x, AXES, pairs)


def per_device(features, positions, neighbours, counts, w_in, w_out, w_charge, wave):
    own, channels = features.shape
    total = wave.shape[1]
    devices = lax.axis_size(AXES)
    half = own // 2
    width = channels + LANES
    share = total // devices
    factor = 4.0 / math.sqrt(own * devices * total)
    wide = 2048
    dma = pltpu.SemaphoreType.DMA
    w_charge = w_charge.reshape(1, channels)
    wave, w_in, w_out, w_charge = (
        pltpu.with_memory_space_constraint(x, pltpu.HBM) for x in (wave, w_in, w_out, w_charge)
    )

    edge = pltpu.VMEM((half, width), BF16)
    first, last, waves = pl.pallas_call(
        pack_kernel,
        out_shape=(edge, edge, pltpu.VMEM(wave.shape, F32)),
        in_specs=[VMEM] * 4 + [HBM],
        out_specs=(VMEM,) * 3,
        scratch_shapes=[dma],
    )(features, positions, neighbours.T, counts.reshape(1, own), wave)
    before = shifted(last, 1)
    after = shifted(first, -1)

    table = pltpu.VMEM((own, total), BF16)
    kept = pltpu.VMEM(w_in.shape, BF16)
    cosine, sine, coef, w_first, w_second, w_read = pl.pallas_call(
        functools.partial(trig_kernel, tile=256, chunk=32, factor=factor),
        out_shape=(table, table, pltpu.VMEM((8, total), F32), kept, kept)
        + (pltpu.VMEM((1, channels), F32),),
        in_specs=[VMEM] * 2 + [HBM] * 3,
        out_specs=(VMEM,) * 6,
        scratch_shapes=[pltpu.VMEM((own, LANES), BF16)]
        + [pltpu.VMEM((own, 256), F32)] * 2
        + [dma((3,))],
        compiler_params=pltpu.CompilerParams(vmem_limit_bytes=16 << 20),
        cost_estimate=pl.CostEstimate(
            flops=own * total * 40, bytes_accessed=4 * own * total, transcendentals=0
        ),
    )(positions, waves, w_in, w_out, w_charge)

    hidden, partial = pl.pallas_call(
        functools.partial(layer_kernel, tile=wide),
        out_shape=(
            jax.ShapeDtypeStruct((own, channels), BF16),
            jax.ShapeDtypeStruct((devices, 2, share), F32),
        ),
        in_specs=[VMEM] * 9,
        out_specs=(VMEM, VMEM),
        scratch_shapes=[
            pltpu.VMEM((4 * half + HALO, channels), BF16),
            pltpu.VMEM((own + 3 * HALO, channels), BF16),
            pltpu.VMEM((own // HALO + 2, 2 * HALO, 2 * LANES), BF16),
        ],
        compiler_params=pltpu.CompilerParams(vmem_limit_bytes=16 << 20),
    )(before, first, last, after, w_first, w_second, w_read, cosine, sine)

    swapped = lax.all_to_all(partial, AXES, 0, 0, tiled=True)
    mine = jnp.sum(swapped, axis=0)
    spread = jnp.broadcast_to(mine[None], (devices, 2, share))
    sums = lax.all_to_all(spread, AXES, 0, 0, tiled=True)

    per = wide // share
    fixed = lambda step: (0, 0)
    across = lambda step: (0, step)
    potential, field = pl.pallas_call(
        response_kernel,
        grid=(total // wide,),
        out_shape=(
            jax.ShapeDtypeStruct((1, own), F32),
            jax.ShapeDtypeStruct((3, own), F32),
        ),
        in_specs=[
            pl.BlockSpec((per, 2, share), lambda step: (step, 0, 0)),
            pl.BlockSpec((8, wide), across),
            pl.BlockSpec((own, wide), across),
            pl.BlockSpec((own, wide), across),
        ],
        out_specs=(pl.BlockSpec((1, own), fixed), pl.BlockSpec((3, own), fixed)),
        scratch_shapes=[pltpu.VMEM((8, own), F32)],
        compiler_params=pltpu.CompilerParams(vmem_limit_bytes=56 << 20),
    )(sums, coef, cosine, sine)
    return (hidden, potential.reshape(own), field)


def solution(mesh):
    placed = (
        P(AXES, None),
        P(None, AXES),
        P(AXES, None),
        P(AXES),
        P(),
        P(),
        P(),
        P(),
    )
    return jax.shard_map(
        per_device,
        mesh=mesh,
        in_specs=placed,
        out_specs=(P(AXES, None), P(AXES), P(None, AXES)),
        check_vma=False,
    )
```

time: 148 us -> 69.1 us (0.47)
  blocking collectives: 80.1 us -> 25.9 us
  local copies, waits for them, and re-layouts: 15 us -> 0.73 us
  Pallas kernels: 44.9 us -> 35.1 us
    all_gather x1 -> x0, blocking collectives: 65 us -> none  [per_device(): sums = lax.all_gather(mine, AXES)]
    unnamed x25 -> x8, local copies, waits for them, and re-layouts: 15 us -> 0.69 us
    all_to_all x0 -> x1, blocking collectives: none -> 10.8 us  [per_device(): sums = lax.all_to_all(spread, AXES, 0, 0, tiled=True)]
    pallas_call x4, Pallas kernels: 44.9 us -> 35.1 us  [the longest x1 16 us: per_device(): pl.pallas_call(functools.partial(trig_kernel, tile=256, chunk=32, factor=...]
  transfers between devices with their start and end apart: 2 -> 2, of which waited for: 0 -> 0; matrix products, arithmetic and copies ran while one was open for 0% -> 0% of each run, Pallas kernels for 14% -> 23%
where the time goes in v2:
time: 69.1 us; the launch traced here: 68.8 us
  Pallas kernels  35.1 us (51%)
  blocking collectives  25.9 us (37%)
  starting transfers between devices  6.23 us (9%)
  local copies, waits for them, and re-layouts  0.73 us (1%)
  between operations  0.72 us (1%)
    pallas_call x1, Pallas kernels, per_device(): pl.pallas_call(functools.partial(trig_kernel, tile=256, chunk=32, factor=...  16 us
    all_to_all x1, blocking collectives, per_device(): swapped = lax.all_to_all(partial, AXES, 0, 0, tiled=True)  15.1 us
    all_to_all x1, blocking collectives, per_device(): sums = lax.all_to_all(spread, AXES, 0, 0, tiled=True)  10.8 us
    pallas_call x1, Pallas kernels, per_device(): pl.pallas_call(response_kernel, grid=(total // wide,), out_shape=(jax.Sha...  10.7 us
    pallas_call x1, Pallas kernels, per_device(): pl.pallas_call(functools.partial(layer_kernel, tile=wide), out_shape=(jax...  6.48 us
    ppermute x2, starting transfers between devices, shifted(): return lax.ppermute(x, AXES, pairs)  6.23 us
    pallas_call x1, Pallas kernels, per_device(): pl.pallas_call(pack_kernel, out_shape=(edge, edge, pltpu.VMEM(wave.shape,...  1.88 us
  transfers between devices with their start and end apart: 2, of which 0 were waited for; matrix products, arithmetic and copies ran while one was open for 0% of the time, Pallas kernels for 23%

profile of v2, /device:TPU:0, one launch (start us, length us, event | category | flops | bytes accessed | tf_op | source)
XLA Modules:
  0.0 68.8 jit_solution(18146539350400416843)
XLA Ops:
  0.6 1.9 %shard_map.103 = (bf16[128,384]{1,0:T(8,128)(2,1)S(1)}, bf16[128,384]{1,0:T(8,128)(2,1)S(1)}, f32[3,16384]{1,0:T(4,128)S(1)}) custom-call(bf16[256,256]{1,0:T(8,128)(2,1)} %feat_ref.1, f32[3,256]{1,0:T(4,128)} %pos_ref.3, s32[64,256]{1,0:T(8,128)} %bitcast.4, s32[1,256]{1,0:T(1,128)} %bitcast.5, f32[3,16384]{1,0:T(4,128)} %wave_ref.1), custom_call_target="tpu_custom_call" | custom-call | tf_op jit(solution)/shard_map/pallas_call | solution.py:296
  2.5 4.9 %collective-permute-start = (bf16[128,384]{1,0:T(8,128)(2,1)S(1)}, bf16[128,384]{1,0:T(8,128)(2,1)S(1)}, u32[]{:S(2)}, u32[]{:S(2)}) collective-permute-start(bf16[128,384]{1,0:T(8,128)(2,1)S(1)} %get-tuple-element.16.last_ref), channel_id=1, source_target_pairs={{0,1},{1,2},{2,3},{3,4},{4,5},{5,6},{6,7},{7,8},{8,9},{9,10},{10,1... | collective-permute-start | bytes 294920 | tf_op jit(solution)/shard_map/ppermute | solution.py:277
  7.5 1.3 %collective-permute-start.1 = (bf16[128,384]{1,0:T(8,128)(2,1)S(1)}, bf16[128,384]{1,0:T(8,128)(2,1)S(1)}, u32[]{:S(2)}, u32[]{:S(2)}) collective-permute-start(bf16[128,384]{1,0:T(8,128)(2,1)S(1)} %get-tuple-element.17.first_ref), channel_id=1, source_target_pairs={{1,0},{2,1},{3,2},{4,3},{5,4},{6,5},{7,6},{8,7},{9,8},{10,9},{11,1... | collective-permute-start | bytes 294920 | tf_op jit(solution)/shard_map/ppermute | solution.py:277
  8.8 0.0 copy-start.3
  8.8 0.7 copy-done.3
  9.5 16.0 %shard_map.104 = (bf16[256,16384]{1,0:T(8,128)(2,1)S(1)}, bf16[256,16384]{1,0:T(8,128)(2,1)S(1)}, f32[8,16384]{1,0:T(8,128)S(1)}, bf16[2,256,256]{2,1,0:T(8,128)...) custom-call(f32[3,256]{1,0:T(4,128)S(1)} %copy-done.3, f32[3,16384]{1,0:T(4,128)S(1)} %get-tuple-element.18.wave_ref, ...), custom_call_target="tpu_custom_call" | custom-call | flops 167772160 | bytes 16777216 | tf_op jit(solution)/shard_map/pallas_call | solution.py:308
  25.5 0.0 copy-start
  25.5 0.0 copy-start.1
  25.5 0.0 copy-start.2
  25.5 0.0 collective-permute-done.before_ref
  25.5 0.0 collective-permute-done.1.after_ref
  25.5 6.5 %shard_map.105 = (bf16[256,256]{1,0:T(8,128)(2,1)}, f32[32,2,512]{2,1,0:T(2,128)S(1)}) custom-call(bf16[128,384]{1,0:T(8,128)(2,1)S(1)} %collective-permute-done.before_ref, bf16[128,384]{1,0:T(8,128)(2,1)S(1)} %get-tuple-element.17.first_ref, bf16[128,384]{1,0:T(8,128)(2,1)S(1)} %get-tuple-element.16.last_ref, ...), custom_call_target="tpu_custom_call" | custom-call | tf_op jit(solution)/shard_map/pallas_call | solution.py:323
  32.0 0.0 copy-done
  32.0 0.0 copy-done.1
  32.0 0.0 copy-done.2
  32.0 15.1 %all_to_all.10 = f32[32,2,512]{2,1,0:T(2,128)S(1)} all-to-all(f32[32,2,512]{2,1,0:T(2,128)S(1)} %get-tuple-element.25), channel_id=1, replica_groups=mesh['brick'=8,'kvec'=4] {'brick','kvec'}, dimensions={0} | all-to-all | bytes 262144 | tf_op jit(solution)/shard_map/all_to_all | solution.py:339
  47.1 0.1 reduce_sum.9
  47.2 10.8 %all_to_all.11.sums_ref = f32[32,2,512]{2,1,0:T(2,128)} all-to-all(f32[32,2,512]{2,1,0:T(2,128)S(1)} %broadcast_in_dim.2), channel_id=1, replica_groups=mesh['brick'=8,'kvec'=4] {'brick','kvec'}, dimensions={0} | all-to-all | bytes 262144 | tf_op jit(solution)/shard_map/all_to_all | solution.py:342
  58.0 10.7 %shard_map.106 = (f32[1,256]{1,0:T(1,128)}, f32[3,256]{1,0:T(4,128)}) custom-call(f32[32,2,512]{2,1,0:T(2,128)} %all_to_all.11.sums_ref, f32[8,16384]{1,0:T(8,128)} %copy-done.2, bf16[256,16384]{1,0:T(8,128)(2,1)} %copy-done, bf16[256,16384]{1,0:T(8,128)(2,1)} %copy-done.1), custom_call_target="tpu_custom_call" | custom-call | tf_op jit(solution)/shard_map/pallas_call | solution.py:347
  (1 shorter events, 0.0 us)
Async XLA Ops:
  2.5 23.0 %collective-permute-start = (bf16[128,384]{1,0:T(8,128)(2,1)S(1)}, bf16[128,384]{1,0:T(8,128)(2,1)S(1)}, u32[]{:S(2)}, u32[]{:S(2)}) collective-permute-start(bf16[128,384]{1,0:T(8,128)(2,1)S(1)} %get-tuple-element.16.last_ref), channel_id=1, source_target_pairs={{0,1},{1,2},{2,3},{3,4},{4,5},{5,6},{6,7},{7,8},{8,9},{9,10},{10,1... | collective-permute-start | bytes 294920 | tf_op jit(solution)/shard_map/ppermute | solution.py:277
  7.5 18.1 %collective-permute-start.1 = (bf16[128,384]{1,0:T(8,128)(2,1)S(1)}, bf16[128,384]{1,0:T(8,128)(2,1)S(1)}, u32[]{:S(2)}, u32[]{:S(2)}) collective-permute-start(bf16[128,384]{1,0:T(8,128)(2,1)S(1)} %get-tuple-element.17.first_ref), channel_id=1, source_target_pairs={{1,0},{2,1},{3,2},{4,3},{5,4},{6,5},{7,6},{8,7},{9,8},{10,9},{11,1... | collective-permute-start | bytes 294920 | tf_op jit(solution)/shard_map/ppermute | solution.py:277
  8.8 0.7 %copy-start.3 = (f32[3,256]{1,0:T(4,128)S(1)}, f32[3,256]{1,0:T(4,128)}, u32[]{:S(2)}) copy-start(f32[3,256]{1,0:T(4,128)} %pos_ref.3) | copy-start | bytes 9220
  25.5 6.5 %copy-start = (bf16[256,16384]{1,0:T(8,128)(2,1)}, bf16[256,16384]{1,0:T(8,128)(2,1)S(1)}, u32[]{:S(2)}) copy-start(bf16[256,16384]{1,0:T(8,128)(2,1)S(1)} %get-tuple-element.22.cos_ref) | copy-start | bytes 25165828
  25.5 6.5 %copy-start.1 = (bf16[256,16384]{1,0:T(8,128)(2,1)}, bf16[256,16384]{1,0:T(8,128)(2,1)S(1)}, u32[]{:S(2)}) copy-start(bf16[256,16384]{1,0:T(8,128)(2,1)S(1)} %get-tuple-element.23.sin_ref) | copy-start | bytes 25165828
  25.5 6.5 %copy-start.2 = (f32[8,16384]{1,0:T(8,128)}, f32[8,16384]{1,0:T(8,128)S(1)}, u32[]{:S(2)}) copy-start(f32[8,16384]{1,0:T(8,128)S(1)} %get-tuple-element.26.coef_ref) | copy-start | bytes 1572868

commit v3 on v2

--- a/solution.py
+++ b/solution.py
@@ -28,12 +28,14 @@
 
 
 def pack_kernel(
-    feat_ref, pos_ref, neigh_ref, counts_ref, wave_ref, first_ref, last_ref, waves_ref, sem
+    feat_ref, pos_ref, neigh_ref, counts_ref, wave_ref, first_ref, last_ref, waves_ref,
+    held_ref, sem,
 ):
     slots, own = neigh_ref.shape
     channels = feat_ref.shape[1]
     copy = pltpu.make_async_copy(wave_ref, waves_ref, sem)
     copy.start()
+    held_ref[...] = pos_ref[...]
     rows = lax.broadcasted_iota(jnp.int32, (slots, own), 1)
     slot = lax.broadcasted_iota(jnp.int32, (slots, own), 0)
     delta = (neigh_ref[...] - HALO - rows).astype(F32)
@@ -60,12 +62,10 @@
         return [float(v) for v in cheb.convert(kind=np.polynomial.Polynomial).coef]
 
     root = math.sqrt(2.0)
-    half_sine = fitted(root * np.sin(np.pi * r) / r, 3)
-    half_cosine = fitted(root * np.cos(np.pi * r), 3)
-    return half_sine, half_cosine
-
-
-HALF_SINE, HALF_COSINE = make_series()
+    return fitted(root * np.sin(np.pi * r) / r, 3)
+
+
+HALF_SINE = make_series()
 
 
 def horner(s, coefs):
@@ -76,8 +76,9 @@
 
 
 def trig_kernel(
-    pos_ref, wave_ref, w_in_ref, w_out_ref, w_charge_ref, cos_ref, sin_ref, coef_ref, w_in_out,
-    w_out_out, w_charge_out, left_ref, even_ref, odd_ref, sems, *, tile, chunk, factor,
+    pos_ref, wave_ref, w_in_ref, w_out_ref, w_charge_ref, cos_ref, sin_ref, cos_t_ref, sin_t_ref,
+    coef_ref, w_in_out, w_out_out, w_charge_out, left_ref, even_ref, odd_ref, turned_ref, sems,
+    turned_sems, *, tile, chunk, factor,
 ):
     own = pos_ref.shape[1]
     total = wave_ref.shape[1]
@@ -113,25 +114,57 @@
             r = t - ((t + magic) - magic)
             s = r * r
             x = r * horner(s, HALF_SINE)
-            y = horner(s, HALF_COSINE)
-            cos_ref[start : start + chunk, span] = (1.0 - x * x).astype(BF16)
-            sin_ref[start : start + chunk, span] = (x * y).astype(BF16)
+            square = x * x
+            rest = jnp.maximum(2.0 - square, 1e-20)
+            cos_ref[start : start + chunk, span] = (1.0 - square).astype(BF16)
+            sin_ref[start : start + chunk, span] = (x * rest * lax.rsqrt(rest)).astype(BF16)
         wave = wave_ref[:, span]
         ksq = jnp.sum(wave * wave, axis=0, keepdims=True)
         coef = factor * jnp.exp(-0.1 * ksq) / ksq
         scaled = coef * jnp.concatenate([jnp.ones((1, tile), F32), wave], axis=0)
         coef_ref[:, span] = jnp.concatenate([scaled, scaled], axis=0)
 
+    def moves(slot, target):
+        rows = place(target)
+        return [
+            pltpu.make_async_copy(
+                turned_ref.at[slot, n], out_ref.at[rows, :], turned_sems.at[slot, n]
+            )
+            for n, out_ref in enumerate((cos_t_ref, sin_t_ref))
+        ]
+
+    def flip(slot, step, target):
+        for n, ref in enumerate((cos_ref, sin_ref)):
+            turned_ref[slot, n] = ref[:, place(step)].T
+        for move in moves(slot, target):
+            move.start()
+
+    def drain():
+        for slot in range(2):
+            for move in moves(slot, count):
+                move.wait()
+
     phase(0, even_ref)
 
     @pl.loop(0, count // 2)
     def _(pair):
         step = 2 * pair
+
+        @pl.when(pair > 0)
+        def _():
+            drain()
+
+        flip(0, jnp.maximum(step - 1, 0), jnp.where(pair == 0, count, step - 1))
         phase(step + 1, odd_ref)
         evaluate(step, even_ref)
+        flip(1, step, step)
         phase(jnp.minimum(step + 2, count - 1), even_ref)
         evaluate(step + 1, odd_ref)
 
+    drain()
+    flip(0, count - 1, count - 1)
+    for move in moves(0, count):
+        move.wait()
     for copy in copies:
         copy.wait()
 
@@ -243,7 +276,6 @@
     row = lax.broadcasted_iota(jnp.int32, (8, share), 0)
     lead = row % 4 == 0
     upper = row < 4
-    dims = (((1,), (1,)), ((), ()))
 
     @pl.when(step == 0)
     def _():
@@ -261,7 +293,7 @@
     total = acc_ref[...]
     for n, ref in enumerate((cos_ref, sin_ref)):
         wide = jnp.concatenate(factors[n], axis=1).astype(BF16)
-        total = total + lax.dot_general(wide, ref[...], dims, preferred_element_type=F32)
+        total = total + jnp.dot(wide, ref[...], preferred_element_type=F32)
     acc_ref[...] = total
 
     @pl.when(step == pl.num_programs(0) - 1)
@@ -293,32 +325,33 @@
     )
 
     edge = pltpu.VMEM((half, width), BF16)
-    first, last, waves = pl.pallas_call(
+    first, last, waves, held = pl.pallas_call(
         pack_kernel,
-        out_shape=(edge, edge, pltpu.VMEM(wave.shape, F32)),
+        out_shape=(edge, edge, pltpu.VMEM(wave.shape, F32), pltpu.VMEM(positions.shape, F32)),
         in_specs=[VMEM] * 4 + [HBM],
-        out_specs=(VMEM,) * 3,
+        out_specs=(VMEM,) * 4,
         scratch_shapes=[dma],
     )(features, positions, neighbours.T, counts.reshape(1, own), wave)
     before = shifted(last, 1)
     after = shifted(first, -1)
 
     table = pltpu.VMEM((own, total), BF16)
+    table_t = pltpu.HBM((total + 256, own), BF16)
     kept = pltpu.VMEM(w_in.shape, BF16)
-    cosine, sine, coef, w_first, w_second, w_read = pl.pallas_call(
+    cosine, sine, cosine_t, sine_t, coef, w_first, w_second, w_read = pl.pallas_call(
         functools.partial(trig_kernel, tile=256, chunk=32, factor=factor),
-        out_shape=(table, table, pltpu.VMEM((8, total), F32), kept, kept)
+        out_shape=(table, table, table_t, table_t, pltpu.VMEM((8, total), F32), kept, kept)
         + (pltpu.VMEM((1, channels), F32),),
         in_specs=[VMEM] * 2 + [HBM] * 3,
-        out_specs=(VMEM,) * 6,
+        out_specs=(VMEM,) * 2 + (HBM,) * 2 + (VMEM,) * 4,
         scratch_shapes=[pltpu.VMEM((own, LANES), BF16)]
         + [pltpu.VMEM((own, 256), F32)] * 2
-        + [dma((3,))],
+        + [pltpu.VMEM((2, 2, 256, own), BF16), dma((3,)), dma((2, 2))],
         compiler_params=pltpu.CompilerParams(vmem_limit_bytes=16 << 20),
         cost_estimate=pl.CostEstimate(
             flops=own * total * 40, bytes_accessed=4 * own * total, transcendentals=0
         ),
-    )(positions, waves, w_in, w_out, w_charge)
+    )(held, waves, w_in, w_out, w_charge)
 
     hidden, partial = pl.pallas_call(
         functools.partial(layer_kernel, tile=wide),
@@ -336,10 +369,10 @@
         compiler_params=pltpu.CompilerParams(vmem_limit_bytes=16 << 20),
     )(before, first, last, after, w_first, w_second, w_read, cosine, sine)
 
-    swapped = lax.all_to_all(partial, AXES, 0, 0, tiled=True)
-    mine = jnp.sum(swapped, axis=0)
+    swapped = lax.all_to_all(partial.astype(BF16), AXES, 0, 0, tiled=True)
+    mine = jnp.sum(swapped.astype(F32), axis=0).astype(BF16)
     spread = jnp.broadcast_to(mine[None], (devices, 2, share))
-    sums = lax.all_to_all(spread, AXES, 0, 0, tiled=True)
+    sums = lax.all_to_all(spread, AXES, 0, 0, tiled=True).astype(F32)
 
     per = wide // share
     fixed = lambda step: (0, 0)
@@ -354,13 +387,13 @@
         in_specs=[
             pl.BlockSpec((per, 2, share), lambda step: (step, 0, 0)),
             pl.BlockSpec((8, wide), across),
-            pl.BlockSpec((own, wide), across),
-            pl.BlockSpec((own, wide), across),
+            pl.BlockSpec((wide, own), lambda step: (step, 0)),
+            pl.BlockSpec((wide, own), lambda step: (step, 0)),
         ],
         out_specs=(pl.BlockSpec((1, own), fixed), pl.BlockSpec((3, own), fixed)),
         scratch_shapes=[pltpu.VMEM((8, own), F32)],
         compiler_params=pltpu.CompilerParams(vmem_limit_bytes=56 << 20),
-    )(sums, coef, cosine, sine)
+    )(sums, coef, cosine_t, sine_t)
     return (hidden, potential.reshape(own), field)
 
 

time: 69.1 us -> 85.8 us (1.24)
  Pallas kernels: 35.1 us -> 54.3 us
  blocking collectives: 25.9 us -> 23.4 us
    pallas_call x1, Pallas kernels: 16 us -> 36.3 us  [per_device(): pl.pallas_call(functools.partial(trig_kernel, tile=256, chunk=32, factor=...]
    all_to_all x2, blocking collectives: 25.9 us -> 23.4 us  [the longest x1 14.2 us: per_device(): swapped = lax.all_to_all(partial.astype(BF16), AXES, 0, 0, tiled=True)]
    pallas_call x1, Pallas kernels: 10.7 us -> 9.63 us  [per_device(): pl.pallas_call(response_kernel, grid=(total // wide,), out_shape=(jax.Sha...]
  transfers between devices with their start and end apart: 2 -> 2, of which waited for: 0 -> 0; matrix products, arithmetic and copies ran while one was open for 0% -> 0% of each run, Pallas kernels for 23% -> 42%
where the time goes in v3:
time: 85.8 us; the launch traced here: 85.5 us
  Pallas kernels  54.3 us (63%)
  blocking collectives  23.4 us (27%)
  starting transfers between devices  6.23 us (7%)
    pallas_call x1, Pallas kernels, per_device(): pl.pallas_call(functools.partial(trig_kernel, tile=256, chunk=32, factor=...  36.3 us
    all_to_all x1, blocking collectives, per_device(): swapped = lax.all_to_all(partial.astype(BF16), AXES, 0, 0, tiled=True)  14.2 us
    pallas_call x1, Pallas kernels, per_device(): pl.pallas_call(response_kernel, grid=(total // wide,), out_shape=(jax.Sha...  9.63 us
    all_to_all x1, blocking collectives, per_device(): sums = lax.all_to_all(spread, AXES, 0, 0, tiled=True).astype(F32)  9.19 us
    pallas_call x1, Pallas kernels, per_device(): pl.pallas_call(functools.partial(layer_kernel, tile=wide), out_shape=(jax...  6.48 us
    ppermute x2, starting transfers between devices, shifted(): return lax.ppermute(x, AXES, pairs)  6.23 us
    pallas_call x1, Pallas kernels, per_device(): pl.pallas_call(pack_kernel, out_shape=(edge, edge, pltpu.VMEM(wave.shape,...  1.88 us
  transfers between devices with their start and end apart: 2, of which 0 were waited for; matrix products, arithmetic and copies ran while one was open for 0% of the time, Pallas kernels for 42%

profile of v3, /device:TPU:0, one launch (start us, length us, event | category | flops | bytes accessed | tf_op | source)
XLA Modules:
  0.0 85.5 jit_solution(15561459059682937099)
XLA Ops:
  0.6 1.9 %shard_map.103 = (bf16[128,384]{1,0:T(8,128)(2,1)S(1)}, bf16[128,384]{1,0:T(8,128)(2,1)S(1)}, f32[3,16384]{1,0:T(4,128)S(1)}, f32[3,256]{1,0:T(4,128)S(1)}) custom-call(bf16[256,256]{1,0:T(8,128)(2,1)} %feat_ref.1, f32[3,256]{1,0:T(4,128)} %pos_ref.1, s32[64,256]{1,0:T(8,128)} %bitcast.4, s32[1,256]{1,0:T(1,128)} %bitcast.5, f32[3,16384]{1,0:T(4,128)} %wave_ref.1), custom_call_target="tpu_custom_call" | custom-call | tf_op jit(solution)/shard_map/pallas_call | solution.py:328
  2.5 4.9 %collective-permute-start = (bf16[128,384]{1,0:T(8,128)(2,1)S(1)}, bf16[128,384]{1,0:T(8,128)(2,1)S(1)}, u32[]{:S(2)}, u32[]{:S(2)}) collective-permute-start(bf16[128,384]{1,0:T(8,128)(2,1)S(1)} %get-tuple-element.19.last_ref), channel_id=1, source_target_pairs={{0,1},{1,2},{2,3},{3,4},{4,5},{5,6},{6,7},{7,8},{8,9},{9,10},{10,1... | collective-permute-start | bytes 294920 | tf_op jit(solution)/shard_map/ppermute | solution.py:309
  7.5 1.3 %collective-permute-start.1 = (bf16[128,384]{1,0:T(8,128)(2,1)S(1)}, bf16[128,384]{1,0:T(8,128)(2,1)S(1)}, u32[]{:S(2)}, u32[]{:S(2)}) collective-permute-start(bf16[128,384]{1,0:T(8,128)(2,1)S(1)} %get-tuple-element.20.first_ref), channel_id=1, source_target_pairs={{1,0},{2,1},{3,2},{4,3},{5,4},{6,5},{7,6},{8,7},{9,8},{10,9},{11,1... | collective-permute-start | bytes 294920 | tf_op jit(solution)/shard_map/ppermute | solution.py:309
  8.8 36.3 %shard_map.104 = (bf16[256,16384]{1,0:T(8,128)(2,1)S(1)}, bf16[256,16384]{1,0:T(8,128)(2,1)S(1)}, bf16[16640,256]{1,0:T(8,128)(2,1)}, bf16[16640,256]{1,0:T(8,12...) custom-call(f32[3,256]{1,0:T(4,128)S(1)} %get-tuple-element.21.pos_r, ...), custom_call_target="tpu_custom_call" | custom-call | flops 167772160 | bytes 16777216 | tf_op jit(solution)/shard_map/pallas_call | solution.py:341
  45.1 0.0 copy-start
  45.1 0.0 collective-permute-done.before_ref
  45.1 0.0 collective-permute-done.1.after_ref
  45.1 6.5 %shard_map.105 = (bf16[256,256]{1,0:T(8,128)(2,1)}, f32[32,2,512]{2,1,0:T(2,128)S(1)}) custom-call(bf16[128,384]{1,0:T(8,128)(2,1)S(1)} %collective-permute-done.before_ref, bf16[128,384]{1,0:T(8,128)(2,1)S(1)} %get-tuple-element.20.first_ref, bf16[128,384]{1,0:T(8,128)(2,1)S(1)} %get-tuple-element.19.last_ref, ...), custom_call_target="tpu_custom_call" | custom-call | tf_op jit(solution)/shard_map/pallas_call | solution.py:356
  51.6 0.0 copy-done
  51.6 14.2 %all_to_all.10 = bf16[32,2,512]{2,1,0:T(2,128)(2,1)S(1)} all-to-all(bf16[32,2,512]{2,1,0:T(2,128)(2,1)S(1)} %convert_element_type.8), channel_id=1, replica_groups=mesh['brick'=8,'kvec'=4] {'brick','kvec'}, dimensions={0} | all-to-all | bytes 131072 | tf_op jit(solution)/shard_map/all_to_all | solution.py:372
  65.9 0.1 reduce_sum.12
  66.0 9.2 %all_to_all.11 = bf16[32,2,512]{2,1,0:T(2,128)(2,1)S(1)} all-to-all(bf16[32,2,512]{2,1,0:T(2,128)(2,1)S(1)} %broadcast_in_dim.2), channel_id=1, replica_groups=mesh['brick'=8,'kvec'=4] {'brick','kvec'}, dimensions={0} | all-to-all | bytes 131072 | tf_op jit(solution)/shard_map/all_to_all | solution.py:375
  75.2 0.7 convert_element_type.9.sums_ref
  75.9 9.6 %shard_map.106 = (f32[1,256]{1,0:T(1,128)}, f32[3,256]{1,0:T(4,128)}) custom-call(f32[32,2,512]{2,1,0:T(2,128)} %convert_element_type.9.sums_ref, f32[8,16384]{1,0:T(8,128)} %copy-done, bf16[16640,256]{1,0:T(8,128)(2,1)} %get-tuple-element.31.cos_ref, bf16[16640,256]{1,0:T(8,128)(2,1)} %get-tuple-element.32.sin_ref), custom_call_target="tpu_custom_call" | custom-call | tf_op jit(solution)/shard_map/pallas_call | solution.py:380
  (2 shorter events, 0.1 us)
Async XLA Ops:
  2.5 42.6 %collective-permute-start = (bf16[128,384]{1,0:T(8,128)(2,1)S(1)}, bf16[128,384]{1,0:T(8,128)(2,1)S(1)}, u32[]{:S(2)}, u32[]{:S(2)}) collective-permute-start(bf16[128,384]{1,0:T(8,128)(2,1)S(1)} %get-tuple-element.19.last_ref), channel_id=1, source_target_pairs={{0,1},{1,2},{2,3},{3,4},{4,5},{5,6},{6,7},{7,8},{8,9},{9,10},{10,1... | collective-permute-start | bytes 294920 | tf_op jit(solution)/shard_map/ppermute | solution.py:309
  7.5 37.6 %collective-permute-start.1 = (bf16[128,384]{1,0:T(8,128)(2,1)S(1)}, bf16[128,384]{1,0:T(8,128)(2,1)S(1)}, u32[]{:S(2)}, u32[]{:S(2)}) collective-permute-start(bf16[128,384]{1,0:T(8,128)(2,1)S(1)} %get-tuple-element.20.first_ref), channel_id=1, source_target_pairs={{1,0},{2,1},{3,2},{4,3},{5,4},{6,5},{7,6},{8,7},{9,8},{10,9},{11,1... | collective-permute-start | bytes 294920 | tf_op jit(solution)/shard_map/ppermute | solution.py:309
  45.1 6.5 %copy-start = (f32[8,16384]{1,0:T(8,128)}, f32[8,16384]{1,0:T(8,128)S(1)}, u32[]{:S(2)}) copy-start(f32[8,16384]{1,0:T(8,128)S(1)} %get-tuple-element.30.coef_ref) | copy-start | bytes 1572868

commit v4 on v2

--- a/solution.py
+++ b/solution.py
@@ -28,12 +28,14 @@
 
 
 def pack_kernel(
-    feat_ref, pos_ref, neigh_ref, counts_ref, wave_ref, first_ref, last_ref, waves_ref, sem
+    feat_ref, pos_ref, neigh_ref, counts_ref, wave_ref, first_ref, last_ref, waves_ref,
+    held_ref, sem,
 ):
     slots, own = neigh_ref.shape
     channels = feat_ref.shape[1]
     copy = pltpu.make_async_copy(wave_ref, waves_ref, sem)
     copy.start()
+    held_ref[...] = pos_ref[...]
     rows = lax.broadcasted_iota(jnp.int32, (slots, own), 1)
     slot = lax.broadcasted_iota(jnp.int32, (slots, own), 0)
     delta = (neigh_ref[...] - HALO - rows).astype(F32)
@@ -60,12 +62,10 @@
         return [float(v) for v in cheb.convert(kind=np.polynomial.Polynomial).coef]
 
     root = math.sqrt(2.0)
-    half_sine = fitted(root * np.sin(np.pi * r) / r, 3)
-    half_cosine = fitted(root * np.cos(np.pi * r), 3)
-    return half_sine, half_cosine
-
-
-HALF_SINE, HALF_COSINE = make_series()
+    return fitted(root * np.sin(np.pi * r) / r, 3)
+
+
+HALF_SINE = make_series()
 
 
 def horner(s, coefs):
@@ -113,9 +113,10 @@
             r = t - ((t + magic) - magic)
             s = r * r
             x = r * horner(s, HALF_SINE)
-            y = horner(s, HALF_COSINE)
-            cos_ref[start : start + chunk, span] = (1.0 - x * x).astype(BF16)
-            sin_ref[start : start + chunk, span] = (x * y).astype(BF16)
+            square = x * x
+            rest = jnp.maximum(2.0 - square, 1e-20)
+            cos_ref[start : start + chunk, span] = (1.0 - square).astype(BF16)
+            sin_ref[start : start + chunk, span] = (x * rest * lax.rsqrt(rest)).astype(BF16)
         wave = wave_ref[:, span]
         ksq = jnp.sum(wave * wave, axis=0, keepdims=True)
         coef = factor * jnp.exp(-0.1 * ksq) / ksq
@@ -237,38 +238,40 @@
                 sums_ref[step * per + q, n : n + 1, :] = part[:, q * share : (q + 1) * share]
 
 
-def response_kernel(sums_ref, coef_ref, cos_ref, sin_ref, pot_ref, field_ref, acc_ref):
-    step = pl.program_id(0)
-    per, _, share = sums_ref.shape
+def response_kernel(sums_ref, coef_ref, cos_ref, sin_ref, pot_ref, field_ref, acc_ref, *, tile):
+    groups, _, share = sums_ref.shape
+    per = tile // share
     row = lax.broadcasted_iota(jnp.int32, (8, share), 0)
     lead = row % 4 == 0
     upper = row < 4
     dims = (((1,), (1,)), ((), ()))
-
-    @pl.when(step == 0)
-    def _():
-        acc_ref[...] = jnp.zeros_like(acc_ref)
-
-    factors = ([], [])
-    for q in range(per):
-        scaled = coef_ref[:, q * share : (q + 1) * share]
-        cosine = sums_ref[q, 0:1, :]
-        sine = sums_ref[q, 1:2, :]
-        for n, (top, other) in enumerate(((cosine, -sine), (sine, cosine))):
-            full = scaled * jnp.where(lead, top, other)
-            hi = full.astype(BF16).astype(F32)
-            factors[n].append(jnp.where(upper, hi, full - hi))
-    total = acc_ref[...]
-    for n, ref in enumerate((cos_ref, sin_ref)):
-        wide = jnp.concatenate(factors[n], axis=1).astype(BF16)
-        total = total + lax.dot_general(wide, ref[...], dims, preferred_element_type=F32)
-    acc_ref[...] = total
-
-    @pl.when(step == pl.num_programs(0) - 1)
-    def _():
-        result = acc_ref[:4] + acc_ref[4:]
-        pot_ref[...] = result[0:1]
-        field_ref[...] = result[1:4]
+    acc_ref[...] = jnp.zeros_like(acc_ref)
+
+    @pl.loop(0, groups // per)
+    def _(step):
+        span = pl.ds(pl.multiple_of(step * tile, tile), tile)
+        coef = coef_ref[:, span]
+        factors = ([], [])
+        for q in range(per):
+            scaled = coef[:, q * share : (q + 1) * share]
+            sums = sums_ref[step * per + q].astype(F32)
+            cosine = sums[0:1]
+            sine = sums[1:2]
+            for n, (top, other) in enumerate(((cosine, -sine), (sine, cosine))):
+                full = scaled * jnp.where(lead, top, other)
+                hi = full.astype(BF16).astype(F32)
+                factors[n].append(jnp.where(upper, hi, full - hi))
+        total = acc_ref[...]
+        for n, ref in enumerate((cos_ref, sin_ref)):
+            wide = jnp.concatenate(factors[n], axis=1).astype(BF16)
+            total = total + lax.dot_general(
+                wide, ref[:, span], dims, preferred_element_type=F32
+            )
+        acc_ref[...] = total
+
+    result = acc_ref[:4] + acc_ref[4:]
+    pot_ref[...] = result[0:1]
+    field_ref[...] = result[1:4]
 
 
 def shifted(x, step):
@@ -293,11 +296,11 @@
     )
 
     edge = pltpu.VMEM((half, width), BF16)
-    first, last, waves = pl.pallas_call(
+    first, last, waves, held = pl.pallas_call(
         pack_kernel,
-        out_shape=(edge, edge, pltpu.VMEM(wave.shape, F32)),
+        out_shape=(edge, edge, pltpu.VMEM(wave.shape, F32), pltpu.VMEM(positions.shape, F32)),
         in_specs=[VMEM] * 4 + [HBM],
-        out_specs=(VMEM,) * 3,
+        out_specs=(VMEM,) * 4,
         scratch_shapes=[dma],
     )(features, positions, neighbours.T, counts.reshape(1, own), wave)
     before = shifted(last, 1)
@@ -318,7 +321,7 @@
         cost_estimate=pl.CostEstimate(
             flops=own * total * 40, bytes_accessed=4 * own * total, transcendentals=0
         ),
-    )(positions, waves, w_in, w_out, w_charge)
+    )(held, waves, w_in, w_out, w_charge)
 
     hidden, partial = pl.pallas_call(
         functools.partial(layer_kernel, tile=wide),
@@ -336,30 +339,22 @@
         compiler_params=pltpu.CompilerParams(vmem_limit_bytes=16 << 20),
     )(before, first, last, after, w_first, w_second, w_read, cosine, sine)
 
-    swapped = lax.all_to_all(partial, AXES, 0, 0, tiled=True)
-    mine = jnp.sum(swapped, axis=0)
+    swapped = lax.all_to_all(partial.astype(BF16), AXES, 0, 0, tiled=True)
+    mine = jnp.sum(swapped.astype(F32), axis=0).astype(BF16)
     spread = jnp.broadcast_to(mine[None], (devices, 2, share))
     sums = lax.all_to_all(spread, AXES, 0, 0, tiled=True)
 
-    per = wide // share
-    fixed = lambda step: (0, 0)
-    across = lambda step: (0, step)
+    cosine, sine = (pltpu.with_memory_space_constraint(x, pltpu.VMEM) for x in (cosine, sine))
     potential, field = pl.pallas_call(
-        response_kernel,
-        grid=(total // wide,),
+        functools.partial(response_kernel, tile=wide),
         out_shape=(
             jax.ShapeDtypeStruct((1, own), F32),
             jax.ShapeDtypeStruct((3, own), F32),
         ),
-        in_specs=[
-            pl.BlockSpec((per, 2, share), lambda step: (step, 0, 0)),
-            pl.BlockSpec((8, wide), across),
-            pl.BlockSpec((own, wide), across),
-            pl.BlockSpec((own, wide), across),
-        ],
-        out_specs=(pl.BlockSpec((1, own), fixed), pl.BlockSpec((3, own), fixed)),
+        in_specs=[VMEM] * 4,
+        out_specs=(VMEM, VMEM),
         scratch_shapes=[pltpu.VMEM((8, own), F32)],
-        compiler_params=pltpu.CompilerParams(vmem_limit_bytes=56 << 20),
+        compiler_params=pltpu.CompilerParams(vmem_limit_bytes=4 << 20),
     )(sums, coef, cosine, sine)
     return (hidden, potential.reshape(own), field)
 

time: 69.1 us -> 66.9 us (0.968)
  local copies, waits for them, and re-layouts: 0.73 us -> 6.81 us
  Pallas kernels: 35.1 us -> 29.3 us
  blocking collectives: 25.9 us -> 23.4 us
    unnamed x8, local copies, waits for them, and re-layouts: 0.69 us -> 6.77 us
    pallas_call x1, Pallas kernels: 10.7 us -> 5.87 us  [per_device(): pl.pallas_call(functools.partial(response_kernel, tile=wide), out_shape=(...]
    all_to_all x1, blocking collectives: 10.8 us -> 9.19 us  [per_device(): sums = lax.all_to_all(spread, AXES, 0, 0, tiled=True)]
    pallas_call x1, Pallas kernels: 16 us -> 15 us  [per_device(): pl.pallas_call(functools.partial(trig_kernel, tile=256, chunk=32, factor=...]
    all_to_all x1, blocking collectives: 15.1 us -> 14.2 us  [per_device(): swapped = lax.all_to_all(partial.astype(BF16), AXES, 0, 0, tiled=True)]
where the time goes in v4:
time: 66.9 us; the launch traced here: 66.5 us
  Pallas kernels  29.3 us (44%)
  blocking collectives  23.4 us (35%)
  local copies, waits for them, and re-layouts  6.81 us (10%)
  starting transfers between devices  6.23 us (9%)
  between operations  0.71 us (1%)
    pallas_call x1, Pallas kernels, per_device(): pl.pallas_call(functools.partial(trig_kernel, tile=256, chunk=32, factor=...  15 us
    all_to_all x1, blocking collectives, per_device(): swapped = lax.all_to_all(partial.astype(BF16), AXES, 0, 0, tiled=True)  14.2 us
    all_to_all x1, blocking collectives, per_device(): sums = lax.all_to_all(spread, AXES, 0, 0, tiled=True)  9.19 us
    unnamed x8, local copies, waits for them, and re-layouts  6.77 us
    pallas_call x1, Pallas kernels, per_device(): pl.pallas_call(functools.partial(layer_kernel, tile=wide), out_shape=(jax...  6.48 us
    ppermute x2, starting transfers between devices, shifted(): return lax.ppermute(x, AXES, pairs)  6.23 us
    pallas_call x1, Pallas kernels, per_device(): pl.pallas_call(functools.partial(response_kernel, tile=wide), out_shape=(...  5.87 us
    pallas_call x1, Pallas kernels, per_device(): pl.pallas_call(pack_kernel, out_shape=(edge, edge, pltpu.VMEM(wave.shape,...  1.88 us
  transfers between devices with their start and end apart: 2, of which 0 were waited for; matrix products, arithmetic and copies ran while one was open for 0% of the time, Pallas kernels for 23%

profile of v4, /device:TPU:0, one launch (start us, length us, event | category | flops | bytes accessed | tf_op | source)
XLA Modules:
  0.0 66.5 jit_solution(15544628333810743368)
XLA Ops:
  0.6 1.9 %shard_map.103 = (bf16[128,384]{1,0:T(8,128)(2,1)S(1)}, bf16[128,384]{1,0:T(8,128)(2,1)S(1)}, f32[3,16384]{1,0:T(4,128)S(1)}, f32[3,256]{1,0:T(4,128)S(1)}) custom-call(bf16[256,256]{1,0:T(8,128)(2,1)} %feat_ref.1, f32[3,256]{1,0:T(4,128)} %pos_ref.1, s32[64,256]{1,0:T(8,128)} %bitcast.4, s32[1,256]{1,0:T(1,128)} %bitcast.5, f32[3,16384]{1,0:T(4,128)} %wave_ref.1), custom_call_target="tpu_custom_call" | custom-call | tf_op jit(solution)/shard_map/pallas_call | solution.py:299
  2.5 4.9 %collective-permute-start = (bf16[128,384]{1,0:T(8,128)(2,1)S(1)}, bf16[128,384]{1,0:T(8,128)(2,1)S(1)}, u32[]{:S(2)}, u32[]{:S(2)}) collective-permute-start(bf16[128,384]{1,0:T(8,128)(2,1)S(1)} %get-tuple-element.17.last_ref), channel_id=1, source_target_pairs={{0,1},{1,2},{2,3},{3,4},{4,5},{5,6},{6,7},{7,8},{8,9},{9,10},{10,1... | collective-permute-start | bytes 294920 | tf_op jit(solution)/shard_map/ppermute | solution.py:280
  7.5 1.3 %collective-permute-start.1 = (bf16[128,384]{1,0:T(8,128)(2,1)S(1)}, bf16[128,384]{1,0:T(8,128)(2,1)S(1)}, u32[]{:S(2)}, u32[]{:S(2)}) collective-permute-start(bf16[128,384]{1,0:T(8,128)(2,1)S(1)} %get-tuple-element.18.first_ref), channel_id=1, source_target_pairs={{1,0},{2,1},{3,2},{4,3},{5,4},{6,5},{7,6},{8,7},{9,8},{10,9},{11,1... | collective-permute-start | bytes 294920 | tf_op jit(solution)/shard_map/ppermute | solution.py:280
  8.8 15.0 %shard_map.104 = (bf16[256,16384]{1,0:T(8,128)(2,1)S(1)}, bf16[256,16384]{1,0:T(8,128)(2,1)S(1)}, f32[8,16384]{1,0:T(8,128)S(1)}, bf16[2,256,256]{2,1,0:T(8,128)...) custom-call(f32[3,256]{1,0:T(4,128)S(1)} %get-tuple-element.19.pos_ref, ...), custom_call_target="tpu_custom_call" | custom-call | flops 167772160 | bytes 16777216 | tf_op jit(solution)/shard_map/pallas_call | solution.py:311
  23.8 0.0 copy-start
  23.8 0.0 copy-start.2
  23.8 0.0 collective-permute-done.before_ref
  23.8 0.0 collective-permute-done.1.after_ref
  23.8 6.5 %shard_map.105 = (bf16[256,256]{1,0:T(8,128)(2,1)}, f32[32,2,512]{2,1,0:T(2,128)S(1)}) custom-call(bf16[128,384]{1,0:T(8,128)(2,1)S(1)} %collective-permute-done.before_ref, bf16[128,384]{1,0:T(8,128)(2,1)S(1)} %get-tuple-element.18.first_ref, bf16[128,384]{1,0:T(8,128)(2,1)S(1)} %get-tuple-element.17.last_ref, ...), custom_call_target="tpu_custom_call" | custom-call | tf_op jit(solution)/shard_map/pallas_call | solution.py:326
  30.3 0.0 copy-done
  30.3 0.0 copy-done.2
  30.4 14.2 %all_to_all.10 = bf16[32,2,512]{2,1,0:T(2,128)(2,1)S(1)} all-to-all(bf16[32,2,512]{2,1,0:T(2,128)(2,1)S(1)} %convert_element_type.2), channel_id=1, replica_groups=mesh['brick'=8,'kvec'=4] {'brick','kvec'}, dimensions={0} | all-to-all | bytes 131072 | tf_op jit(solution)/shard_map/all_to_all | solution.py:342
  44.6 0.1 reduce_sum.12
  44.7 9.2 %all_to_all.11.sums_ref = bf16[32,2,512]{2,1,0:T(2,128)(2,1)S(1)} all-to-all(bf16[32,2,512]{2,1,0:T(2,128)(2,1)S(1)} %broadcast_in_dim.2), channel_id=1, replica_groups=mesh['brick'=8,'kvec'=4] {'brick','kvec'}, dimensions={0} | all-to-all | bytes 131072 | tf_op jit(solution)/shard_map/all_to_all | solution.py:345
  53.9 0.0 copy-start.1
  53.9 3.4 %copy-done.1 = bf16[256,16384]{1,0:T(8,128)(2,1)S(1)} copy-done((bf16[256,16384]{1,0:T(8,128)(2,1)S(1)}, bf16[256,16384]{1,0:T(8,128)(2,1)}, u32[]{:S(2)}) %copy-start.1) | copy-done | bytes 8388632
  57.3 0.0 copy-start.3
  57.3 3.4 %copy-done.3 = bf16[256,16384]{1,0:T(8,128)(2,1)S(1)} copy-done((bf16[256,16384]{1,0:T(8,128)(2,1)S(1)}, bf16[256,16384]{1,0:T(8,128)(2,1)}, u32[]{:S(2)}) %copy-start.3) | copy-done | bytes 8388632
  60.7 5.9 %shard_map.106 = (f32[1,256]{1,0:T(1,128)}, f32[3,256]{1,0:T(4,128)}) custom-call(bf16[32,2,512]{2,1,0:T(2,128)(2,1)S(1)} %all_to_all.11.sums_ref, f32[8,16384]{1,0:T(8,128)S(1)} %get-tuple-element.28.coef_ref, bf16[256,16384]{1,0:T(8,128)(2,1)S(1)} %copy-done.1, bf16[256,16384]{1,0:T(8,128)(2,1)S(1)} %copy-done.3), custom_call_target="tpu_custom_call" | custom-call | tf_op jit(solution)/shard_map/pallas_call | solution.py:348
  (2 shorter events, 0.1 us)
Async XLA Ops:
  2.5 21.3 %collective-permute-start = (bf16[128,384]{1,0:T(8,128)(2,1)S(1)}, bf16[128,384]{1,0:T(8,128)(2,1)S(1)}, u32[]{:S(2)}, u32[]{:S(2)}) collective-permute-start(bf16[128,384]{1,0:T(8,128)(2,1)S(1)} %get-tuple-element.17.last_ref), channel_id=1, source_target_pairs={{0,1},{1,2},{2,3},{3,4},{4,5},{5,6},{6,7},{7,8},{8,9},{9,10},{10,1... | collective-permute-start | bytes 294920 | tf_op jit(solution)/shard_map/ppermute | solution.py:280
  7.5 16.4 %collective-permute-start.1 = (bf16[128,384]{1,0:T(8,128)(2,1)S(1)}, bf16[128,384]{1,0:T(8,128)(2,1)S(1)}, u32[]{:S(2)}, u32[]{:S(2)}) collective-permute-start(bf16[128,384]{1,0:T(8,128)(2,1)S(1)} %get-tuple-element.18.first_ref), channel_id=1, source_target_pairs={{1,0},{2,1},{3,2},{4,3},{5,4},{6,5},{7,6},{8,7},{9,8},{10,9},{11,1... | collective-permute-start | bytes 294920 | tf_op jit(solution)/shard_map/ppermute | solution.py:280
  23.8 6.5 %copy-start = (bf16[256,16384]{1,0:T(8,128)(2,1)}, bf16[256,16384]{1,0:T(8,128)(2,1)S(1)}, u32[]{:S(2)}) copy-start(bf16[256,16384]{1,0:T(8,128)(2,1)S(1)} %get-tuple-element.24.cos_ref) | copy-start | bytes 25165828
  23.8 6.5 %copy-start.2 = (bf16[256,16384]{1,0:T(8,128)(2,1)}, bf16[256,16384]{1,0:T(8,128)(2,1)S(1)}, u32[]{:S(2)}) copy-start(bf16[256,16384]{1,0:T(8,128)(2,1)S(1)} %get-tuple-element.25.sin_ref) | copy-start | bytes 25165828
  53.9 3.4 %copy-start.1 = (bf16[256,16384]{1,0:T(8,128)(2,1)S(1)}, bf16[256,16384]{1,0:T(8,128)(2,1)}, u32[]{:S(2)}) copy-start(bf16[256,16384]{1,0:T(8,128)(2,1)} %copy-done) | copy-start | bytes 25165828
  57.3 3.4 %copy-start.3 = (bf16[256,16384]{1,0:T(8,128)(2,1)S(1)}, bf16[256,16384]{1,0:T(8,128)(2,1)}, u32[]{:S(2)}) copy-start(bf16[256,16384]{1,0:T(8,128)(2,1)} %copy-done.2) | copy-start | bytes 25165828

commit v5 on v4

--- a/solution.py
+++ b/solution.py
@@ -3,7 +3,6 @@
 
 import jax
 import jax.numpy as jnp
-import numpy as np
 from jax import lax
 from jax.experimental import pallas as pl
 from jax.experimental.pallas import tpu as pltpu
@@ -51,21 +50,7 @@
     copy.wait()
 
 
-def make_series():
-    nodes = 400
-    x = np.cos((np.arange(nodes) + 0.5) * np.pi / nodes)
-    s = 0.125 * (x + 1.0)
-    r = np.sqrt(s)
-
-    def fitted(values, degree):
-        cheb = np.polynomial.chebyshev.Chebyshev.fit(s, values, degree, domain=[0.0, 0.25])
-        return [float(v) for v in cheb.convert(kind=np.polynomial.Polynomial).coef]
-
-    root = math.sqrt(2.0)
-    return fitted(root * np.sin(np.pi * r) / r, 3)
-
-
-HALF_SINE = make_series()
+HALF_SINE = (4.438831262995637, -7.228964613368321, 3.149392241482131)
 
 
 def horner(s, coefs):
@@ -94,8 +79,8 @@
     left = jnp.concatenate([a, a, b, b, a, c] + [jnp.zeros((80, own), F32)], axis=0)
     left_ref[...] = left.T.astype(BF16)
     tail5 = jnp.zeros((5, tile), F32)
-    magic = 12582912.0
     count = total // tile
+    group = 8
 
     def place(step):
         return pl.ds(pl.multiple_of(step * tile, tile), tile)
@@ -110,28 +95,37 @@
         span = place(step)
         for start in range(0, own, chunk):
             t = in_ref[start : start + chunk, :]
-            r = t - ((t + magic) - magic)
-            s = r * r
-            x = r * horner(s, HALF_SINE)
+            r = t - jnp.round(t)
+            x = r * horner(r * r, HALF_SINE)
             square = x * x
-            rest = jnp.maximum(2.0 - square, 1e-20)
+            rest = 2.000002 - square
             cos_ref[start : start + chunk, span] = (1.0 - square).astype(BF16)
             sin_ref[start : start + chunk, span] = (x * rest * lax.rsqrt(rest)).astype(BF16)
-        wave = wave_ref[:, span]
-        ksq = jnp.sum(wave * wave, axis=0, keepdims=True)
+
+    def scale(step):
+        waves = [wave_ref[:, place(step + n)] for n in range(group)]
+        ksq = jnp.zeros((group, tile), F32)
+        for c in range(3):
+            part = jnp.concatenate([w[c : c + 1] for w in waves], axis=0)
+            ksq = ksq + part * part
         coef = factor * jnp.exp(-0.1 * ksq) / ksq
-        scaled = coef * jnp.concatenate([jnp.ones((1, tile), F32), wave], axis=0)
-        coef_ref[:, span] = jnp.concatenate([scaled, scaled], axis=0)
+        one = jnp.ones((1, tile), F32)
+        for n, w in enumerate(waves):
+            coef_ref[:, place(step + n)] = coef[n : n + 1] * jnp.concatenate(
+                [one, w, one, w], axis=0
+            )
 
     phase(0, even_ref)
 
-    @pl.loop(0, count // 2)
-    def _(pair):
-        step = 2 * pair
-        phase(step + 1, odd_ref)
-        evaluate(step, even_ref)
-        phase(jnp.minimum(step + 2, count - 1), even_ref)
-        evaluate(step + 1, odd_ref)
+    @pl.loop(0, count // group)
+    def _(block):
+        base = group * block
+        scale(base)
+        for step in range(0, group, 2):
+            phase(base + step + 1, odd_ref)
+            evaluate(base + step, even_ref)
+            phase(jnp.minimum(base + step + 2, count - 1), even_ref)
+            evaluate(base + step + 1, odd_ref)
 
     for copy in copies:
         copy.wait()
@@ -231,11 +225,18 @@
     @pl.loop(0, sums_ref.shape[0] // per)
     def _(step):
         span = pl.ds(pl.multiple_of(step * tile, tile), tile)
-        for n, ref in enumerate((cos_ref, sin_ref)):
+        both = []
+        for ref in (cos_ref, sin_ref):
             part = jnp.dot(charges, ref[:, span], preferred_element_type=F32)
-            part = part[0:1] + part[1:2] + part[2:3]
-            for q in range(per):
-                sums_ref[step * per + q, n : n + 1, :] = part[:, q * share : (q + 1) * share]
+            both.append(part[0:1] + part[1:2] + part[2:3])
+        both = jnp.concatenate(both, axis=0).astype(BF16)
+        for q in range(per):
+            sums_ref[step * per + q] = both[:, q * share : (q + 1) * share]
+
+
+def sum_kernel(parts_ref, out_ref):
+    total = jnp.sum(parts_ref[...].astype(F32), axis=0, keepdims=True)
+    out_ref[...] = jnp.broadcast_to(total, parts_ref.shape).astype(BF16)
 
 
 def response_kernel(sums_ref, coef_ref, cos_ref, sin_ref, pot_ref, field_ref, acc_ref, *, tile):
@@ -288,7 +289,7 @@
     width = channels + LANES
     share = total // devices
     factor = 4.0 / math.sqrt(own * devices * total)
-    wide = 2048
+    wide = 4096
     dma = pltpu.SemaphoreType.DMA
     w_charge = w_charge.reshape(1, channels)
     wave, w_in, w_out, w_charge = (
@@ -327,7 +328,7 @@
         functools.partial(layer_kernel, tile=wide),
         out_shape=(
             jax.ShapeDtypeStruct((own, channels), BF16),
-            jax.ShapeDtypeStruct((devices, 2, share), F32),
+            jax.ShapeDtypeStruct((devices, 2, share), BF16),
         ),
         in_specs=[VMEM] * 9,
         out_specs=(VMEM, VMEM),
@@ -339,9 +340,14 @@
         compiler_params=pltpu.CompilerParams(vmem_limit_bytes=16 << 20),
     )(before, first, last, after, w_first, w_second, w_read, cosine, sine)
 
-    swapped = lax.all_to_all(partial.astype(BF16), AXES, 0, 0, tiled=True)
-    mine = jnp.sum(swapped.astype(F32), axis=0).astype(BF16)
-    spread = jnp.broadcast_to(mine[None], (devices, 2, share))
+    swapped = lax.all_to_all(partial, AXES, 0, 0, tiled=True)
+    spread = pl.pallas_call(
+        sum_kernel,
+        out_shape=jax.ShapeDtypeStruct((devices, 2, share), BF16),
+        in_specs=[VMEM],
+        out_specs=VMEM,
+        compiler_params=pltpu.CompilerParams(vmem_limit_bytes=4 << 20),
+    )(swapped)
     sums = lax.all_to_all(spread, AXES, 0, 0, tiled=True)
 
     cosine, sine = (pltpu.with_memory_space_constraint(x, pltpu.VMEM) for x in (cosine, sine))

time: 66.9 us -> 53.2 us (0.80)
  local copies, waits for them, and re-layouts: 6.81 us -> 0 us
  Pallas kernels: 29.3 us -> 22.7 us
    unnamed x8 -> x0, local copies, waits for them, and re-layouts: 6.77 us -> none
    pallas_call x1, Pallas kernels: 15 us -> 9.6 us  [per_device(): pl.pallas_call(functools.partial(trig_kernel, tile=256, chunk=32, factor=...]
    pallas_call x1, Pallas kernels: 6.48 us -> 5.73 us  [per_device(): pl.pallas_call(functools.partial(layer_kernel, tile=wide), out_shape=(jax...]
  transfers between devices with their start and end apart: 2 -> 2, of which waited for: 0 -> 0; matrix products, arithmetic and copies ran while one was open for 0% -> 0% of each run, Pallas kernels for 23% -> 18%
where the time goes in v5:
time: 53.2 us; the launch traced here: 53 us
  blocking collectives  23.4 us (44%)
  Pallas kernels  22.7 us (43%)
  starting transfers between devices  6.23 us (12%)
  between operations  0.68 us (1%)
    all_to_all x1, blocking collectives, per_device(): swapped = lax.all_to_all(partial, AXES, 0, 0, tiled=True)  14.2 us
    pallas_call x1, Pallas kernels, per_device(): pl.pallas_call(functools.partial(trig_kernel, tile=256, chunk=32, factor=...  9.6 us
    all_to_all x1, blocking collectives, per_device(): sums = lax.all_to_all(spread, AXES, 0, 0, tiled=True)  9.19 us
    ppermute x2, starting transfers between devices, shifted(): return lax.ppermute(x, AXES, pairs)  6.23 us
    pallas_call x1, Pallas kernels, per_device(): pl.pallas_call(functools.partial(layer_kernel, tile=wide), out_shape=(jax...  5.73 us
    pallas_call x1, Pallas kernels, per_device(): pl.pallas_call(functools.partial(response_kernel, tile=wide), out_shape=(...  5.4 us
    pallas_call x1, Pallas kernels, per_device(): pl.pallas_call(pack_kernel, out_shape=(edge, edge, pltpu.VMEM(wave.shape,...  1.88 us
  transfers between devices with their start and end apart: 2, of which 0 were waited for; matrix products, arithmetic and copies ran while one was open for 0% of the time, Pallas kernels for 18%

profile of v5, /device:TPU:0, one launch (start us, length us, event | category | flops | bytes accessed | tf_op | source)
XLA Modules:
  0.0 53.0 jit_solution(18024564438865360527)
XLA Ops:
  0.6 1.9 %shard_map.103 = (bf16[128,384]{1,0:T(8,128)(2,1)S(1)}, bf16[128,384]{1,0:T(8,128)(2,1)S(1)}, f32[3,16384]{1,0:T(4,128)S(1)}, f32[3,256]{1,0:T(4,128)S(1)}) custom-call(bf16[256,256]{1,0:T(8,128)(2,1)} %feat_ref.1, f32[3,256]{1,0:T(4,128)} %pos_ref.1, s32[64,256]{1,0:T(8,128)} %bitcast.4, s32[1,256]{1,0:T(1,128)} %bitcast.5, f32[3,16384]{1,0:T(4,128)} %wave_ref.1), custom_call_target="tpu_custom_call" | custom-call | tf_op jit(solution)/shard_map/pallas_call | solution.py:300
  2.5 4.9 %collective-permute-start = (bf16[128,384]{1,0:T(8,128)(2,1)S(1)}, bf16[128,384]{1,0:T(8,128)(2,1)S(1)}, u32[]{:S(2)}, u32[]{:S(2)}) collective-permute-start(bf16[128,384]{1,0:T(8,128)(2,1)S(1)} %get-tuple-element.17.last_ref), channel_id=1, source_target_pairs={{0,1},{1,2},{2,3},{3,4},{4,5},{5,6},{6,7},{7,8},{8,9},{9,10},{10,1... | collective-permute-start | bytes 294920 | tf_op jit(solution)/shard_map/ppermute | solution.py:281
  7.5 1.3 %collective-permute-start.1 = (bf16[128,384]{1,0:T(8,128)(2,1)S(1)}, bf16[128,384]{1,0:T(8,128)(2,1)S(1)}, u32[]{:S(2)}, u32[]{:S(2)}) collective-permute-start(bf16[128,384]{1,0:T(8,128)(2,1)S(1)} %get-tuple-element.18.first_ref), channel_id=1, source_target_pairs={{1,0},{2,1},{3,2},{4,3},{5,4},{6,5},{7,6},{8,7},{9,8},{10,9},{11,1... | collective-permute-start | bytes 294920 | tf_op jit(solution)/shard_map/ppermute | solution.py:281
  8.8 9.6 %shard_map.104 = (bf16[256,16384]{1,0:T(8,128)(2,1)S(1)}, bf16[256,16384]{1,0:T(8,128)(2,1)S(1)}, f32[8,16384]{1,0:T(8,128)S(1)}, bf16[2,256,256]{2,1,0:T(8,128)...) custom-call(f32[3,256]{1,0:T(4,128)S(1)} %get-tuple-element.19.pos_ref, ...), custom_call_target="tpu_custom_call" | custom-call | flops 167772160 | bytes 16777216 | tf_op jit(solution)/shard_map/pallas_call | solution.py:312
  18.4 0.0 collective-permute-done.before_ref
  18.4 0.0 collective-permute-done.1.after_ref
  18.4 5.7 %shard_map.105 = (bf16[256,256]{1,0:T(8,128)(2,1)}, bf16[32,2,512]{2,1,0:T(2,128)(2,1)S(1)}) custom-call(bf16[128,384]{1,0:T(8,128)(2,1)S(1)} %collective-permute-done.before_ref, bf16[128,384]{1,0:T(8,128)(2,1)S(1)} %get-tuple-element.18.first_ref, bf16[128,384]{1,0:T(8,128)(2,1)S(1)} %get-tuple-element.17.last_ref, ...), custom_call_target="tpu_custom_call" | custom-call | tf_op jit(solution)/shard_map/pallas_call | solution.py:327
  24.1 14.2 %all_to_all.10.parts_ref = bf16[32,2,512]{2,1,0:T(2,128)(2,1)S(1)} all-to-all(bf16[32,2,512]{2,1,0:T(2,128)(2,1)S(1)} %get-tuple-element.27), channel_id=1, replica_groups=mesh['brick'=8,'kvec'=4] {'brick','kvec'}, dimensions={0} | all-to-all | bytes 131072 | tf_op jit(solution)/shard_map/all_to_all | solution.py:343
  38.3 0.1 shard_map.106
  38.4 9.2 %all_to_all.11.sums_ref = bf16[32,2,512]{2,1,0:T(2,128)(2,1)S(1)} all-to-all(bf16[32,2,512]{2,1,0:T(2,128)(2,1)S(1)} %shard_map.106), channel_id=1, replica_groups=mesh['brick'=8,'kvec'=4] {'brick','kvec'}, dimensions={0} | all-to-all | bytes 131072 | tf_op jit(solution)/shard_map/all_to_all | solution.py:351
  47.6 5.4 %shard_map.107 = (f32[1,256]{1,0:T(1,128)}, f32[3,256]{1,0:T(4,128)}) custom-call(bf16[32,2,512]{2,1,0:T(2,128)(2,1)S(1)} %all_to_all.11.sums_ref, f32[8,16384]{1,0:T(8,128)S(1)} %get-tuple-element.28.coef_ref, bf16[256,16384]{1,0:T(8,128)(2,1)S(1)} %get-tuple-element.24.cos_ref, bf16[256,16384]{1,0:T(8,128)(2,1)S(1)} %get-tuple-element.25.sin_ref), custom_call_target="tpu_custom_call" | custom-call | tf_op jit(solution)/shard_map/pallas_call | solution.py:354
Async XLA Ops:
  2.5 15.8 %collective-permute-start = (bf16[128,384]{1,0:T(8,128)(2,1)S(1)}, bf16[128,384]{1,0:T(8,128)(2,1)S(1)}, u32[]{:S(2)}, u32[]{:S(2)}) collective-permute-start(bf16[128,384]{1,0:T(8,128)(2,1)S(1)} %get-tuple-element.17.last_ref), channel_id=1, source_target_pairs={{0,1},{1,2},{2,3},{3,4},{4,5},{5,6},{6,7},{7,8},{8,9},{9,10},{10,1... | collective-permute-start | bytes 294920 | tf_op jit(solution)/shard_map/ppermute | solution.py:281
  7.5 10.9 %collective-permute-start.1 = (bf16[128,384]{1,0:T(8,128)(2,1)S(1)}, bf16[128,384]{1,0:T(8,128)(2,1)S(1)}, u32[]{:S(2)}, u32[]{:S(2)}) collective-permute-start(bf16[128,384]{1,0:T(8,128)(2,1)S(1)} %get-tuple-element.18.first_ref), channel_id=1, source_target_pairs={{1,0},{2,1},{3,2},{4,3},{5,4},{6,5},{7,6},{8,7},{9,8},{10,9},{11,1... | collective-permute-start | bytes 294920 | tf_op jit(solution)/shard_map/ppermute | solution.py:281

commit v6 on v5

--- a/solution.py
+++ b/solution.py
@@ -348,7 +348,10 @@
         out_specs=VMEM,
         compiler_params=pltpu.CompilerParams(vmem_limit_bytes=4 << 20),
     )(swapped)
-    sums = lax.all_to_all(spread, AXES, 0, 0, tiled=True)
+    near = lax.axis_size("kvec")
+    sums = lax.all_to_all(spread[:near], "kvec", 0, 0, tiled=True)
+    sums = jnp.broadcast_to(sums[None], (devices // near, near, 2, share))
+    sums = lax.all_to_all(sums, "brick", 0, 0, tiled=True).reshape(devices, 2, share)
 
     cosine, sine = (pltpu.with_memory_space_constraint(x, pltpu.VMEM) for x in (cosine, sine))
     potential, field = pl.pallas_call(

time: 53.2 us -> 59.5 us (1.12)
  blocking collectives: 23.4 us -> 29.5 us
    all_to_all x1 -> x2, blocking collectives: 9.19 us -> 15.3 us  [the longest x1 7.93 us: per_device(): sums = lax.all_to_all(spread[:near], 'kvec', 0, 0, tiled=True)]
  transfers between devices with their start and end apart: 2 -> 2, of which waited for: 0 -> 0; matrix products, arithmetic and copies ran while one was open for 0% -> 0% of each run, Pallas kernels for 18% -> 16%
where the time goes in v6:
time: 59.5 us; the launch traced here: 59.2 us
  blocking collectives  29.5 us (50%)
  Pallas kernels  22.7 us (38%)
  starting transfers between devices  6.23 us (10%)
  between operations  0.7 us (1%)
    all_to_all x1, blocking collectives, per_device(): swapped = lax.all_to_all(partial, AXES, 0, 0, tiled=True)  14.2 us
    pallas_call x1, Pallas kernels, per_device(): pl.pallas_call(functools.partial(trig_kernel, tile=256, chunk=32, factor=...  9.6 us
    all_to_all x1, blocking collectives, per_device(): sums = lax.all_to_all(spread[:near], 'kvec', 0, 0, tiled=True)  7.93 us
    all_to_all x1, blocking collectives, per_device(): lax.all_to_all(sums, 'brick', 0, 0, tiled=True).reshape(devices, 2, share)  7.4 us
    ppermute x2, starting transfers between devices, shifted(): return lax.ppermute(x, AXES, pairs)  6.23 us
    pallas_call x1, Pallas kernels, per_device(): pl.pallas_call(functools.partial(layer_kernel, tile=wide), out_shape=(jax...  5.73 us
    pallas_call x1, Pallas kernels, per_device(): pl.pallas_call(functools.partial(response_kernel, tile=wide), out_shape=(...  5.4 us
    pallas_call x1, Pallas kernels, per_device(): pl.pallas_call(pack_kernel, out_shape=(edge, edge, pltpu.VMEM(wave.shape,...  1.88 us
  transfers between devices with their start and end apart: 2, of which 0 were waited for; matrix products, arithmetic and copies ran while one was open for 0% of the time, Pallas kernels for 16%

profile of v6, /device:TPU:0, one launch (start us, length us, event | category | flops | bytes accessed | tf_op | source)
XLA Modules:
  0.0 59.2 jit_solution(16309105048819469599)
XLA Ops:
  0.6 1.9 %shard_map.103 = (bf16[128,384]{1,0:T(8,128)(2,1)S(1)}, bf16[128,384]{1,0:T(8,128)(2,1)S(1)}, f32[3,16384]{1,0:T(4,128)S(1)}, f32[3,256]{1,0:T(4,128)S(1)}) custom-call(bf16[256,256]{1,0:T(8,128)(2,1)} %feat_ref.1, f32[3,256]{1,0:T(4,128)} %pos_ref.1, s32[64,256]{1,0:T(8,128)} %bitcast.6, s32[1,256]{1,0:T(1,128)} %bitcast.7, f32[3,16384]{1,0:T(4,128)} %wave_ref.1), custom_call_target="tpu_custom_call" | custom-call | tf_op jit(solution)/shard_map/pallas_call | solution.py:300
  2.5 4.9 %collective-permute-start = (bf16[128,384]{1,0:T(8,128)(2,1)S(1)}, bf16[128,384]{1,0:T(8,128)(2,1)S(1)}, u32[]{:S(2)}, u32[]{:S(2)}) collective-permute-start(bf16[128,384]{1,0:T(8,128)(2,1)S(1)} %get-tuple-element.17.last_ref), channel_id=1, source_target_pairs={{0,1},{1,2},{2,3},{3,4},{4,5},{5,6},{6,7},{7,8},{8,9},{9,10},{10,1... | collective-permute-start | bytes 294920 | tf_op jit(solution)/shard_map/ppermute | solution.py:281
  7.5 1.3 %collective-permute-start.1 = (bf16[128,384]{1,0:T(8,128)(2,1)S(1)}, bf16[128,384]{1,0:T(8,128)(2,1)S(1)}, u32[]{:S(2)}, u32[]{:S(2)}) collective-permute-start(bf16[128,384]{1,0:T(8,128)(2,1)S(1)} %get-tuple-element.18.first_ref), channel_id=1, source_target_pairs={{1,0},{2,1},{3,2},{4,3},{5,4},{6,5},{7,6},{8,7},{9,8},{10,9},{11,1... | collective-permute-start | bytes 294920 | tf_op jit(solution)/shard_map/ppermute | solution.py:281
  8.8 9.6 %shard_map.104 = (bf16[256,16384]{1,0:T(8,128)(2,1)S(1)}, bf16[256,16384]{1,0:T(8,128)(2,1)S(1)}, f32[8,16384]{1,0:T(8,128)S(1)}, bf16[2,256,256]{2,1,0:T(8,128)...) custom-call(f32[3,256]{1,0:T(4,128)S(1)} %get-tuple-element.19.pos_ref, ...), custom_call_target="tpu_custom_call" | custom-call | flops 167772160 | bytes 16777216 | tf_op jit(solution)/shard_map/pallas_call | solution.py:312
  18.4 0.0 collective-permute-done.before_ref
  18.4 0.0 collective-permute-done.1.after_ref
  18.4 5.7 %shard_map.105 = (bf16[256,256]{1,0:T(8,128)(2,1)}, bf16[32,2,512]{2,1,0:T(2,128)(2,1)S(1)}) custom-call(bf16[128,384]{1,0:T(8,128)(2,1)S(1)} %collective-permute-done.before_ref, bf16[128,384]{1,0:T(8,128)(2,1)S(1)} %get-tuple-element.18.first_ref, bf16[128,384]{1,0:T(8,128)(2,1)S(1)} %get-tuple-element.17.last_ref, ...), custom_call_target="tpu_custom_call" | custom-call | tf_op jit(solution)/shard_map/pallas_call | solution.py:327
  24.1 14.2 %all_to_all.15.parts_ref = bf16[32,2,512]{2,1,0:T(2,128)(2,1)S(1)} all-to-all(bf16[32,2,512]{2,1,0:T(2,128)(2,1)S(1)} %get-tuple-element.27), channel_id=1, replica_groups=mesh['brick'=8,'kvec'=4] {'brick','kvec'}, dimensions={0} | all-to-all | bytes 131072 | tf_op jit(solution)/shard_map/all_to_all | solution.py:343
  38.3 0.1 shard_map.106
  38.4 7.9 %all_to_all.16 = bf16[4,2,512]{2,1,0:T(2,128)(2,1)S(1)} all-to-all(bf16[4,2,512]{2,1,0:T(2,128)(2,1)S(1)} %slice.4), channel_id=1, replica_groups=mesh['brick'=8,'kvec'=4] {'kvec'}, dimensions={0} | all-to-all | bytes 16384 | tf_op jit(solution)/shard_map/all_to_all | solution.py:352
  46.4 7.4 %all_to_all.17 = bf16[8,4,2,512]{3,2,1,0:T(2,128)(2,1)S(1)} all-to-all(bf16[8,4,2,512]{3,2,1,0:T(2,128)(2,1)S(1)} %broadcast_in_dim.2), channel_id=1, replica_groups=mesh['brick'=8,'kvec'=4] {'brick'}, dimensions={0} | all-to-all | bytes 131072 | tf_op jit(solution)/shard_map/all_to_all | solution.py:354
  53.8 5.4 %shard_map.107 = (f32[1,256]{1,0:T(1,128)}, f32[3,256]{1,0:T(4,128)}) custom-call(bf16[32,2,512]{2,1,0:T(2,128)(2,1)S(1)} %bitcast.5, f32[8,16384]{1,0:T(8,128)S(1)} %get-tuple-element.28.coef_ref, bf16[256,16384]{1,0:T(8,128)(2,1)S(1)} %get-tuple-element.24.cos_ref, bf16[256,16384]{1,0:T(8,128)(2,1)S(1)} %get-tuple-element.25.sin_ref), custom_call_target="tpu_custom_call" | custom-call | tf_op jit(solution)/shard_map/pallas_call | solution.py:357
  (2 shorter events, 0.0 us)
Async XLA Ops:
  2.5 15.8 %collective-permute-start = (bf16[128,384]{1,0:T(8,128)(2,1)S(1)}, bf16[128,384]{1,0:T(8,128)(2,1)S(1)}, u32[]{:S(2)}, u32[]{:S(2)}) collective-permute-start(bf16[128,384]{1,0:T(8,128)(2,1)S(1)} %get-tuple-element.17.last_ref), channel_id=1, source_target_pairs={{0,1},{1,2},{2,3},{3,4},{4,5},{5,6},{6,7},{7,8},{8,9},{9,10},{10,1... | collective-permute-start | bytes 294920 | tf_op jit(solution)/shard_map/ppermute | solution.py:281
  7.5 10.9 %collective-permute-start.1 = (bf16[128,384]{1,0:T(8,128)(2,1)S(1)}, bf16[128,384]{1,0:T(8,128)(2,1)S(1)}, u32[]{:S(2)}, u32[]{:S(2)}) collective-permute-start(bf16[128,384]{1,0:T(8,128)(2,1)S(1)} %get-tuple-element.18.first_ref), channel_id=1, source_target_pairs={{1,0},{2,1},{3,2},{4,3},{5,4},{6,5},{7,6},{8,7},{9,8},{10,9},{11,1... | collective-permute-start | bytes 294920 | tf_op jit(solution)/shard_map/ppermute | solution.py:281

commit v7 on v5

--- a/solution.py
+++ b/solution.py
@@ -60,12 +60,69 @@
     return value
 
 
-def trig_kernel(
-    pos_ref, wave_ref, w_in_ref, w_out_ref, w_charge_ref, cos_ref, sin_ref, coef_ref, w_in_out,
-    w_out_out, w_charge_out, left_ref, even_ref, odd_ref, sems, *, tile, chunk, factor,
+def atom_pieces(pos_ref):
+    a, b, c = pieces(pos_ref[...])
+    own = pos_ref.shape[1]
+    left = jnp.concatenate([a, a, b, b, a, c, jnp.zeros((14, own), F32)], axis=0)
+    return left.astype(BF16)
+
+
+def place(step, tile):
+    return pl.ds(pl.multiple_of(step * tile, tile), tile)
+
+
+def phase(wave, left_ref, out_ref):
+    tile = wave.shape[1]
+    u, v, w = pieces(wave * (0.5 / math.pi))
+    right = jnp.concatenate([u, v, u, v, w, u, jnp.zeros((14, tile), F32)], axis=0)
+    out_ref[...] = jnp.dot(right.T.astype(BF16), left_ref[...], preferred_element_type=F32)
+
+
+def evaluate(in_ref, stores, chunk):
+    for start in range(0, in_ref.shape[0], chunk):
+        t = in_ref[start : start + chunk, :]
+        r = t - jnp.round(t)
+        x = r * horner(r * r, HALF_SINE)
+        square = x * x
+        rest = 2.000002 - square
+        cosine = (1.0 - square).astype(BF16)
+        sine = (x * rest * lax.rsqrt(rest)).astype(BF16)
+        for store in stores:
+            store(start, cosine, sine)
+
+
+def into_table(cos_ref, sin_ref, step, tile, chunk):
+    def store(start, cosine, sine):
+        rows = pl.ds(pl.multiple_of(step * tile + start, chunk), chunk)
+        cos_ref[rows, :] = cosine
+        sin_ref[rows, :] = sine
+
+    return store
+
+
+def into_tile(tile_ref, chunk):
+    def store(start, cosine, sine):
+        tile_ref[0, start : start + chunk, :] = cosine
+        tile_ref[1, start : start + chunk, :] = sine
+
+    return store
+
+
+def histogram(delta):
+    place = jnp.where(delta > 0, delta + 63.0, delta + 64.0)
+    place = jnp.where(delta == 0, -1.0, place)
+    deep = lax.broadcasted_iota(jnp.int32, (LANES, LANES), 0).astype(F32)
+    hist = jnp.zeros((LANES, LANES), F32)
+    for slot in range(64):
+        hist = hist + jnp.where(deep == place[slot : slot + 1, :], 1.0, 0.0)
+    return hist.T
+
+
+def early_kernel(
+    pos_ref, wave_ref, first_ref, last_ref, w_in_ref, w_out_ref, w_charge_ref, cos_ref, sin_ref,
+    coef_ref, hist_ref, w_in_out, w_out_out, w_charge_out, left_ref, even_ref, odd_ref, sems,
+    *, tile, chunk, factor,
 ):
-    own = pos_ref.shape[1]
-    total = wave_ref.shape[1]
     copies = [
         pltpu.make_async_copy(source, target, sems.at[n])
         for n, (source, target) in enumerate(
@@ -74,36 +131,15 @@
     ]
     for copy in copies:
         copy.start()
-    zero5 = jnp.zeros((5, own), F32)
-    a, b, c = (jnp.concatenate([p, zero5], axis=0) for p in pieces(pos_ref[...]))
-    left = jnp.concatenate([a, a, b, b, a, c] + [jnp.zeros((80, own), F32)], axis=0)
-    left_ref[...] = left.T.astype(BF16)
-    tail5 = jnp.zeros((5, tile), F32)
-    count = total // tile
+    left_ref[...] = atom_pieces(pos_ref)
+    channels = w_in_ref.shape[1]
+    for n, ref in enumerate((first_ref, last_ref)):
+        hist_ref[n * LANES : (n + 1) * LANES, :] = histogram(ref[:64, channels:].astype(F32))
+    head = cos_ref.shape[0] // tile
     group = 8
 
-    def place(step):
-        return pl.ds(pl.multiple_of(step * tile, tile), tile)
-
-    def phase(step, out_ref):
-        turns = wave_ref[:, place(step)] * (0.5 / math.pi)
-        u, v, w = (jnp.concatenate([p, tail5], axis=0) for p in pieces(turns))
-        right = jnp.concatenate([u, v, u, v, w, u] + [jnp.zeros((80, tile), F32)], axis=0)
-        out_ref[...] = jnp.dot(left_ref[...], right.astype(BF16), preferred_element_type=F32)
-
-    def evaluate(step, in_ref):
-        span = place(step)
-        for start in range(0, own, chunk):
-            t = in_ref[start : start + chunk, :]
-            r = t - jnp.round(t)
-            x = r * horner(r * r, HALF_SINE)
-            square = x * x
-            rest = 2.000002 - square
-            cos_ref[start : start + chunk, span] = (1.0 - square).astype(BF16)
-            sin_ref[start : start + chunk, span] = (x * rest * lax.rsqrt(rest)).astype(BF16)
-
     def scale(step):
-        waves = [wave_ref[:, place(step + n)] for n in range(group)]
+        waves = [wave_ref[:, place(step + n, tile)] for n in range(group)]
         ksq = jnp.zeros((group, tile), F32)
         for c in range(3):
             part = jnp.concatenate([w[c : c + 1] for w in waves], axis=0)
@@ -111,21 +147,25 @@
         coef = factor * jnp.exp(-0.1 * ksq) / ksq
         one = jnp.ones((1, tile), F32)
         for n, w in enumerate(waves):
-            coef_ref[:, place(step + n)] = coef[n : n + 1] * jnp.concatenate(
+            coef_ref[:, place(step + n, tile)] = coef[n : n + 1] * jnp.concatenate(
                 [one, w, one, w], axis=0
             )
 
-    phase(0, even_ref)
-
-    @pl.loop(0, count // group)
+    def turn(step, out_ref):
+        phase(wave_ref[:, place(step, tile)], left_ref, out_ref)
+
+    turn(0, even_ref)
+
+    @pl.loop(0, head // 4)
     def _(block):
-        base = group * block
-        scale(base)
-        for step in range(0, group, 2):
-            phase(base + step + 1, odd_ref)
-            evaluate(base + step, even_ref)
-            phase(jnp.minimum(base + step + 2, count - 1), even_ref)
-            evaluate(base + step + 1, odd_ref)
+        base = 4 * block
+        scale(4 * base)
+        scale(4 * base + group)
+        for step in range(0, 4, 2):
+            turn(base + step + 1, odd_ref)
+            evaluate(even_ref, [into_table(cos_ref, sin_ref, base + step, tile, chunk)], chunk)
+            turn(jnp.minimum(base + step + 2, head - 1), even_ref)
+            evaluate(odd_ref, [into_table(cos_ref, sin_ref, base + step + 1, tile, chunk)], chunk)
 
     for copy in copies:
         copy.wait()
@@ -136,8 +176,10 @@
 
 
 def layer_kernel(
-    before_ref, first_ref, last_ref, after_ref, w_in_ref, w_out_ref, w_charge_ref, cos_ref,
-    sin_ref, hidden_ref, sums_ref, feat_ref, mid_ref, matrix_ref, *, tile,
+    before_ref, first_ref, last_ref, after_ref, w_in_ref, w_out_ref, w_charge_ref, hist_ref,
+    pos_ref, wave_ref, cos_head_ref, sin_head_ref, hidden_ref, sums_ref, cos_ref, sin_ref,
+    feat_ref, mid_ref, matrix_ref, left_ref, charge_ref, even_ref, odd_ref, even_tile_ref,
+    odd_tile_ref, *, tile, chunk,
 ):
     parts = (before_ref, first_ref, last_ref, after_ref)
     half = before_ref.shape[0]
@@ -151,19 +193,9 @@
     ext_rows = jnp.concatenate(rows + [jnp.zeros((8, LANES), F32)], axis=1)
     ext_cols = jnp.concatenate([r.T for r in rows], axis=0)
     lane = lax.broadcasted_iota(jnp.int32, (HALO, LANES), 1)
-    deep = lax.broadcasted_iota(jnp.int32, (LANES, LANES), 0).astype(F32)
-    deltas = [e[:64] for e in extras]
-    ends = jnp.where(lane < HALO, deltas[3], deltas[0])
-    hists = []
-    for delta in (ends, deltas[1], deltas[2]):
-        place = jnp.where(delta > 0, delta + 63.0, delta + 64.0)
-        place = jnp.where(delta == 0, -1.0, place)
-        hist = jnp.zeros((LANES, LANES), F32)
-        for slot in range(64):
-            hist = hist + jnp.where(deep == place[slot : slot + 1, :], 1.0, 0.0)
-        hists.append(hist.T)
-    hist_all = (hists[0][HALO:], hists[1][:HALO], hists[1][HALO:], hists[2][:HALO])
-    hist_all = hist_all + (hists[2][HALO:], hists[0][:HALO])
+    ends = histogram(jnp.where(lane < HALO, extras[3][:64], extras[0][:64]))
+    inner = [hist_ref[n * HALO : (n + 1) * HALO, :] for n in range(own // HALO)]
+    hist_all = [ends[HALO:]] + inner + [ends[:HALO]]
     blocks = (own + 2 * HALO) // HALO
     zeros = jnp.zeros((HALO, LANES), F32)
     for block in range(blocks):
@@ -219,19 +251,59 @@
     hi, mid, lo = pieces(charge)
     charges = jnp.concatenate([hi, mid, lo, jnp.zeros((5, own), F32)], axis=0).astype(BF16)
 
+    charge_ref[...] = charges
+    left_ref[...] = atom_pieces(pos_ref)
+    head = cos_head_ref.shape[0] // tile
+    late = cos_ref.shape[0] // tile
     share = sums_ref.shape[2]
-    per = tile // share
-
-    @pl.loop(0, sums_ref.shape[0] // per)
-    def _(step):
-        span = pl.ds(pl.multiple_of(step * tile, tile), tile)
-        both = []
-        for ref in (cos_ref, sin_ref):
-            part = jnp.dot(charges, ref[:, span], preferred_element_type=F32)
-            both.append(part[0:1] + part[1:2] + part[2:3])
-        both = jnp.concatenate(both, axis=0).astype(BF16)
+    per = 2 * tile // share
+    dims = (((1,), (1,)), ((), ()))
+
+    def turn(step, out_ref):
+        phase(wave_ref[:, place(head + step, tile)], left_ref, out_ref)
+
+    def added(table):
+        part = lax.dot_general(charge_ref[...], table, dims, preferred_element_type=F32)
+        return part[0:1] + part[1:2] + part[2:3]
+
+    def keep(index, pair):
         for q in range(per):
-            sums_ref[step * per + q] = both[:, q * share : (q + 1) * share]
+            sums_ref[index * per + q] = pair[:, q * share : (q + 1) * share].astype(BF16)
+
+    def joined(parts):
+        return jnp.concatenate(
+            [jnp.concatenate(list(row), axis=1) for row in zip(*parts)], axis=0
+        )
+
+    turn(0, even_ref)
+
+    @pl.loop(0, head // 2)
+    def _(block):
+        parts = []
+        for n in range(2):
+            rows = place(2 * block + n, tile)
+            parts.append((added(cos_head_ref[rows, :]), added(sin_head_ref[rows, :])))
+        keep(block, joined(parts))
+        for pair in range(3):
+            step = 6 * block + 2 * pair
+            turn(step + 1, odd_ref)
+            evaluate(
+                even_ref,
+                [into_table(cos_ref, sin_ref, step, tile, chunk), into_tile(even_tile_ref, chunk)],
+                chunk,
+            )
+            turn(jnp.minimum(step + 2, late - 1), even_ref)
+            parts = [(added(even_tile_ref[0]), added(even_tile_ref[1]))]
+            evaluate(
+                odd_ref,
+                [
+                    into_table(cos_ref, sin_ref, step + 1, tile, chunk),
+                    into_tile(odd_tile_ref, chunk),
+                ],
+                chunk,
+            )
+            parts.append((added(odd_tile_ref[0]), added(odd_tile_ref[1])))
+            keep(head // 2 + 3 * block + pair, joined(parts))
 
 
 def sum_kernel(parts_ref, out_ref):
@@ -239,38 +311,35 @@
     out_ref[...] = jnp.broadcast_to(total, parts_ref.shape).astype(BF16)
 
 
-def response_kernel(sums_ref, coef_ref, cos_ref, sin_ref, pot_ref, field_ref, acc_ref, *, tile):
-    groups, _, share = sums_ref.shape
+def response_kernel(
+    sums_ref, coef_ref, cos_head_ref, sin_head_ref, cos_ref, sin_ref, pot_ref, field_ref, *, tile
+):
+    share = sums_ref.shape[2]
     per = tile // share
     row = lax.broadcasted_iota(jnp.int32, (8, share), 0)
     lead = row % 4 == 0
     upper = row < 4
-    dims = (((1,), (1,)), ((), ()))
-    acc_ref[...] = jnp.zeros_like(acc_ref)
-
-    @pl.loop(0, groups // per)
-    def _(step):
-        span = pl.ds(pl.multiple_of(step * tile, tile), tile)
-        coef = coef_ref[:, span]
+    totals = []
+    segments = [(cos_head_ref, sin_head_ref, k) for k in range(0, cos_head_ref.shape[0], tile)]
+    segments += [(cos_ref, sin_ref, k) for k in range(0, cos_ref.shape[0], tile)]
+    for index, (cos_part, sin_part, start) in enumerate(segments):
         factors = ([], [])
-        for q in range(per):
-            scaled = coef[:, q * share : (q + 1) * share]
-            sums = sums_ref[step * per + q].astype(F32)
+        for q in range(index * per, (index + 1) * per):
+            scaled = coef_ref[:, q * share : (q + 1) * share]
+            sums = sums_ref[q].astype(F32)
             cosine = sums[0:1]
             sine = sums[1:2]
             for n, (top, other) in enumerate(((cosine, -sine), (sine, cosine))):
                 full = scaled * jnp.where(lead, top, other)
                 hi = full.astype(BF16).astype(F32)
                 factors[n].append(jnp.where(upper, hi, full - hi))
-        total = acc_ref[...]
-        for n, ref in enumerate((cos_ref, sin_ref)):
+        for n, ref in enumerate((cos_part, sin_part)):
             wide = jnp.concatenate(factors[n], axis=1).astype(BF16)
-            total = total + lax.dot_general(
-                wide, ref[:, span], dims, preferred_element_type=F32
+            totals.append(
+                jnp.dot(wide, ref[start : start + tile, :], preferred_element_type=F32)
             )
-        acc_ref[...] = total
-
-    result = acc_ref[:4] + acc_ref[4:]
+    total = sum(totals[1:], totals[0])
+    result = total[:4] + total[4:]
     pot_ref[...] = result[0:1]
     field_ref[...] = result[1:4]
 
@@ -289,7 +358,6 @@
     width = channels + LANES
     share = total // devices
     factor = 4.0 / math.sqrt(own * devices * total)
-    wide = 4096
     dma = pltpu.SemaphoreType.DMA
     w_charge = w_charge.reshape(1, channels)
     wave, w_in, w_out, w_charge = (
@@ -307,38 +375,54 @@
     before = shifted(last, 1)
     after = shifted(first, -1)
 
-    table = pltpu.VMEM((own, total), BF16)
+    early = total // 4
+    tile, chunk = 256, 32
     kept = pltpu.VMEM(w_in.shape, BF16)
-    cosine, sine, coef, w_first, w_second, w_read = pl.pallas_call(
-        functools.partial(trig_kernel, tile=256, chunk=32, factor=factor),
-        out_shape=(table, table, pltpu.VMEM((8, total), F32), kept, kept)
-        + (pltpu.VMEM((1, channels), F32),),
-        in_specs=[VMEM] * 2 + [HBM] * 3,
-        out_specs=(VMEM,) * 6,
-        scratch_shapes=[pltpu.VMEM((own, LANES), BF16)]
-        + [pltpu.VMEM((own, 256), F32)] * 2
-        + [dma((3,))],
-        compiler_params=pltpu.CompilerParams(vmem_limit_bytes=16 << 20),
+    table = pltpu.VMEM((early, own), BF16)
+    phases = [pltpu.VMEM((tile, own), F32)] * 2
+    grant = pltpu.CompilerParams(vmem_limit_bytes=16 << 20)
+    cos_head, sin_head, coef, hist, w_first, w_second, w_read = pl.pallas_call(
+        functools.partial(early_kernel, tile=tile, chunk=chunk, factor=factor),
+        out_shape=(
+            table,
+            table,
+            pltpu.VMEM((8, total), F32),
+            pltpu.VMEM((own, LANES), F32),
+            kept,
+            kept,
+            pltpu.VMEM((1, channels), F32),
+        ),
+        in_specs=[VMEM] * 4 + [HBM] * 3,
+        out_specs=(VMEM,) * 7,
+        scratch_shapes=[pltpu.VMEM((32, own), BF16)] + phases + [dma((3,))],
+        compiler_params=grant,
         cost_estimate=pl.CostEstimate(
-            flops=own * total * 40, bytes_accessed=4 * own * total, transcendentals=0
+            flops=own * early * 40, bytes_accessed=4 * own * early, transcendentals=0
         ),
-    )(held, waves, w_in, w_out, w_charge)
-
-    hidden, partial = pl.pallas_call(
-        functools.partial(layer_kernel, tile=wide),
+    )(held, waves, first, last, w_in, w_out, w_charge)
+
+    table = pltpu.VMEM((total - early, own), BF16)
+    hidden, partial, cos_late, sin_late = pl.pallas_call(
+        functools.partial(layer_kernel, tile=tile, chunk=chunk),
         out_shape=(
             jax.ShapeDtypeStruct((own, channels), BF16),
             jax.ShapeDtypeStruct((devices, 2, share), BF16),
+            table,
+            table,
         ),
-        in_specs=[VMEM] * 9,
-        out_specs=(VMEM, VMEM),
+        in_specs=[VMEM] * 12,
+        out_specs=(VMEM,) * 4,
         scratch_shapes=[
             pltpu.VMEM((4 * half + HALO, channels), BF16),
             pltpu.VMEM((own + 3 * HALO, channels), BF16),
             pltpu.VMEM((own // HALO + 2, 2 * HALO, 2 * LANES), BF16),
-        ],
-        compiler_params=pltpu.CompilerParams(vmem_limit_bytes=16 << 20),
-    )(before, first, last, after, w_first, w_second, w_read, cosine, sine)
+            pltpu.VMEM((32, own), BF16),
+            pltpu.VMEM((8, own), BF16),
+        ]
+        + phases
+        + [pltpu.VMEM((2, tile, own), BF16)] * 2,
+        compiler_params=grant,
+    )(before, first, last, after, w_first, w_second, w_read, hist, held, waves, cos_head, sin_head)
 
     swapped = lax.all_to_all(partial, AXES, 0, 0, tiled=True)
     spread = pl.pallas_call(
@@ -350,18 +434,20 @@
     )(swapped)
     sums = lax.all_to_all(spread, AXES, 0, 0, tiled=True)
 
-    cosine, sine = (pltpu.with_memory_space_constraint(x, pltpu.VMEM) for x in (cosine, sine))
+    tables = [
+        pltpu.with_memory_space_constraint(x, pltpu.VMEM)
+        for x in (cos_head, sin_head, cos_late, sin_late)
+    ]
     potential, field = pl.pallas_call(
-        functools.partial(response_kernel, tile=wide),
+        functools.partial(response_kernel, tile=4096),
         out_shape=(
             jax.ShapeDtypeStruct((1, own), F32),
             jax.ShapeDtypeStruct((3, own), F32),
         ),
-        in_specs=[VMEM] * 4,
+        in_specs=[VMEM] * 6,
         out_specs=(VMEM, VMEM),
-        scratch_shapes=[pltpu.VMEM((8, own), F32)],
         compiler_params=pltpu.CompilerParams(vmem_limit_bytes=4 << 20),
-    )(sums, coef, cosine, sine)
+    )(sums, coef, *tables)
     return (hidden, potential.reshape(own), field)
 
 

time: 53.2 us -> 53.1 us (level)
  waiting for transfers between devices: 0.01 us -> 2.38 us
  Pallas kernels: 22.7 us -> 21.1 us
  blocking collectives: 23.4 us -> 22.4 us
    ppermute x2, waiting for transfers between devices: 0.01 us -> 2.38 us  [shifted(): return lax.ppermute(x, AXES, pairs)]
    pallas_call x3, Pallas kernels: 20.7 us -> 19.1 us  [the longest x1 12.2 us: per_device(): pl.pallas_call(functools.partial(layer_kernel, tile=tile, chunk=chunk), o...]
    all_to_all x1, blocking collectives: 14.2 us -> 13.2 us  [per_device(): swapped = lax.all_to_all(partial, AXES, 0, 0, tiled=True)]
  transfers between devices with their start and end apart: 2 -> 2, of which waited for: 0 -> 1; matrix products, arithmetic and copies ran while one was open for 0% -> 0% of each run, Pallas kernels for 18% -> 8%
where the time goes in v7:
time: 53.1 us; the launch traced here: 52.8 us
  blocking collectives  22.4 us (42%)
  Pallas kernels  21.1 us (40%)
  starting transfers between devices  6.23 us (12%)
  waiting for transfers between devices  2.38 us (4%)
  between operations  0.68 us (1%)
    all_to_all x1, blocking collectives, per_device(): swapped = lax.all_to_all(partial, AXES, 0, 0, tiled=True)  13.2 us
    pallas_call x1, Pallas kernels, per_device(): pl.pallas_call(functools.partial(layer_kernel, tile=tile, chunk=chunk), o...  12.2 us
    all_to_all x1, blocking collectives, per_device(): sums = lax.all_to_all(spread, AXES, 0, 0, tiled=True)  9.19 us
    ppermute x2, starting transfers between devices, shifted(): return lax.ppermute(x, AXES, pairs)  6.23 us
    pallas_call x1, Pallas kernels, per_device(): pl.pallas_call(functools.partial(early_kernel, tile=tile, chunk=chunk, fa...  4.07 us
    pallas_call x1, Pallas kernels, per_device(): pl.pallas_call(functools.partial(response_kernel, tile=4096), out_shape=(...  2.91 us
    ppermute x2, waiting for transfers between devices, shifted(): return lax.ppermute(x, AXES, pairs)  2.38 us
    pallas_call x1, Pallas kernels, per_device(): pl.pallas_call(pack_kernel, out_shape=(edge, edge, pltpu.VMEM(wave.shape,...  1.88 us
  transfers between devices with their start and end apart: 2, of which 1 were waited for; matrix products, arithmetic and copies ran while one was open for 0% of the time, Pallas kernels for 8%

profile of v7, /device:TPU:0, one launch (start us, length us, event | category | flops | bytes accessed | tf_op | source)
XLA Modules:
  0.0 52.8 jit_solution(14002471112671473017)
XLA Ops:
  0.6 1.9 %shard_map.103 = (bf16[128,384]{1,0:T(8,128)(2,1)S(1)}, bf16[128,384]{1,0:T(8,128)(2,1)S(1)}, f32[3,16384]{1,0:T(4,128)S(1)}, f32[3,256]{1,0:T(4,128)S(1)}) custom-call(bf16[256,256]{1,0:T(8,128)(2,1)} %feat_ref.1, f32[3,256]{1,0:T(4,128)} %pos_ref.1, s32[64,256]{1,0:T(8,128)} %bitcast.4, s32[1,256]{1,0:T(1,128)} %bitcast.5, f32[3,16384]{1,0:T(4,128)} %wave_ref.1), custom_call_target="tpu_custom_call" | custom-call | tf_op jit(solution)/shard_map/pallas_call | solution.py:368
  2.5 4.9 %collective-permute-start = (bf16[128,384]{1,0:T(8,128)(2,1)S(1)}, bf16[128,384]{1,0:T(8,128)(2,1)S(1)}, u32[]{:S(2)}, u32[]{:S(2)}) collective-permute-start(bf16[128,384]{1,0:T(8,128)(2,1)S(1)} %get-tuple-element.20.last_ref), channel_id=1, source_target_pairs={{0,1},{1,2},{2,3},{3,4},{4,5},{5,6},{6,7},{7,8},{8,9},{9,10},{10,1... | collective-permute-start | bytes 294920 | tf_op jit(solution)/shard_map/ppermute | solution.py:350
  7.5 1.3 %collective-permute-start.1 = (bf16[128,384]{1,0:T(8,128)(2,1)S(1)}, bf16[128,384]{1,0:T(8,128)(2,1)S(1)}, u32[]{:S(2)}, u32[]{:S(2)}) collective-permute-start(bf16[128,384]{1,0:T(8,128)(2,1)S(1)} %get-tuple-element.21.first_ref), channel_id=1, source_target_pairs={{1,0},{2,1},{3,2},{4,3},{5,4},{6,5},{7,6},{8,7},{9,8},{10,9},{11,1... | collective-permute-start | bytes 294920 | tf_op jit(solution)/shard_map/ppermute | solution.py:350
  8.8 4.1 %shard_map.104 = (bf16[4096,256]{1,0:T(8,128)(2,1)S(1)}, bf16[4096,256]{1,0:T(8,128)(2,1)S(1)}, f32[8,16384]{1,0:T(8,128)S(1)}, f32[256,128]{1,0:T(8,128)S(1)}, ...) custom-call(f32[3,256]{1,0:T(4,128)S(1)} %get-tuple-element.22.pos_ref, ...), custom_call_target="tpu_custom_call" | custom-call | flops 41943040 | bytes 4194304 | tf_op jit(solution)/shard_map/pallas_call | solution.py:384
  12.8 0.0 collective-permute-done.before_ref
  12.9 2.4 %collective-permute-done.1.after_ref = bf16[128,384]{1,0:T(8,128)(2,1)S(1)} collective-permute-done((bf16[128,384]{1,0:T(8,128)(2,1)S(1)}, bf16[128,384]{1,0:T(8,128)(2,1)S(1)}, u32[]{:S(2)}, u32[]{:S(2)}) %collective-permute-start.1) | collective-permute-done | bytes 98336 | tf_op jit(solution)/shard_map/ppermute | solution.py:350
  15.2 12.2 %shard_map.105 = (bf16[256,256]{1,0:T(8,128)(2,1)}, bf16[32,2,512]{2,1,0:T(2,128)(2,1)S(1)}, bf16[12288,256]{1,0:T(8,128)(2,1)S(1)}, bf16[12288,256]{1,0:T(8,128)(2,1)S(1)}) custom-call(bf16[128,384]{1,0:T(8,128)(2,1)S(1)} %collective-permute-done.before_ref, bf16[128,384]{1,0:T(8,128)(2,1)S(1)} %get-tuple-element.21.first_ref, ...), custom_call_target="tpu_custom_call" | custom-call | tf_op jit(solution)/shard_map/pallas_call | solution.py:405
  27.4 13.2 %all_to_all.10.parts_ref = bf16[32,2,512]{2,1,0:T(2,128)(2,1)S(1)} all-to-all(bf16[32,2,512]{2,1,0:T(2,128)(2,1)S(1)} %get-tuple-element.31), channel_id=1, replica_groups=mesh['brick'=8,'kvec'=4] {'brick','kvec'}, dimensions={0} | all-to-all | bytes 131072 | tf_op jit(solution)/shard_map/all_to_all | solution.py:427
  40.6 0.1 shard_map.106
  40.7 9.2 %all_to_all.11.sums_ref = bf16[32,2,512]{2,1,0:T(2,128)(2,1)S(1)} all-to-all(bf16[32,2,512]{2,1,0:T(2,128)(2,1)S(1)} %shard_map.106), channel_id=1, replica_groups=mesh['brick'=8,'kvec'=4] {'brick','kvec'}, dimensions={0} | all-to-all | bytes 131072 | tf_op jit(solution)/shard_map/all_to_all | solution.py:435
  49.9 2.9 %shard_map.107 = (f32[1,256]{1,0:T(1,128)}, f32[3,256]{1,0:T(4,128)}) custom-call(bf16[32,2,512]{2,1,0:T(2,128)(2,1)S(1)} %all_to_all.11.sums_ref, f32[8,16384]{1,0:T(8,128)S(1)} %get-tuple-element.32.coef_ref, bf16[4096,256]{1,0:T(8,128)(2,1)S(1)} %get-tuple-element.28.cos_head_ref, bf16[4096,256]{1,0:T(8,128)(2,1)S(1)} %get-tuple-element.29.sin_head_ref, ...), custom_call_target="tpu_custom_call" | custom-call | tf_op jit(solution)/shard_map/pallas_call | solution.py:441
Async XLA Ops:
  2.5 10.3 %collective-permute-start = (bf16[128,384]{1,0:T(8,128)(2,1)S(1)}, bf16[128,384]{1,0:T(8,128)(2,1)S(1)}, u32[]{:S(2)}, u32[]{:S(2)}) collective-permute-start(bf16[128,384]{1,0:T(8,128)(2,1)S(1)} %get-tuple-element.20.last_ref), channel_id=1, source_target_pairs={{0,1},{1,2},{2,3},{3,4},{4,5},{5,6},{6,7},{7,8},{8,9},{9,10},{10,1... | collective-permute-start | bytes 294920 | tf_op jit(solution)/shard_map/ppermute | solution.py:350
  7.5 7.8 %collective-permute-start.1 = (bf16[128,384]{1,0:T(8,128)(2,1)S(1)}, bf16[128,384]{1,0:T(8,128)(2,1)S(1)}, u32[]{:S(2)}, u32[]{:S(2)}) collective-permute-start(bf16[128,384]{1,0:T(8,128)(2,1)S(1)} %get-tuple-element.21.first_ref), channel_id=1, source_target_pairs={{1,0},{2,1},{3,2},{4,3},{5,4},{6,5},{7,6},{8,7},{9,8},{10,9},{11,1... | collective-permute-start | bytes 294920 | tf_op jit(solution)/shard_map/ppermute | solution.py:350

commit v8 on v7

--- a/solution.py
+++ b/solution.py
@@ -111,11 +111,14 @@
 def histogram(delta):
     place = jnp.where(delta > 0, delta + 63.0, delta + 64.0)
     place = jnp.where(delta == 0, -1.0, place)
-    deep = lax.broadcasted_iota(jnp.int32, (LANES, LANES), 0).astype(F32)
-    hist = jnp.zeros((LANES, LANES), F32)
+    deep = lax.broadcasted_iota(jnp.int32, (LANES, LANES), 0).astype(F32).astype(BF16)
+    one = jnp.ones((LANES, LANES), BF16)
+    zero = jnp.zeros((LANES, LANES), BF16)
+    hist = zero
     for slot in range(64):
-        hist = hist + jnp.where(deep == place[slot : slot + 1, :], 1.0, 0.0)
-    return hist.T
+        row = jnp.broadcast_to(place[slot : slot + 1, :], (16, LANES)).astype(BF16)
+        hist = hist + jnp.where(deep == jnp.concatenate([row] * 8, axis=0), one, zero)
+    return hist.astype(F32).T
 
 
 def early_kernel(
@@ -262,38 +265,34 @@
     def turn(step, out_ref):
         phase(wave_ref[:, place(head + step, tile)], left_ref, out_ref)
 
-    def added(table):
-        part = lax.dot_general(charge_ref[...], table, dims, preferred_element_type=F32)
-        return part[0:1] + part[1:2] + part[2:3]
-
-    def keep(index, pair):
-        for q in range(per):
-            sums_ref[index * per + q] = pair[:, q * share : (q + 1) * share].astype(BF16)
-
-    def joined(parts):
-        return jnp.concatenate(
-            [jnp.concatenate(list(row), axis=1) for row in zip(*parts)], axis=0
-        )
+    def added(step, cos_tile, sin_tile, odd):
+        rows = []
+        for table in (cos_tile, sin_tile):
+            part = lax.dot_general(charge_ref[...], table, dims, preferred_element_type=F32)
+            rows.append(part[0:1] + part[1:2] + part[2:3])
+        index = (step - odd) // 2 * per + odd * (per - 1)
+        lanes = odd * (2 - per) * tile
+        sums_ref[index, :, lanes : lanes + tile] = jnp.concatenate(rows, axis=0)
 
     turn(0, even_ref)
 
     @pl.loop(0, head // 2)
     def _(block):
-        parts = []
         for n in range(2):
-            rows = place(2 * block + n, tile)
-            parts.append((added(cos_head_ref[rows, :]), added(sin_head_ref[rows, :])))
-        keep(block, joined(parts))
+            step = 2 * block + n
+            rows = place(step, tile)
+            added(step, cos_head_ref[rows, :], sin_head_ref[rows, :], n)
         for pair in range(3):
             step = 6 * block + 2 * pair
             turn(step + 1, odd_ref)
+            added(head + step - 1, odd_tile_ref[0], odd_tile_ref[1], 1)
             evaluate(
                 even_ref,
                 [into_table(cos_ref, sin_ref, step, tile, chunk), into_tile(even_tile_ref, chunk)],
                 chunk,
             )
             turn(jnp.minimum(step + 2, late - 1), even_ref)
-            parts = [(added(even_tile_ref[0]), added(even_tile_ref[1]))]
+            added(head + step, even_tile_ref[0], even_tile_ref[1], 0)
             evaluate(
                 odd_ref,
                 [
@@ -302,8 +301,8 @@
                 ],
                 chunk,
             )
-            parts.append((added(odd_tile_ref[0]), added(odd_tile_ref[1])))
-            keep(head // 2 + 3 * block + pair, joined(parts))
+
+    added(head + late - 1, odd_tile_ref[0], odd_tile_ref[1], 1)
 
 
 def sum_kernel(parts_ref, out_ref):
@@ -406,7 +405,7 @@
         functools.partial(layer_kernel, tile=tile, chunk=chunk),
         out_shape=(
             jax.ShapeDtypeStruct((own, channels), BF16),
-            jax.ShapeDtypeStruct((devices, 2, share), BF16),
+            jax.ShapeDtypeStruct((devices, 2, share), F32),
             table,
             table,
         ),
@@ -424,7 +423,7 @@
         compiler_params=grant,
     )(before, first, last, after, w_first, w_second, w_read, hist, held, waves, cos_head, sin_head)
 
-    swapped = lax.all_to_all(partial, AXES, 0, 0, tiled=True)
+    swapped = lax.all_to_all(partial.astype(BF16), AXES, 0, 0, tiled=True)
     spread = pl.pallas_call(
         sum_kernel,
         out_shape=jax.ShapeDtypeStruct((devices, 2, share), BF16),

time: 53.1 us -> 52.2 us (0.983)
  Pallas kernels: 21.1 us -> 19.8 us
    pallas_call x1, Pallas kernels: 12.2 us -> 11.3 us  [per_device(): pl.pallas_call(functools.partial(layer_kernel, tile=tile, chunk=chunk), o...]
  transfers between devices with their start and end apart: 2 -> 2, of which waited for: 1 -> 1; matrix products, arithmetic and copies ran while one was open for 0% -> 0% of each run, Pallas kernels for 8% -> 7%
where the time goes in v8:
time: 52.2 us; the launch traced here: 52 us
  blocking collectives  22.4 us (43%)
  Pallas kernels  19.8 us (38%)
  starting transfers between devices  6.23 us (12%)
  waiting for transfers between devices  2.75 us (5%)
  between operations  0.68 us (1%)
    all_to_all x1, blocking collectives, per_device(): swapped = lax.all_to_all(partial.astype(BF16), AXES, 0, 0, tiled=True)  13.3 us
    pallas_call x1, Pallas kernels, per_device(): pl.pallas_call(functools.partial(layer_kernel, tile=tile, chunk=chunk), o...  11.3 us
    all_to_all x1, blocking collectives, per_device(): sums = lax.all_to_all(spread, AXES, 0, 0, tiled=True)  9.19 us
    ppermute x2, starting transfers between devices, shifted(): return lax.ppermute(x, AXES, pairs)  6.23 us
    pallas_call x1, Pallas kernels, per_device(): pl.pallas_call(functools.partial(early_kernel, tile=tile, chunk=chunk, fa...  3.7 us
    pallas_call x1, Pallas kernels, per_device(): pl.pallas_call(functools.partial(response_kernel, tile=4096), out_shape=(...  2.91 us
    ppermute x2, waiting for transfers between devices, shifted(): return lax.ppermute(x, AXES, pairs)  2.75 us
    pallas_call x1, Pallas kernels, per_device(): pl.pallas_call(pack_kernel, out_shape=(edge, edge, pltpu.VMEM(wave.shape,...  1.88 us
  transfers between devices with their start and end apart: 2, of which 1 were waited for; matrix products, arithmetic and copies ran while one was open for 0% of the time, Pallas kernels for 7%

profile of v8, /device:TPU:0, one launch (start us, length us, event | category | flops | bytes accessed | tf_op | source)
XLA Modules:
  0.0 52.0 jit_solution(2961865539516328755)
XLA Ops:
  0.6 1.9 %shard_map.103 = (bf16[128,384]{1,0:T(8,128)(2,1)S(1)}, bf16[128,384]{1,0:T(8,128)(2,1)S(1)}, f32[3,16384]{1,0:T(4,128)S(1)}, f32[3,256]{1,0:T(4,128)S(1)}) custom-call(bf16[256,256]{1,0:T(8,128)(2,1)} %feat_ref.1, f32[3,256]{1,0:T(4,128)} %pos_ref.1, s32[64,256]{1,0:T(8,128)} %bitcast.4, s32[1,256]{1,0:T(1,128)} %bitcast.5, f32[3,16384]{1,0:T(4,128)} %wave_ref.1), custom_call_target="tpu_custom_call" | custom-call | tf_op jit(solution)/shard_map/pallas_call | solution.py:367
  2.5 4.9 %collective-permute-start = (bf16[128,384]{1,0:T(8,128)(2,1)S(1)}, bf16[128,384]{1,0:T(8,128)(2,1)S(1)}, u32[]{:S(2)}, u32[]{:S(2)}) collective-permute-start(bf16[128,384]{1,0:T(8,128)(2,1)S(1)} %get-tuple-element.20.last_ref), channel_id=1, source_target_pairs={{0,1},{1,2},{2,3},{3,4},{4,5},{5,6},{6,7},{7,8},{8,9},{9,10},{10,1... | collective-permute-start | bytes 294920 | tf_op jit(solution)/shard_map/ppermute | solution.py:349
  7.5 1.3 %collective-permute-start.1 = (bf16[128,384]{1,0:T(8,128)(2,1)S(1)}, bf16[128,384]{1,0:T(8,128)(2,1)S(1)}, u32[]{:S(2)}, u32[]{:S(2)}) collective-permute-start(bf16[128,384]{1,0:T(8,128)(2,1)S(1)} %get-tuple-element.21.first_ref), channel_id=1, source_target_pairs={{1,0},{2,1},{3,2},{4,3},{5,4},{6,5},{7,6},{8,7},{9,8},{10,9},{11,1... | collective-permute-start | bytes 294920 | tf_op jit(solution)/shard_map/ppermute | solution.py:349
  8.8 3.7 %shard_map.104 = (bf16[4096,256]{1,0:T(8,128)(2,1)S(1)}, bf16[4096,256]{1,0:T(8,128)(2,1)S(1)}, f32[8,16384]{1,0:T(8,128)S(1)}, f32[256,128]{1,0:T(8,128)S(1)}, ...) custom-call(f32[3,256]{1,0:T(4,128)S(1)} %get-tuple-element.22.pos_ref, ...), custom_call_target="tpu_custom_call" | custom-call | flops 41943040 | bytes 4194304 | tf_op jit(solution)/shard_map/pallas_call | solution.py:383
  12.5 0.0 collective-permute-done.before_ref
  12.5 2.7 %collective-permute-done.1.after_ref = bf16[128,384]{1,0:T(8,128)(2,1)S(1)} collective-permute-done((bf16[128,384]{1,0:T(8,128)(2,1)S(1)}, bf16[128,384]{1,0:T(8,128)(2,1)S(1)}, u32[]{:S(2)}, u32[]{:S(2)}) %collective-permute-start.1) | collective-permute-done | bytes 98336 | tf_op jit(solution)/shard_map/ppermute | solution.py:349
  15.2 11.3 %shard_map.105 = (bf16[256,256]{1,0:T(8,128)(2,1)}, f32[32,2,512]{2,1,0:T(2,128)S(1)}, bf16[12288,256]{1,0:T(8,128)(2,1)S(1)}, bf16[12288,256]{1,0:T(8,128)(2,1)S(1)}) custom-call(bf16[128,384]{1,0:T(8,128)(2,1)S(1)} %collective-permute-done.before_ref, bf16[128,384]{1,0:T(8,128)(2,1)S(1)} %get-tuple-element.21.first_ref, ...), custom_call_target="tpu_custom_call" | custom-call | tf_op jit(solution)/shard_map/pallas_call | solution.py:404
  26.6 13.3 %all_to_all.10.parts_ref = bf16[32,2,512]{2,1,0:T(2,128)(2,1)S(1)} all-to-all(bf16[32,2,512]{2,1,0:T(2,128)(2,1)S(1)} %convert_element_type.3), channel_id=1, replica_groups=mesh['brick'=8,'kvec'=4] {'brick','kvec'}, dimensions={0} | all-to-all | bytes 131072 | tf_op jit(solution)/shard_map/all_to_all | solution.py:426
  39.8 0.1 shard_map.106
  39.9 9.2 %all_to_all.11.sums_ref = bf16[32,2,512]{2,1,0:T(2,128)(2,1)S(1)} all-to-all(bf16[32,2,512]{2,1,0:T(2,128)(2,1)S(1)} %shard_map.106), channel_id=1, replica_groups=mesh['brick'=8,'kvec'=4] {'brick','kvec'}, dimensions={0} | all-to-all | bytes 131072 | tf_op jit(solution)/shard_map/all_to_all | solution.py:434
  49.1 2.9 %shard_map.107 = (f32[1,256]{1,0:T(1,128)}, f32[3,256]{1,0:T(4,128)}) custom-call(bf16[32,2,512]{2,1,0:T(2,128)(2,1)S(1)} %all_to_all.11.sums_ref, f32[8,16384]{1,0:T(8,128)S(1)} %get-tuple-element.32.coef_ref, bf16[4096,256]{1,0:T(8,128)(2,1)S(1)} %get-tuple-element.28.cos_head_ref, bf16[4096,256]{1,0:T(8,128)(2,1)S(1)} %get-tuple-element.29.sin_head_ref, ...), custom_call_target="tpu_custom_call" | custom-call | tf_op jit(solution)/shard_map/pallas_call | solution.py:440
  (1 shorter events, 0.0 us)
Async XLA Ops:
  2.5 10.0 %collective-permute-start = (bf16[128,384]{1,0:T(8,128)(2,1)S(1)}, bf16[128,384]{1,0:T(8,128)(2,1)S(1)}, u32[]{:S(2)}, u32[]{:S(2)}) collective-permute-start(bf16[128,384]{1,0:T(8,128)(2,1)S(1)} %get-tuple-element.20.last_ref), channel_id=1, source_target_pairs={{0,1},{1,2},{2,3},{3,4},{4,5},{5,6},{6,7},{7,8},{8,9},{9,10},{10,1... | collective-permute-start | bytes 294920 | tf_op jit(solution)/shard_map/ppermute | solution.py:349
  7.5 7.8 %collective-permute-start.1 = (bf16[128,384]{1,0:T(8,128)(2,1)S(1)}, bf16[128,384]{1,0:T(8,128)(2,1)S(1)}, u32[]{:S(2)}, u32[]{:S(2)}) collective-permute-start(bf16[128,384]{1,0:T(8,128)(2,1)S(1)} %get-tuple-element.21.first_ref), channel_id=1, source_target_pairs={{1,0},{2,1},{3,2},{4,3},{5,4},{6,5},{7,6},{8,7},{9,8},{10,9},{11,1... | collective-permute-start | bytes 294920 | tf_op jit(solution)/shard_map/ppermute | solution.py:349

commit v9 on v8

--- a/solution.py
+++ b/solution.py
@@ -162,8 +162,7 @@
     @pl.loop(0, head // 4)
     def _(block):
         base = 4 * block
-        scale(4 * base)
-        scale(4 * base + group)
+        scale(2 * base)
         for step in range(0, 4, 2):
             turn(base + step + 1, odd_ref)
             evaluate(even_ref, [into_table(cos_ref, sin_ref, base + step, tile, chunk)], chunk)
@@ -276,14 +275,13 @@
 
     turn(0, even_ref)
 
-    @pl.loop(0, head // 2)
+    @pl.loop(0, late // 4)
     def _(block):
-        for n in range(2):
-            step = 2 * block + n
-            rows = place(step, tile)
-            added(step, cos_head_ref[rows, :], sin_head_ref[rows, :], n)
-        for pair in range(3):
-            step = 6 * block + 2 * pair
+        for pair in range(2):
+            step = 4 * block + 2 * pair
+            for n in range(2):
+                rows = place(step + n, tile)
+                added(step + n, cos_head_ref[rows, :], sin_head_ref[rows, :], n)
             turn(step + 1, odd_ref)
             added(head + step - 1, odd_tile_ref[0], odd_tile_ref[1], 1)
             evaluate(
@@ -374,7 +372,7 @@
     before = shifted(last, 1)
     after = shifted(first, -1)
 
-    early = total // 4
+    early = total // 2
     tile, chunk = 256, 32
     kept = pltpu.VMEM(w_in.shape, BF16)
     table = pltpu.VMEM((early, own), BF16)

time: 52.2 us -> 51 us (0.977)
  waiting for transfers between devices: 2.75 us -> 0.01 us
  blocking collectives: 22.4 us -> 23.4 us
  Pallas kernels: 19.8 us -> 20.4 us
    pallas_call x1, Pallas kernels: 3.7 us -> 6.6 us  [per_device(): pl.pallas_call(functools.partial(early_kernel, tile=tile, chunk=chunk, fa...]
    ppermute x2, waiting for transfers between devices: 2.75 us -> 0.01 us  [shifted(): return lax.ppermute(x, AXES, pairs)]
    pallas_call x1, Pallas kernels: 11.3 us -> 8.94 us  [per_device(): pl.pallas_call(functools.partial(layer_kernel, tile=tile, chunk=chunk), o...]
    all_to_all x1, blocking collectives: 13.3 us -> 14.2 us  [per_device(): swapped = lax.all_to_all(partial.astype(BF16), AXES, 0, 0, tiled=True)]
  transfers between devices with their start and end apart: 2 -> 2, of which waited for: 1 -> 0; matrix products, arithmetic and copies ran while one was open for 0% -> 0% of each run, Pallas kernels for 7% -> 13%
where the time goes in v9:
time: 51 us; the launch traced here: 50.8 us
  blocking collectives  23.4 us (46%)
  Pallas kernels  20.4 us (40%)
  starting transfers between devices  6.23 us (12%)
  between operations  0.69 us (1%)
    all_to_all x1, blocking collectives, per_device(): swapped = lax.all_to_all(partial.astype(BF16), AXES, 0, 0, tiled=True)  14.2 us
    all_to_all x1, blocking collectives, per_device(): sums = lax.all_to_all(spread, AXES, 0, 0, tiled=True)  9.19 us
    pallas_call x1, Pallas kernels, per_device(): pl.pallas_call(functools.partial(layer_kernel, tile=tile, chunk=chunk), o...  8.94 us
    pallas_call x1, Pallas kernels, per_device(): pl.pallas_call(functools.partial(early_kernel, tile=tile, chunk=chunk, fa...  6.6 us
    ppermute x2, starting transfers between devices, shifted(): return lax.ppermute(x, AXES, pairs)  6.23 us
    pallas_call x1, Pallas kernels, per_device(): pl.pallas_call(functools.partial(response_kernel, tile=4096), out_shape=(...  2.92 us
    pallas_call x1, Pallas kernels, per_device(): pl.pallas_call(pack_kernel, out_shape=(edge, edge, pltpu.VMEM(wave.shape,...  1.88 us
  transfers between devices with their start and end apart: 2, of which 0 were waited for; matrix products, arithmetic and copies ran while one was open for 0% of the time, Pallas kernels for 13%

profile of v9, /device:TPU:0, one launch (start us, length us, event | category | flops | bytes accessed | tf_op | source)
XLA Modules:
  0.0 50.8 jit_solution(5196714782784917583)
XLA Ops:
  0.6 1.9 %shard_map.103 = (bf16[128,384]{1,0:T(8,128)(2,1)S(1)}, bf16[128,384]{1,0:T(8,128)(2,1)S(1)}, f32[3,16384]{1,0:T(4,128)S(1)}, f32[3,256]{1,0:T(4,128)S(1)}) custom-call(bf16[256,256]{1,0:T(8,128)(2,1)} %feat_ref.1, f32[3,256]{1,0:T(4,128)} %pos_ref.1, s32[64,256]{1,0:T(8,128)} %bitcast.4, s32[1,256]{1,0:T(1,128)} %bitcast.5, f32[3,16384]{1,0:T(4,128)} %wave_ref.1), custom_call_target="tpu_custom_call" | custom-call | tf_op jit(solution)/shard_map/pallas_call | solution.py:365
  2.5 4.9 %collective-permute-start = (bf16[128,384]{1,0:T(8,128)(2,1)S(1)}, bf16[128,384]{1,0:T(8,128)(2,1)S(1)}, u32[]{:S(2)}, u32[]{:S(2)}) collective-permute-start(bf16[128,384]{1,0:T(8,128)(2,1)S(1)} %get-tuple-element.20.last_ref), channel_id=1, source_target_pairs={{0,1},{1,2},{2,3},{3,4},{4,5},{5,6},{6,7},{7,8},{8,9},{9,10},{10,1... | collective-permute-start | bytes 294920 | tf_op jit(solution)/shard_map/ppermute | solution.py:347
  7.5 1.3 %collective-permute-start.1 = (bf16[128,384]{1,0:T(8,128)(2,1)S(1)}, bf16[128,384]{1,0:T(8,128)(2,1)S(1)}, u32[]{:S(2)}, u32[]{:S(2)}) collective-permute-start(bf16[128,384]{1,0:T(8,128)(2,1)S(1)} %get-tuple-element.21.first_ref), channel_id=1, source_target_pairs={{1,0},{2,1},{3,2},{4,3},{5,4},{6,5},{7,6},{8,7},{9,8},{10,9},{11,1... | collective-permute-start | bytes 294920 | tf_op jit(solution)/shard_map/ppermute | solution.py:347
  8.8 6.6 %shard_map.104 = (bf16[8192,256]{1,0:T(8,128)(2,1)S(1)}, bf16[8192,256]{1,0:T(8,128)(2,1)S(1)}, f32[8,16384]{1,0:T(8,128)S(1)}, f32[256,128]{1,0:T(8,128)S(1)}, ...) custom-call(f32[3,256]{1,0:T(4,128)S(1)} %get-tuple-element.22.pos_ref, ...), custom_call_target="tpu_custom_call" | custom-call | flops 83886080 | bytes 8388608 | tf_op jit(solution)/shard_map/pallas_call | solution.py:381
  15.4 0.0 collective-permute-done.before_ref
  15.4 0.0 collective-permute-done.1.after_ref
  15.4 8.9 %shard_map.105 = (bf16[256,256]{1,0:T(8,128)(2,1)}, f32[32,2,512]{2,1,0:T(2,128)S(1)}, bf16[8192,256]{1,0:T(8,128)(2,1)S(1)}, bf16[8192,256]{1,0:T(8,128)(2,1)S(1)}) custom-call(bf16[128,384]{1,0:T(8,128)(2,1)S(1)} %collective-permute-done.before_ref, bf16[128,384]{1,0:T(8,128)(2,1)S(1)} %get-tuple-element.21.first_ref, ...), custom_call_target="tpu_custom_call" | custom-call | tf_op jit(solution)/shard_map/pallas_call | solution.py:402
  24.4 14.2 %all_to_all.10.parts_ref = bf16[32,2,512]{2,1,0:T(2,128)(2,1)S(1)} all-to-all(bf16[32,2,512]{2,1,0:T(2,128)(2,1)S(1)} %convert_element_type.3), channel_id=1, replica_groups=mesh['brick'=8,'kvec'=4] {'brick','kvec'}, dimensions={0} | all-to-all | bytes 131072 | tf_op jit(solution)/shard_map/all_to_all | solution.py:424
  38.6 0.1 shard_map.106
  38.7 9.2 %all_to_all.11.sums_ref = bf16[32,2,512]{2,1,0:T(2,128)(2,1)S(1)} all-to-all(bf16[32,2,512]{2,1,0:T(2,128)(2,1)S(1)} %shard_map.106), channel_id=1, replica_groups=mesh['brick'=8,'kvec'=4] {'brick','kvec'}, dimensions={0} | all-to-all | bytes 131072 | tf_op jit(solution)/shard_map/all_to_all | solution.py:432
  47.9 2.9 %shard_map.107 = (f32[1,256]{1,0:T(1,128)}, f32[3,256]{1,0:T(4,128)}) custom-call(bf16[32,2,512]{2,1,0:T(2,128)(2,1)S(1)} %all_to_all.11.sums_ref, f32[8,16384]{1,0:T(8,128)S(1)} %get-tuple-element.32.coef_ref, bf16[8192,256]{1,0:T(8,128)(2,1)S(1)} %get-tuple-element.28.cos_head_ref, bf16[8192,256]{1,0:T(8,128)(2,1)S(1)} %get-tuple-element.29.sin_head_ref, ...), custom_call_target="tpu_custom_call" | custom-call | tf_op jit(solution)/shard_map/pallas_call | solution.py:438
  (1 shorter events, 0.0 us)
Async XLA Ops:
  2.5 12.9 %collective-permute-start = (bf16[128,384]{1,0:T(8,128)(2,1)S(1)}, bf16[128,384]{1,0:T(8,128)(2,1)S(1)}, u32[]{:S(2)}, u32[]{:S(2)}) collective-permute-start(bf16[128,384]{1,0:T(8,128)(2,1)S(1)} %get-tuple-element.20.last_ref), channel_id=1, source_target_pairs={{0,1},{1,2},{2,3},{3,4},{4,5},{5,6},{6,7},{7,8},{8,9},{9,10},{10,1... | collective-permute-start | bytes 294920 | tf_op jit(solution)/shard_map/ppermute | solution.py:347
  7.5 7.9 %collective-permute-start.1 = (bf16[128,384]{1,0:T(8,128)(2,1)S(1)}, bf16[128,384]{1,0:T(8,128)(2,1)S(1)}, u32[]{:S(2)}, u32[]{:S(2)}) collective-permute-start(bf16[128,384]{1,0:T(8,128)(2,1)S(1)} %get-tuple-element.21.first_ref), channel_id=1, source_target_pairs={{1,0},{2,1},{3,2},{4,3},{5,4},{6,5},{7,6},{8,7},{9,8},{10,9},{11,1... | collective-permute-start | bytes 294920 | tf_op jit(solution)/shard_map/ppermute | solution.py:347

commit v10 on v9

--- a/solution.py
+++ b/solution.py
@@ -101,9 +101,11 @@
 
 
 def into_tile(tile_ref, chunk):
+    tile = tile_ref.shape[0] // 2
+
     def store(start, cosine, sine):
-        tile_ref[0, start : start + chunk, :] = cosine
-        tile_ref[1, start : start + chunk, :] = sine
+        tile_ref[start : start + chunk, :] = cosine
+        tile_ref[tile + start : tile + start + chunk, :] = sine
 
     return store
 
@@ -140,17 +142,18 @@
         hist_ref[n * LANES : (n + 1) * LANES, :] = histogram(ref[:64, channels:].astype(F32))
     head = cos_ref.shape[0] // tile
     group = 8
+    width = 4 * tile // group
 
     def scale(step):
-        waves = [wave_ref[:, place(step + n, tile)] for n in range(group)]
-        ksq = jnp.zeros((group, tile), F32)
+        waves = [wave_ref[:, place(4 * step + n, width)] for n in range(group)]
+        ksq = jnp.zeros((group, width), F32)
         for c in range(3):
             part = jnp.concatenate([w[c : c + 1] for w in waves], axis=0)
             ksq = ksq + part * part
         coef = factor * jnp.exp(-0.1 * ksq) / ksq
-        one = jnp.ones((1, tile), F32)
+        one = jnp.ones((1, width), F32)
         for n, w in enumerate(waves):
-            coef_ref[:, place(step + n, tile)] = coef[n : n + 1] * jnp.concatenate(
+            coef_ref[:, place(4 * step + n, width)] = coef[n : n + 1] * jnp.concatenate(
                 [one, w, one, w], axis=0
             )
 
@@ -159,15 +162,14 @@
 
     turn(0, even_ref)
 
-    @pl.loop(0, head // 4)
+    @pl.loop(0, head // 2)
     def _(block):
-        base = 4 * block
-        scale(2 * base)
-        for step in range(0, 4, 2):
-            turn(base + step + 1, odd_ref)
-            evaluate(even_ref, [into_table(cos_ref, sin_ref, base + step, tile, chunk)], chunk)
-            turn(jnp.minimum(base + step + 2, head - 1), even_ref)
-            evaluate(odd_ref, [into_table(cos_ref, sin_ref, base + step + 1, tile, chunk)], chunk)
+        step = 2 * block
+        scale(step)
+        turn(step + 1, odd_ref)
+        evaluate(even_ref, [into_table(cos_ref, sin_ref, step, tile, chunk)], chunk)
+        turn(jnp.minimum(step + 2, head - 1), even_ref)
+        evaluate(odd_ref, [into_table(cos_ref, sin_ref, step + 1, tile, chunk)], chunk)
 
     for copy in copies:
         copy.wait()
@@ -258,49 +260,47 @@
     head = cos_head_ref.shape[0] // tile
     late = cos_ref.shape[0] // tile
     share = sums_ref.shape[2]
-    per = 2 * tile // share
+    per = tile // share
     dims = (((1,), (1,)), ((), ()))
 
     def turn(step, out_ref):
         phase(wave_ref[:, place(head + step, tile)], left_ref, out_ref)
 
-    def added(step, cos_tile, sin_tile, odd):
-        rows = []
-        for table in (cos_tile, sin_tile):
-            part = lax.dot_general(charge_ref[...], table, dims, preferred_element_type=F32)
-            rows.append(part[0:1] + part[1:2] + part[2:3])
-        index = (step - odd) // 2 * per + odd * (per - 1)
-        lanes = odd * (2 - per) * tile
-        sums_ref[index, :, lanes : lanes + tile] = jnp.concatenate(rows, axis=0)
+    def product(table):
+        part = lax.dot_general(charge_ref[...], table, dims, preferred_element_type=F32)
+        return part[0:1] + part[1:2] + part[2:3]
+
+    def keep(step, cosine, sine):
+        both = jnp.concatenate([cosine, sine], axis=0)
+        for q in range(per):
+            sums_ref[step * per + q] = both[:, q * share : (q + 1) * share]
+
+    def added(step, tile_ref):
+        both = product(tile_ref[...])
+        keep(step, both[:, :tile], both[:, tile:])
 
     turn(0, even_ref)
 
-    @pl.loop(0, late // 4)
+    @pl.loop(0, late // 2)
     def _(block):
-        for pair in range(2):
-            step = 4 * block + 2 * pair
-            for n in range(2):
-                rows = place(step + n, tile)
-                added(step + n, cos_head_ref[rows, :], sin_head_ref[rows, :], n)
-            turn(step + 1, odd_ref)
-            added(head + step - 1, odd_tile_ref[0], odd_tile_ref[1], 1)
+        step = 2 * block
+        for n, (t_ref, next_ref, tile_ref, last_tile_ref) in enumerate(
+            (
+                (even_ref, odd_ref, even_tile_ref, odd_tile_ref),
+                (odd_ref, even_ref, odd_tile_ref, even_tile_ref),
+            )
+        ):
+            rows = place(step + n, tile)
+            turn(jnp.minimum(step + n + 1, late - 1), next_ref)
+            added(head + step + n - 1, last_tile_ref)
+            keep(step + n, product(cos_head_ref[rows, :]), product(sin_head_ref[rows, :]))
             evaluate(
-                even_ref,
-                [into_table(cos_ref, sin_ref, step, tile, chunk), into_tile(even_tile_ref, chunk)],
+                t_ref,
+                [into_table(cos_ref, sin_ref, step + n, tile, chunk), into_tile(tile_ref, chunk)],
                 chunk,
             )
-            turn(jnp.minimum(step + 2, late - 1), even_ref)
-            added(head + step, even_tile_ref[0], even_tile_ref[1], 0)
-            evaluate(
-                odd_ref,
-                [
-                    into_table(cos_ref, sin_ref, step + 1, tile, chunk),
-                    into_tile(odd_tile_ref, chunk),
-                ],
-                chunk,
-            )
-
-    added(head + late - 1, odd_tile_ref[0], odd_tile_ref[1], 1)
+
+    added(head + late - 1, odd_tile_ref)
 
 
 def sum_kernel(parts_ref, out_ref):
@@ -373,7 +373,7 @@
     after = shifted(first, -1)
 
     early = total // 2
-    tile, chunk = 256, 32
+    tile, chunk = 512, 32
     kept = pltpu.VMEM(w_in.shape, BF16)
     table = pltpu.VMEM((early, own), BF16)
     phases = [pltpu.VMEM((tile, own), F32)] * 2
@@ -417,7 +417,7 @@
             pltpu.VMEM((8, own), BF16),
         ]
         + phases
-        + [pltpu.VMEM((2, tile, own), BF16)] * 2,
+        + [pltpu.VMEM((2 * tile, own), BF16)] * 2,
         compiler_params=grant,
     )(before, first, last, after, w_first, w_second, w_read, hist, held, waves, cos_head, sin_head)
 

time: 51 us -> 53.4 us (1.047)
  Pallas kernels: 20.4 us -> 22.8 us
    pallas_call x1, Pallas kernels: 8.94 us -> 11.3 us  [per_device(): pl.pallas_call(functools.partial(layer_kernel, tile=tile, chunk=chunk), o...]
  transfers between devices with their start and end apart: 2 -> 2, of which waited for: 0 -> 0; matrix products, arithmetic and copies ran while one was open for 0% -> 0% of each run, Pallas kernels for 13% -> 12%
where the time goes in v10:
time: 53.4 us; the launch traced here: 53.1 us
  blocking collectives  23.4 us (44%)
  Pallas kernels  22.8 us (43%)
  starting transfers between devices  6.23 us (12%)
  between operations  0.69 us (1%)
    all_to_all x1, blocking collectives, per_device(): swapped = lax.all_to_all(partial.astype(BF16), AXES, 0, 0, tiled=True)  14.2 us
    pallas_call x1, Pallas kernels, per_device(): pl.pallas_call(functools.partial(layer_kernel, tile=tile, chunk=chunk), o...  11.3 us
    all_to_all x1, blocking collectives, per_device(): sums = lax.all_to_all(spread, AXES, 0, 0, tiled=True)  9.19 us
    pallas_call x1, Pallas kernels, per_device(): pl.pallas_call(functools.partial(early_kernel, tile=tile, chunk=chunk, fa...  6.6 us
    ppermute x2, starting transfers between devices, shifted(): return lax.ppermute(x, AXES, pairs)  6.23 us
    pallas_call x1, Pallas kernels, per_device(): pl.pallas_call(functools.partial(response_kernel, tile=4096), out_shape=(...  2.92 us
    pallas_call x1, Pallas kernels, per_device(): pl.pallas_call(pack_kernel, out_shape=(edge, edge, pltpu.VMEM(wave.shape,...  1.88 us
  transfers between devices with their start and end apart: 2, of which 0 were waited for; matrix products, arithmetic and copies ran while one was open for 0% of the time, Pallas kernels for 12%

profile of v10, /device:TPU:0, one launch (start us, length us, event | category | flops | bytes accessed | tf_op | source)
XLA Modules:
  0.0 53.1 jit_solution(3445065649707871345)
XLA Ops:
  0.6 1.9 %shard_map.103 = (bf16[128,384]{1,0:T(8,128)(2,1)S(1)}, bf16[128,384]{1,0:T(8,128)(2,1)S(1)}, f32[3,16384]{1,0:T(4,128)S(1)}, f32[3,256]{1,0:T(4,128)S(1)}) custom-call(bf16[256,256]{1,0:T(8,128)(2,1)} %feat_ref.1, f32[3,256]{1,0:T(4,128)} %pos_ref.1, s32[64,256]{1,0:T(8,128)} %bitcast.4, s32[1,256]{1,0:T(1,128)} %bitcast.5, f32[3,16384]{1,0:T(4,128)} %wave_ref.1), custom_call_target="tpu_custom_call" | custom-call | tf_op jit(solution)/shard_map/pallas_call | solution.py:365
  2.5 4.9 %collective-permute-start = (bf16[128,384]{1,0:T(8,128)(2,1)S(1)}, bf16[128,384]{1,0:T(8,128)(2,1)S(1)}, u32[]{:S(2)}, u32[]{:S(2)}) collective-permute-start(bf16[128,384]{1,0:T(8,128)(2,1)S(1)} %get-tuple-element.20.last_ref), channel_id=1, source_target_pairs={{0,1},{1,2},{2,3},{3,4},{4,5},{5,6},{6,7},{7,8},{8,9},{9,10},{10,1... | collective-permute-start | bytes 294920 | tf_op jit(solution)/shard_map/ppermute | solution.py:347
  7.5 1.3 %collective-permute-start.1 = (bf16[128,384]{1,0:T(8,128)(2,1)S(1)}, bf16[128,384]{1,0:T(8,128)(2,1)S(1)}, u32[]{:S(2)}, u32[]{:S(2)}) collective-permute-start(bf16[128,384]{1,0:T(8,128)(2,1)S(1)} %get-tuple-element.21.first_ref), channel_id=1, source_target_pairs={{1,0},{2,1},{3,2},{4,3},{5,4},{6,5},{7,6},{8,7},{9,8},{10,9},{11,1... | collective-permute-start | bytes 294920 | tf_op jit(solution)/shard_map/ppermute | solution.py:347
  8.8 6.6 %shard_map.104 = (bf16[8192,256]{1,0:T(8,128)(2,1)S(1)}, bf16[8192,256]{1,0:T(8,128)(2,1)S(1)}, f32[8,16384]{1,0:T(8,128)S(1)}, f32[256,128]{1,0:T(8,128)S(1)}, ...) custom-call(f32[3,256]{1,0:T(4,128)S(1)} %get-tuple-element.22.pos_ref, ...), custom_call_target="tpu_custom_call" | custom-call | flops 83886080 | bytes 8388608 | tf_op jit(solution)/shard_map/pallas_call | solution.py:381
  15.4 0.0 collective-permute-done.before_ref
  15.4 0.0 collective-permute-done.1.after_ref
  15.4 11.3 %shard_map.105 = (bf16[256,256]{1,0:T(8,128)(2,1)}, f32[32,2,512]{2,1,0:T(2,128)S(1)}, bf16[8192,256]{1,0:T(8,128)(2,1)S(1)}, bf16[8192,256]{1,0:T(8,128)(2,1)S(1)}) custom-call(bf16[128,384]{1,0:T(8,128)(2,1)S(1)} %collective-permute-done.before_ref, bf16[128,384]{1,0:T(8,128)(2,1)S(1)} %get-tuple-element.21.first_ref, ...), custom_call_target="tpu_custom_call" | custom-call | tf_op jit(solution)/shard_map/pallas_call | solution.py:402
  26.7 14.2 %all_to_all.10.parts_ref = bf16[32,2,512]{2,1,0:T(2,128)(2,1)S(1)} all-to-all(bf16[32,2,512]{2,1,0:T(2,128)(2,1)S(1)} %convert_element_type.3), channel_id=1, replica_groups=mesh['brick'=8,'kvec'=4] {'brick','kvec'}, dimensions={0} | all-to-all | bytes 131072 | tf_op jit(solution)/shard_map/all_to_all | solution.py:424
  40.9 0.1 shard_map.106
  41.0 9.2 %all_to_all.11.sums_ref = bf16[32,2,512]{2,1,0:T(2,128)(2,1)S(1)} all-to-all(bf16[32,2,512]{2,1,0:T(2,128)(2,1)S(1)} %shard_map.106), channel_id=1, replica_groups=mesh['brick'=8,'kvec'=4] {'brick','kvec'}, dimensions={0} | all-to-all | bytes 131072 | tf_op jit(solution)/shard_map/all_to_all | solution.py:432
  50.2 2.9 %shard_map.107 = (f32[1,256]{1,0:T(1,128)}, f32[3,256]{1,0:T(4,128)}) custom-call(bf16[32,2,512]{2,1,0:T(2,128)(2,1)S(1)} %all_to_all.11.sums_ref, f32[8,16384]{1,0:T(8,128)S(1)} %get-tuple-element.32.coef_ref, bf16[8192,256]{1,0:T(8,128)(2,1)S(1)} %get-tuple-element.28.cos_head_ref, bf16[8192,256]{1,0:T(8,128)(2,1)S(1)} %get-tuple-element.29.sin_head_ref, ...), custom_call_target="tpu_custom_call" | custom-call | tf_op jit(solution)/shard_map/pallas_call | solution.py:438
  (1 shorter events, 0.0 us)
Async XLA Ops:
  2.5 12.9 %collective-permute-start = (bf16[128,384]{1,0:T(8,128)(2,1)S(1)}, bf16[128,384]{1,0:T(8,128)(2,1)S(1)}, u32[]{:S(2)}, u32[]{:S(2)}) collective-permute-start(bf16[128,384]{1,0:T(8,128)(2,1)S(1)} %get-tuple-element.20.last_ref), channel_id=1, source_target_pairs={{0,1},{1,2},{2,3},{3,4},{4,5},{5,6},{6,7},{7,8},{8,9},{9,10},{10,1... | collective-permute-start | bytes 294920 | tf_op jit(solution)/shard_map/ppermute | solution.py:347
  7.5 7.9 %collective-permute-start.1 = (bf16[128,384]{1,0:T(8,128)(2,1)S(1)}, bf16[128,384]{1,0:T(8,128)(2,1)S(1)}, u32[]{:S(2)}, u32[]{:S(2)}) collective-permute-start(bf16[128,384]{1,0:T(8,128)(2,1)S(1)} %get-tuple-element.21.first_ref), channel_id=1, source_target_pairs={{1,0},{2,1},{3,2},{4,3},{5,4},{6,5},{7,6},{8,7},{9,8},{10,9},{11,1... | collective-permute-start | bytes 294920 | tf_op jit(solution)/shard_map/ppermute | solution.py:347

commit v11 on v9

--- a/solution.py
+++ b/solution.py
@@ -71,15 +71,28 @@
     return pl.ds(pl.multiple_of(step * tile, tile), tile)
 
 
-def phase(wave, left_ref, out_ref):
+def phase_pieces(wave, left_ref, out_ref, size):
     tile = wave.shape[1]
     u, v, w = pieces(wave * (0.5 / math.pi))
     right = jnp.concatenate([u, v, u, v, w, u, jnp.zeros((14, tile), F32)], axis=0)
-    out_ref[...] = jnp.dot(right.T.astype(BF16), left_ref[...], preferred_element_type=F32)
-
-
-def evaluate(in_ref, stores, chunk):
-    for start in range(0, in_ref.shape[0], chunk):
+    right = right.T.astype(BF16)
+
+    def piece(start):
+        out_ref[start : start + size, :] = jnp.dot(
+            right[start : start + size], left_ref[...], preferred_element_type=F32
+        )
+
+    return [functools.partial(piece, start) for start in range(0, tile, size)]
+
+
+def evaluate(in_ref, stores, chunk, woven):
+    starts = range(0, in_ref.shape[0], chunk)
+    for n, start in enumerate(starts):
+        for turn, work in enumerate(woven):
+            shift = 0 if turn % 2 else len(starts) - 1
+            low, high = ((m * len(work) + shift) // len(starts) for m in (n, n + 1))
+            for piece in work[low:high]:
+                piece()
         t = in_ref[start : start + chunk, :]
         r = t - jnp.round(t)
         x = r * horner(r * r, HALF_SINE)
@@ -155,19 +168,21 @@
             )
 
     def turn(step, out_ref):
-        phase(wave_ref[:, place(step, tile)], left_ref, out_ref)
-
-    turn(0, even_ref)
+        return phase_pieces(wave_ref[:, place(step, tile)], left_ref, out_ref, 64)
+
+    for piece in turn(0, even_ref):
+        piece()
 
     @pl.loop(0, head // 4)
     def _(block):
         base = 4 * block
         scale(2 * base)
-        for step in range(0, 4, 2):
-            turn(base + step + 1, odd_ref)
-            evaluate(even_ref, [into_table(cos_ref, sin_ref, base + step, tile, chunk)], chunk)
-            turn(jnp.minimum(base + step + 2, head - 1), even_ref)
-            evaluate(odd_ref, [into_table(cos_ref, sin_ref, base + step + 1, tile, chunk)], chunk)
+        for n in range(4):
+            now, later = (even_ref, odd_ref) if n % 2 == 0 else (odd_ref, even_ref)
+            work = turn(jnp.minimum(base + n + 1, head - 1), later)
+            evaluate(
+                now, [into_table(cos_ref, sin_ref, base + n, tile, chunk)], chunk, [work]
+            )
 
     for copy in copies:
         copy.wait()
@@ -262,45 +277,58 @@
     dims = (((1,), (1,)), ((), ()))
 
     def turn(step, out_ref):
-        phase(wave_ref[:, place(head + step, tile)], left_ref, out_ref)
-
-    def added(step, cos_tile, sin_tile, odd):
-        rows = []
-        for table in (cos_tile, sin_tile):
-            part = lax.dot_general(charge_ref[...], table, dims, preferred_element_type=F32)
-            rows.append(part[0:1] + part[1:2] + part[2:3])
+        return phase_pieces(wave_ref[:, place(head + step, tile)], left_ref, out_ref, 64)
+
+    def products(step, odd, tables):
         index = (step - odd) // 2 * per + odd * (per - 1)
         lanes = odd * (2 - per) * tile
-        sums_ref[index, :, lanes : lanes + tile] = jnp.concatenate(rows, axis=0)
-
-    turn(0, even_ref)
+
+        def piece(n, start):
+            part = lax.dot_general(
+                charge_ref[...], tables(n, start), dims, preferred_element_type=F32
+            )
+            part = part[0:1] + part[1:2] + part[2:3]
+            sums_ref[index, n : n + 1, lanes + start : lanes + start + LANES] = part
+
+        return [
+            functools.partial(piece, n, start)
+            for n in range(2)
+            for start in range(0, tile, LANES)
+        ]
+
+    def late_table(tile_ref):
+        return lambda n, start: tile_ref[n, start : start + LANES, :]
+
+    def head_table(step):
+        refs = (cos_head_ref, sin_head_ref)
+        return lambda n, start: refs[n][
+            pl.ds(pl.multiple_of(step * tile + start, LANES), LANES), :
+        ]
+
+    for piece in turn(0, even_ref):
+        piece()
 
     @pl.loop(0, late // 4)
     def _(block):
-        for pair in range(2):
-            step = 4 * block + 2 * pair
-            for n in range(2):
-                rows = place(step + n, tile)
-                added(step + n, cos_head_ref[rows, :], sin_head_ref[rows, :], n)
-            turn(step + 1, odd_ref)
-            added(head + step - 1, odd_tile_ref[0], odd_tile_ref[1], 1)
-            evaluate(
-                even_ref,
-                [into_table(cos_ref, sin_ref, step, tile, chunk), into_tile(even_tile_ref, chunk)],
-                chunk,
-            )
-            turn(jnp.minimum(step + 2, late - 1), even_ref)
-            added(head + step, even_tile_ref[0], even_tile_ref[1], 0)
-            evaluate(
-                odd_ref,
-                [
-                    into_table(cos_ref, sin_ref, step + 1, tile, chunk),
-                    into_tile(odd_tile_ref, chunk),
-                ],
-                chunk,
-            )
-
-    added(head + late - 1, odd_tile_ref[0], odd_tile_ref[1], 1)
+        base = 4 * block
+        slots = ((even_ref, even_tile_ref), (odd_ref, odd_tile_ref))
+        for n in range(4):
+            now, now_tile = slots[n % 2]
+            later, last_tile = slots[1 - n % 2]
+            step = base + n
+            work = [
+                turn(jnp.minimum(step + 1, late - 1), later),
+                products(head + step - 1, 1 - n % 2, late_table(last_tile)),
+                products(step, n % 2, head_table(step)),
+            ]
+            stores = [
+                into_table(cos_ref, sin_ref, step, tile, chunk),
+                into_tile(now_tile, chunk),
+            ]
+            evaluate(now, stores, chunk, work)
+
+    for piece in products(head + late - 1, 1, late_table(odd_tile_ref)):
+        piece()
 
 
 def sum_kernel(parts_ref, out_ref):

time: 51 us -> 52.9 us (1.037)
  Pallas kernels: 20.4 us -> 22.2 us
    pallas_call x1, Pallas kernels: 8.94 us -> 10.5 us  [per_device(): pl.pallas_call(functools.partial(layer_kernel, tile=tile, chunk=chunk), o...]
where the time goes in v11:
time: 52.9 us; the launch traced here: 52.6 us
  blocking collectives  23.4 us (44%)
  Pallas kernels  22.2 us (42%)
  starting transfers between devices  6.23 us (12%)
  between operations  0.69 us (1%)
    all_to_all x1, blocking collectives, per_device(): swapped = lax.all_to_all(partial.astype(BF16), AXES, 0, 0, tiled=True)  14.2 us
    pallas_call x1, Pallas kernels, per_device(): pl.pallas_call(functools.partial(layer_kernel, tile=tile, chunk=chunk), o...  10.5 us
    all_to_all x1, blocking collectives, per_device(): sums = lax.all_to_all(spread, AXES, 0, 0, tiled=True)  9.19 us
    pallas_call x1, Pallas kernels, per_device(): pl.pallas_call(functools.partial(early_kernel, tile=tile, chunk=chunk, fa...  6.85 us
    ppermute x2, starting transfers between devices, shifted(): return lax.ppermute(x, AXES, pairs)  6.23 us
    pallas_call x1, Pallas kernels, per_device(): pl.pallas_call(functools.partial(response_kernel, tile=4096), out_shape=(...  2.92 us
    pallas_call x1, Pallas kernels, per_device(): pl.pallas_call(pack_kernel, out_shape=(edge, edge, pltpu.VMEM(wave.shape,...  1.88 us
  transfers between devices with their start and end apart: 2, of which 0 were waited for; matrix products, arithmetic and copies ran while one was open for 0% of the time, Pallas kernels for 13%

profile of v11, /device:TPU:0, one launch (start us, length us, event | category | flops | bytes accessed | tf_op | source)
XLA Modules:
  0.0 52.6 jit_solution(15336804653139150000)
XLA Ops:
  0.6 1.9 %shard_map.103 = (bf16[128,384]{1,0:T(8,128)(2,1)S(1)}, bf16[128,384]{1,0:T(8,128)(2,1)S(1)}, f32[3,16384]{1,0:T(4,128)S(1)}, f32[3,256]{1,0:T(4,128)S(1)}) custom-call(bf16[256,256]{1,0:T(8,128)(2,1)} %feat_ref.1, f32[3,256]{1,0:T(4,128)} %pos_ref.1, s32[64,256]{1,0:T(8,128)} %bitcast.4, s32[1,256]{1,0:T(1,128)} %bitcast.5, f32[3,16384]{1,0:T(4,128)} %wave_ref.1), custom_call_target="tpu_custom_call" | custom-call | tf_op jit(solution)/shard_map/pallas_call | solution.py:393
  2.5 4.9 %collective-permute-start = (bf16[128,384]{1,0:T(8,128)(2,1)S(1)}, bf16[128,384]{1,0:T(8,128)(2,1)S(1)}, u32[]{:S(2)}, u32[]{:S(2)}) collective-permute-start(bf16[128,384]{1,0:T(8,128)(2,1)S(1)} %get-tuple-element.20.last_ref), channel_id=1, source_target_pairs={{0,1},{1,2},{2,3},{3,4},{4,5},{5,6},{6,7},{7,8},{8,9},{9,10},{10,1... | collective-permute-start | bytes 294920 | tf_op jit(solution)/shard_map/ppermute | solution.py:375
  7.5 1.3 %collective-permute-start.1 = (bf16[128,384]{1,0:T(8,128)(2,1)S(1)}, bf16[128,384]{1,0:T(8,128)(2,1)S(1)}, u32[]{:S(2)}, u32[]{:S(2)}) collective-permute-start(bf16[128,384]{1,0:T(8,128)(2,1)S(1)} %get-tuple-element.21.first_ref), channel_id=1, source_target_pairs={{1,0},{2,1},{3,2},{4,3},{5,4},{6,5},{7,6},{8,7},{9,8},{10,9},{11,1... | collective-permute-start | bytes 294920 | tf_op jit(solution)/shard_map/ppermute | solution.py:375
  8.8 6.8 %shard_map.104 = (bf16[8192,256]{1,0:T(8,128)(2,1)S(1)}, bf16[8192,256]{1,0:T(8,128)(2,1)S(1)}, f32[8,16384]{1,0:T(8,128)S(1)}, f32[256,128]{1,0:T(8,128)S(1)}, ...) custom-call(f32[3,256]{1,0:T(4,128)S(1)} %get-tuple-element.22.pos_ref, ...), custom_call_target="tpu_custom_call" | custom-call | flops 83886080 | bytes 8388608 | tf_op jit(solution)/shard_map/pallas_call | solution.py:409
  15.6 0.0 collective-permute-done.before_ref
  15.6 0.0 collective-permute-done.1.after_ref
  15.6 10.5 %shard_map.105 = (bf16[256,256]{1,0:T(8,128)(2,1)}, f32[32,2,512]{2,1,0:T(2,128)S(1)}, bf16[8192,256]{1,0:T(8,128)(2,1)S(1)}, bf16[8192,256]{1,0:T(8,128)(2,1)S(1)}) custom-call(bf16[128,384]{1,0:T(8,128)(2,1)S(1)} %collective-permute-done.before_ref, bf16[128,384]{1,0:T(8,128)(2,1)S(1)} %get-tuple-element.21.first_ref, ...), custom_call_target="tpu_custom_call" | custom-call | tf_op jit(solution)/shard_map/pallas_call | solution.py:430
  26.2 14.2 %all_to_all.10.parts_ref = bf16[32,2,512]{2,1,0:T(2,128)(2,1)S(1)} all-to-all(bf16[32,2,512]{2,1,0:T(2,128)(2,1)S(1)} %convert_element_type.3), channel_id=1, replica_groups=mesh['brick'=8,'kvec'=4] {'brick','kvec'}, dimensions={0} | all-to-all | bytes 131072 | tf_op jit(solution)/shard_map/all_to_all | solution.py:452
  40.4 0.1 shard_map.106
  40.5 9.2 %all_to_all.11.sums_ref = bf16[32,2,512]{2,1,0:T(2,128)(2,1)S(1)} all-to-all(bf16[32,2,512]{2,1,0:T(2,128)(2,1)S(1)} %shard_map.106), channel_id=1, replica_groups=mesh['brick'=8,'kvec'=4] {'brick','kvec'}, dimensions={0} | all-to-all | bytes 131072 | tf_op jit(solution)/shard_map/all_to_all | solution.py:460
  49.7 2.9 %shard_map.107 = (f32[1,256]{1,0:T(1,128)}, f32[3,256]{1,0:T(4,128)}) custom-call(bf16[32,2,512]{2,1,0:T(2,128)(2,1)S(1)} %all_to_all.11.sums_ref, f32[8,16384]{1,0:T(8,128)S(1)} %get-tuple-element.32.coef_ref, bf16[8192,256]{1,0:T(8,128)(2,1)S(1)} %get-tuple-element.28.cos_head_ref, bf16[8192,256]{1,0:T(8,128)(2,1)S(1)} %get-tuple-element.29.sin_head_ref, ...), custom_call_target="tpu_custom_call" | custom-call | tf_op jit(solution)/shard_map/pallas_call | solution.py:466
  (1 shorter events, 0.0 us)
Async XLA Ops:
  2.5 13.1 %collective-permute-start = (bf16[128,384]{1,0:T(8,128)(2,1)S(1)}, bf16[128,384]{1,0:T(8,128)(2,1)S(1)}, u32[]{:S(2)}, u32[]{:S(2)}) collective-permute-start(bf16[128,384]{1,0:T(8,128)(2,1)S(1)} %get-tuple-element.20.last_ref), channel_id=1, source_target_pairs={{0,1},{1,2},{2,3},{3,4},{4,5},{5,6},{6,7},{7,8},{8,9},{9,10},{10,1... | collective-permute-start | bytes 294920 | tf_op jit(solution)/shard_map/ppermute | solution.py:375
  7.5 8.2 %collective-permute-start.1 = (bf16[128,384]{1,0:T(8,128)(2,1)S(1)}, bf16[128,384]{1,0:T(8,128)(2,1)S(1)}, u32[]{:S(2)}, u32[]{:S(2)}) collective-permute-start(bf16[128,384]{1,0:T(8,128)(2,1)S(1)} %get-tuple-element.21.first_ref), channel_id=1, source_target_pairs={{1,0},{2,1},{3,2},{4,3},{5,4},{6,5},{7,6},{8,7},{9,8},{10,9},{11,1... | collective-permute-start | bytes 294920 | tf_op jit(solution)/shard_map/ppermute | solution.py:375

commit v12 on v9

--- a/solution.py
+++ b/solution.py
@@ -63,8 +63,8 @@
 def atom_pieces(pos_ref):
     a, b, c = pieces(pos_ref[...])
     own = pos_ref.shape[1]
-    left = jnp.concatenate([a, a, b, b, a, c, jnp.zeros((14, own), F32)], axis=0)
-    return left.astype(BF16)
+    left = jnp.concatenate([a, a, b, b, a, c, jnp.zeros((LANES - 18, own), F32)], axis=0)
+    return left.T.astype(BF16)[:, :32]
 
 
 def place(step, tile):
@@ -75,7 +75,7 @@
     tile = wave.shape[1]
     u, v, w = pieces(wave * (0.5 / math.pi))
     right = jnp.concatenate([u, v, u, v, w, u, jnp.zeros((14, tile), F32)], axis=0)
-    out_ref[...] = jnp.dot(right.T.astype(BF16), left_ref[...], preferred_element_type=F32)
+    out_ref[...] = jnp.dot(left_ref[...], right.astype(BF16), preferred_element_type=F32)
 
 
 def evaluate(in_ref, stores, chunk):
@@ -93,9 +93,8 @@
 
 def into_table(cos_ref, sin_ref, step, tile, chunk):
     def store(start, cosine, sine):
-        rows = pl.ds(pl.multiple_of(step * tile + start, chunk), chunk)
-        cos_ref[rows, :] = cosine
-        sin_ref[rows, :] = sine
+        cos_ref[start : start + chunk, place(step, tile)] = cosine
+        sin_ref[start : start + chunk, place(step, tile)] = sine
 
     return store
 
@@ -123,8 +122,8 @@
 
 def early_kernel(
     pos_ref, wave_ref, first_ref, last_ref, w_in_ref, w_out_ref, w_charge_ref, cos_ref, sin_ref,
-    coef_ref, hist_ref, w_in_out, w_out_out, w_charge_out, left_ref, even_ref, odd_ref, sems,
-    *, tile, chunk, factor,
+    hist_ref, w_in_out, w_out_out, w_charge_out, left_ref, even_ref, odd_ref, sems,
+    *, tile, chunk,
 ):
     copies = [
         pltpu.make_async_copy(source, target, sems.at[n])
@@ -138,21 +137,7 @@
     channels = w_in_ref.shape[1]
     for n, ref in enumerate((first_ref, last_ref)):
         hist_ref[n * LANES : (n + 1) * LANES, :] = histogram(ref[:64, channels:].astype(F32))
-    head = cos_ref.shape[0] // tile
-    group = 8
-
-    def scale(step):
-        waves = [wave_ref[:, place(step + n, tile)] for n in range(group)]
-        ksq = jnp.zeros((group, tile), F32)
-        for c in range(3):
-            part = jnp.concatenate([w[c : c + 1] for w in waves], axis=0)
-            ksq = ksq + part * part
-        coef = factor * jnp.exp(-0.1 * ksq) / ksq
-        one = jnp.ones((1, tile), F32)
-        for n, w in enumerate(waves):
-            coef_ref[:, place(step + n, tile)] = coef[n : n + 1] * jnp.concatenate(
-                [one, w, one, w], axis=0
-            )
+    head = cos_ref.shape[1] // tile
 
     def turn(step, out_ref):
         phase(wave_ref[:, place(step, tile)], left_ref, out_ref)
@@ -162,7 +147,6 @@
     @pl.loop(0, head // 4)
     def _(block):
         base = 4 * block
-        scale(2 * base)
         for step in range(0, 4, 2):
             turn(base + step + 1, odd_ref)
             evaluate(even_ref, [into_table(cos_ref, sin_ref, base + step, tile, chunk)], chunk)
@@ -180,8 +164,8 @@
 def layer_kernel(
     before_ref, first_ref, last_ref, after_ref, w_in_ref, w_out_ref, w_charge_ref, hist_ref,
     pos_ref, wave_ref, cos_head_ref, sin_head_ref, hidden_ref, sums_ref, cos_ref, sin_ref,
-    feat_ref, mid_ref, matrix_ref, left_ref, charge_ref, even_ref, odd_ref, even_tile_ref,
-    odd_tile_ref, *, tile, chunk,
+    coef_ref, feat_ref, mid_ref, matrix_ref, left_ref, charge_ref, even_ref, odd_ref, even_tile_ref,
+    odd_tile_ref, *, tile, chunk, factor,
 ):
     parts = (before_ref, first_ref, last_ref, after_ref)
     half = before_ref.shape[0]
@@ -255,50 +239,58 @@
 
     charge_ref[...] = charges
     left_ref[...] = atom_pieces(pos_ref)
-    head = cos_head_ref.shape[0] // tile
-    late = cos_ref.shape[0] // tile
+    head = cos_head_ref.shape[1] // tile
+    late = cos_ref.shape[1] // tile
     share = sums_ref.shape[2]
     per = 2 * tile // share
-    dims = (((1,), (1,)), ((), ()))
+    group = 8
+
+    def scale(step):
+        waves = [wave_ref[:, place(step + n, tile)] for n in range(group)]
+        ksq = jnp.zeros((group, tile), F32)
+        for c in range(3):
+            part = jnp.concatenate([w[c : c + 1] for w in waves], axis=0)
+            ksq = ksq + part * part
+        coef = factor * jnp.exp(-0.1 * ksq) / ksq
+        one = jnp.ones((1, tile), F32)
+        for n, w in enumerate(waves):
+            coef_ref[:, place(step + n, tile)] = coef[n : n + 1] * jnp.concatenate(
+                [one, w, one, w], axis=0
+            )
 
     def turn(step, out_ref):
         phase(wave_ref[:, place(head + step, tile)], left_ref, out_ref)
 
     def added(step, cos_tile, sin_tile, odd):
-        rows = []
-        for table in (cos_tile, sin_tile):
-            part = lax.dot_general(charge_ref[...], table, dims, preferred_element_type=F32)
-            rows.append(part[0:1] + part[1:2] + part[2:3])
         index = (step - odd) // 2 * per + odd * (per - 1)
         lanes = odd * (2 - per) * tile
-        sums_ref[index, :, lanes : lanes + tile] = jnp.concatenate(rows, axis=0)
+        for n, table in enumerate((cos_tile, sin_tile)):
+            part = jnp.dot(charge_ref[...], table, preferred_element_type=F32)
+            part = part[0:1] + part[1:2] + part[2:3]
+            sums_ref[index, n : n + 1, lanes : lanes + tile] = part
 
     turn(0, even_ref)
 
     @pl.loop(0, late // 4)
     def _(block):
-        for pair in range(2):
-            step = 4 * block + 2 * pair
-            for n in range(2):
-                rows = place(step + n, tile)
-                added(step + n, cos_head_ref[rows, :], sin_head_ref[rows, :], n)
-            turn(step + 1, odd_ref)
-            added(head + step - 1, odd_tile_ref[0], odd_tile_ref[1], 1)
-            evaluate(
-                even_ref,
-                [into_table(cos_ref, sin_ref, step, tile, chunk), into_tile(even_tile_ref, chunk)],
-                chunk,
-            )
-            turn(jnp.minimum(step + 2, late - 1), even_ref)
-            added(head + step, even_tile_ref[0], even_tile_ref[1], 0)
-            evaluate(
-                odd_ref,
-                [
-                    into_table(cos_ref, sin_ref, step + 1, tile, chunk),
-                    into_tile(odd_tile_ref, chunk),
-                ],
-                chunk,
-            )
+        base = 4 * block
+        slots = ((even_ref, even_tile_ref), (odd_ref, odd_tile_ref))
+        for n in range(4):
+            now, now_tile = slots[n % 2]
+            later, last_tile = slots[1 - n % 2]
+            step = base + n
+            turn(jnp.minimum(step + 1, late - 1), later)
+            added(head + step - 1, last_tile[0], last_tile[1], 1 - n % 2)
+            for m in range(3 * n, 3 * n + 3):
+                span = place(3 * base + m, tile)
+                added(3 * base + m, cos_head_ref[:, span], sin_head_ref[:, span], m % 2)
+            if n % 2 == 0:
+                scale(4 * base + 4 * n)
+            stores = [
+                into_table(cos_ref, sin_ref, step, tile, chunk),
+                into_tile(now_tile, chunk),
+            ]
+            evaluate(now, stores, chunk)
 
     added(head + late - 1, odd_tile_ref[0], odd_tile_ref[1], 1)
 
@@ -312,29 +304,34 @@
     sums_ref, coef_ref, cos_head_ref, sin_head_ref, cos_ref, sin_ref, pot_ref, field_ref, *, tile
 ):
     share = sums_ref.shape[2]
-    per = tile // share
     row = lax.broadcasted_iota(jnp.int32, (8, share), 0)
     lead = row % 4 == 0
     upper = row < 4
-    totals = []
-    segments = [(cos_head_ref, sin_head_ref, k) for k in range(0, cos_head_ref.shape[0], tile)]
-    segments += [(cos_ref, sin_ref, k) for k in range(0, cos_ref.shape[0], tile)]
-    for index, (cos_part, sin_part, start) in enumerate(segments):
-        factors = ([], [])
-        for q in range(index * per, (index + 1) * per):
-            scaled = coef_ref[:, q * share : (q + 1) * share]
-            sums = sums_ref[q].astype(F32)
-            cosine = sums[0:1]
-            sine = sums[1:2]
-            for n, (top, other) in enumerate(((cosine, -sine), (sine, cosine))):
-                full = scaled * jnp.where(lead, top, other)
-                hi = full.astype(BF16).astype(F32)
-                factors[n].append(jnp.where(upper, hi, full - hi))
-        for n, ref in enumerate((cos_part, sin_part)):
-            wide = jnp.concatenate(factors[n], axis=1).astype(BF16)
-            totals.append(
-                jnp.dot(wide, ref[start : start + tile, :], preferred_element_type=F32)
-            )
+    totals = [None] * 4
+    dims = (((1,), (1,)), ((), ()))
+    head = cos_head_ref.shape[1]
+    for q in range(sums_ref.shape[0]):
+        scaled = coef_ref[:, q * share : (q + 1) * share]
+        sums = sums_ref[q].astype(F32)
+        cosine = sums[0:1]
+        sine = sums[1:2]
+        early = q * share < head
+        offset = q * share - (0 if early else head)
+        refs = (cos_head_ref, sin_head_ref) if early else (cos_ref, sin_ref)
+        for n, (top, other) in enumerate(((cosine, -sine), (sine, cosine))):
+            full = scaled * jnp.where(lead, top, other)
+            hi = full.astype(BF16).astype(F32)
+            wide = jnp.where(upper, hi, full - hi).astype(BF16)
+            for start in range(0, share, tile):
+                part = lax.dot_general(
+                    wide[:, start : start + tile],
+                    refs[n][:, offset + start : offset + start + tile],
+                    dims,
+                    preferred_element_type=F32,
+                )
+                spot = (2 * start // tile + n) % 4
+                totals[spot] = part if totals[spot] is None else totals[spot] + part
+    totals = [t for t in totals if t is not None]
     total = sum(totals[1:], totals[0])
     result = total[:4] + total[4:]
     pot_ref[...] = result[0:1]
@@ -372,52 +369,52 @@
     before = shifted(last, 1)
     after = shifted(first, -1)
 
-    early = total // 2
+    early = 3 * total // 4
     tile, chunk = 256, 32
     kept = pltpu.VMEM(w_in.shape, BF16)
-    table = pltpu.VMEM((early, own), BF16)
-    phases = [pltpu.VMEM((tile, own), F32)] * 2
+    table = pltpu.VMEM((own, early), BF16)
+    phases = [pltpu.VMEM((own, tile), F32)] * 2
     grant = pltpu.CompilerParams(vmem_limit_bytes=16 << 20)
-    cos_head, sin_head, coef, hist, w_first, w_second, w_read = pl.pallas_call(
-        functools.partial(early_kernel, tile=tile, chunk=chunk, factor=factor),
+    cos_head, sin_head, hist, w_first, w_second, w_read = pl.pallas_call(
+        functools.partial(early_kernel, tile=tile, chunk=chunk),
         out_shape=(
             table,
             table,
-            pltpu.VMEM((8, total), F32),
             pltpu.VMEM((own, LANES), F32),
             kept,
             kept,
             pltpu.VMEM((1, channels), F32),
         ),
         in_specs=[VMEM] * 4 + [HBM] * 3,
-        out_specs=(VMEM,) * 7,
-        scratch_shapes=[pltpu.VMEM((32, own), BF16)] + phases + [dma((3,))],
+        out_specs=(VMEM,) * 6,
+        scratch_shapes=[pltpu.VMEM((own, 32), BF16)] + phases + [dma((3,))],
         compiler_params=grant,
         cost_estimate=pl.CostEstimate(
             flops=own * early * 40, bytes_accessed=4 * own * early, transcendentals=0
         ),
     )(held, waves, first, last, w_in, w_out, w_charge)
 
-    table = pltpu.VMEM((total - early, own), BF16)
-    hidden, partial, cos_late, sin_late = pl.pallas_call(
-        functools.partial(layer_kernel, tile=tile, chunk=chunk),
+    table = pltpu.VMEM((own, total - early), BF16)
+    hidden, partial, cos_late, sin_late, coef = pl.pallas_call(
+        functools.partial(layer_kernel, tile=tile, chunk=chunk, factor=factor),
         out_shape=(
             jax.ShapeDtypeStruct((own, channels), BF16),
             jax.ShapeDtypeStruct((devices, 2, share), F32),
             table,
             table,
+            pltpu.VMEM((8, total), F32),
         ),
         in_specs=[VMEM] * 12,
-        out_specs=(VMEM,) * 4,
+        out_specs=(VMEM,) * 5,
         scratch_shapes=[
             pltpu.VMEM((4 * half + HALO, channels), BF16),
             pltpu.VMEM((own + 3 * HALO, channels), BF16),
             pltpu.VMEM((own // HALO + 2, 2 * HALO, 2 * LANES), BF16),
-            pltpu.VMEM((32, own), BF16),
+            pltpu.VMEM((own, 32), BF16),
             pltpu.VMEM((8, own), BF16),
         ]
         + phases
-        + [pltpu.VMEM((2, tile, own), BF16)] * 2,
+        + [pltpu.VMEM((2, own, tile), BF16)] * 2,
         compiler_params=grant,
     )(before, first, last, after, w_first, w_second, w_read, hist, held, waves, cos_head, sin_head)
 
@@ -436,7 +433,7 @@
         for x in (cos_head, sin_head, cos_late, sin_late)
     ]
     potential, field = pl.pallas_call(
-        functools.partial(response_kernel, tile=4096),
+        functools.partial(response_kernel, tile=tile),
         out_shape=(
             jax.ShapeDtypeStruct((1, own), F32),
             jax.ShapeDtypeStruct((3, own), F32),

time: 51 us -> 53.4 us (1.047)
  Pallas kernels: 20.4 us -> 22.8 us
    pallas_call x3, Pallas kernels: 18.5 us -> 20.9 us  [the longest x1 8.26 us: per_device(): pl.pallas_call(functools.partial(early_kernel, tile=tile, chunk=chunk), o...]
  transfers between devices with their start and end apart: 2 -> 2, of which waited for: 0 -> 0; matrix products, arithmetic and copies ran while one was open for 0% -> 0% of each run, Pallas kernels for 13% -> 16%
where the time goes in v12:
time: 53.4 us; the launch traced here: 53.2 us
  blocking collectives  23.4 us (44%)
  Pallas kernels  22.8 us (43%)
  starting transfers between devices  6.23 us (12%)
  between operations  0.69 us (1%)
    all_to_all x1, blocking collectives, per_device(): swapped = lax.all_to_all(partial.astype(BF16), AXES, 0, 0, tiled=True)  14.2 us
    all_to_all x1, blocking collectives, per_device(): sums = lax.all_to_all(spread, AXES, 0, 0, tiled=True)  9.19 us
    pallas_call x1, Pallas kernels, per_device(): pl.pallas_call(functools.partial(early_kernel, tile=tile, chunk=chunk), o...  8.26 us
    pallas_call x1, Pallas kernels, per_device(): pl.pallas_call(functools.partial(layer_kernel, tile=tile, chunk=chunk, fa...  7.57 us
    ppermute x2, starting transfers between devices, shifted(): return lax.ppermute(x, AXES, pairs)  6.23 us
    pallas_call x1, Pallas kernels, per_device(): pl.pallas_call(functools.partial(response_kernel, tile=tile), out_shape=(...  5.03 us
    pallas_call x1, Pallas kernels, per_device(): pl.pallas_call(pack_kernel, out_shape=(edge, edge, pltpu.VMEM(wave.shape,...  1.88 us
  transfers between devices with their start and end apart: 2, of which 0 were waited for; matrix products, arithmetic and copies ran while one was open for 0% of the time, Pallas kernels for 16%

profile of v12, /device:TPU:0, one launch (start us, length us, event | category | flops | bytes accessed | tf_op | source)
XLA Modules:
  0.0 53.2 jit_solution(6941558110851131031)
XLA Ops:
  0.6 1.9 %shard_map.103 = (bf16[128,384]{1,0:T(8,128)(2,1)S(1)}, bf16[128,384]{1,0:T(8,128)(2,1)S(1)}, f32[3,16384]{1,0:T(4,128)S(1)}, f32[3,256]{1,0:T(4,128)S(1)}) custom-call(bf16[256,256]{1,0:T(8,128)(2,1)} %feat_ref.1, f32[3,256]{1,0:T(4,128)} %pos_ref.1, s32[64,256]{1,0:T(8,128)} %bitcast.4, s32[1,256]{1,0:T(1,128)} %bitcast.5, f32[3,16384]{1,0:T(4,128)} %wave_ref.1), custom_call_target="tpu_custom_call" | custom-call | tf_op jit(solution)/shard_map/pallas_call | solution.py:362
  2.5 4.9 %collective-permute-start = (bf16[128,384]{1,0:T(8,128)(2,1)S(1)}, bf16[128,384]{1,0:T(8,128)(2,1)S(1)}, u32[]{:S(2)}, u32[]{:S(2)}) collective-permute-start(bf16[128,384]{1,0:T(8,128)(2,1)S(1)} %get-tuple-element.20.last_ref), channel_id=1, source_target_pairs={{0,1},{1,2},{2,3},{3,4},{4,5},{5,6},{6,7},{7,8},{8,9},{9,10},{10,1... | collective-permute-start | bytes 294920 | tf_op jit(solution)/shard_map/ppermute | solution.py:344
  7.5 1.3 %collective-permute-start.1 = (bf16[128,384]{1,0:T(8,128)(2,1)S(1)}, bf16[128,384]{1,0:T(8,128)(2,1)S(1)}, u32[]{:S(2)}, u32[]{:S(2)}) collective-permute-start(bf16[128,384]{1,0:T(8,128)(2,1)S(1)} %get-tuple-element.21.first_ref), channel_id=1, source_target_pairs={{1,0},{2,1},{3,2},{4,3},{5,4},{6,5},{7,6},{8,7},{9,8},{10,9},{11,1... | collective-permute-start | bytes 294920 | tf_op jit(solution)/shard_map/ppermute | solution.py:344
  8.8 8.3 %shard_map.104 = (bf16[256,12288]{1,0:T(8,128)(2,1)S(1)}, bf16[256,12288]{1,0:T(8,128)(2,1)S(1)}, f32[256,128]{1,0:T(8,128)S(1)}, bf16[2,256,256]{2,1,0:T(8,128)...) custom-call(f32[3,256]{1,0:T(4,128)S(1)} %get-tuple-element.22.pos_ref, ...), custom_call_target="tpu_custom_call" | custom-call | flops 125829120 | bytes 12582912 | tf_op jit(solution)/shard_map/pallas_call | solution.py:378
  17.0 0.0 collective-permute-done.before_ref
  17.0 0.0 collective-permute-done.1.after_ref
  17.1 7.6 %shard_map.105 = (bf16[256,256]{1,0:T(8,128)(2,1)}, f32[32,2,512]{2,1,0:T(2,128)S(1)}, bf16[256,4096]{1,0:T(8,128)(2,1)S(1)}, bf16[256,4096]{1,0:T(8,128)(2,1)S(1)}, f32[8,16384]{1,0:T(8,128)S(1)}) custom-call(bf16[128,384]{1,0:T(8,128)(2,1)S(1)} %collective-permute-done.before_ref, bf16[128,384]{1,0:T(8,128)(2,1)S(1)} %get-tuple-element.21.first_ref, ...), custom_call_target="tpu_custom_call" | custom-call | tf_op jit(solution)/shard_map/pallas_call | solution.py:398
  24.7 14.2 %all_to_all.10.parts_ref = bf16[32,2,512]{2,1,0:T(2,128)(2,1)S(1)} all-to-all(bf16[32,2,512]{2,1,0:T(2,128)(2,1)S(1)} %convert_element_type.3), channel_id=1, replica_groups=mesh['brick'=8,'kvec'=4] {'brick','kvec'}, dimensions={0} | all-to-all | bytes 131072 | tf_op jit(solution)/shard_map/all_to_all | solution.py:421
  38.9 0.1 shard_map.106
  39.0 9.2 %all_to_all.11.sums_ref = bf16[32,2,512]{2,1,0:T(2,128)(2,1)S(1)} all-to-all(bf16[32,2,512]{2,1,0:T(2,128)(2,1)S(1)} %shard_map.106), channel_id=1, replica_groups=mesh['brick'=8,'kvec'=4] {'brick','kvec'}, dimensions={0} | all-to-all | bytes 131072 | tf_op jit(solution)/shard_map/all_to_all | solution.py:429
  48.2 5.0 %shard_map.107 = (f32[1,256]{1,0:T(1,128)}, f32[3,256]{1,0:T(4,128)}) custom-call(bf16[32,2,512]{2,1,0:T(2,128)(2,1)S(1)} %all_to_all.11.sums_ref, f32[8,16384]{1,0:T(8,128)S(1)} %get-tuple-element.32.coef_ref, bf16[256,12288]{1,0:T(8,128)(2,1)S(1)} %get-tuple-element.28.cos_head_ref, bf16[256,12288]{1,0:T(8,128)(2,1)S(1)} %get-tuple-element.29.sin_head_ref, ...), custom_call_target="tpu_custom_call" | custom-call | tf_op jit(solution)/shard_map/pallas_call | solution.py:435
  (1 shorter events, 0.0 us)
Async XLA Ops:
  2.5 14.5 %collective-permute-start = (bf16[128,384]{1,0:T(8,128)(2,1)S(1)}, bf16[128,384]{1,0:T(8,128)(2,1)S(1)}, u32[]{:S(2)}, u32[]{:S(2)}) collective-permute-start(bf16[128,384]{1,0:T(8,128)(2,1)S(1)} %get-tuple-element.20.last_ref), channel_id=1, source_target_pairs={{0,1},{1,2},{2,3},{3,4},{4,5},{5,6},{6,7},{7,8},{8,9},{9,10},{10,1... | collective-permute-start | bytes 294920 | tf_op jit(solution)/shard_map/ppermute | solution.py:344
  7.5 9.6 %collective-permute-start.1 = (bf16[128,384]{1,0:T(8,128)(2,1)S(1)}, bf16[128,384]{1,0:T(8,128)(2,1)S(1)}, u32[]{:S(2)}, u32[]{:S(2)}) collective-permute-start(bf16[128,384]{1,0:T(8,128)(2,1)S(1)} %get-tuple-element.21.first_ref), channel_id=1, source_target_pairs={{1,0},{2,1},{3,2},{4,3},{5,4},{6,5},{7,6},{8,7},{9,8},{10,9},{11,1... | collective-permute-start | bytes 294920 | tf_op jit(solution)/shard_map/ppermute | solution.py:344

commit v13 on v9

--- a/solution.py
+++ b/solution.py
@@ -157,12 +157,13 @@
     def turn(step, out_ref):
         phase(wave_ref[:, place(step, tile)], left_ref, out_ref)
 
+    scale(0)
     turn(0, even_ref)
 
     @pl.loop(0, head // 4)
     def _(block):
         base = 4 * block
-        scale(2 * base)
+        scale(2 * base + group)
         for step in range(0, 4, 2):
             turn(base + step + 1, odd_ref)
             evaluate(even_ref, [into_table(cos_ref, sin_ref, base + step, tile, chunk)], chunk)
@@ -219,6 +220,23 @@
         matrix_ref[block, :HALO, :] = upper
         matrix_ref[block, HALO:, :] = lower
 
+    left_ref[...] = atom_pieces(pos_ref)
+    head = cos_head_ref.shape[0] // tile
+    late = cos_ref.shape[0] // tile
+    filled = 8
+    slots = (even_ref, odd_ref)
+
+    def turn(step, out_ref):
+        phase(wave_ref[:, place(head + step, tile)], left_ref, out_ref)
+
+    def filler(step):
+        turn(step + 1, slots[(step + 1) % 2])
+        evaluate(
+            slots[step % 2], [into_table(cos_ref, sin_ref, step, tile, chunk)], chunk
+        )
+
+    turn(0, even_ref)
+
     def advance(source_ref, layer, block_ids, row0, residual):
         messages = []
         for block in block_ids:
@@ -229,11 +247,16 @@
                 preferred_element_type=F32,
             )
             messages.append(out[:HALO] + out[HALO:])
+        filler(4 * layer)
         message = jnp.concatenate(messages, axis=0)
         scale = lax.rsqrt(jnp.mean(message * message, axis=-1, keepdims=True) + 1e-05)
+        filler(4 * layer + 1)
         normed = (message * scale).astype(BF16)
-        inner = silu(jnp.dot(normed, w_in_ref[layer], preferred_element_type=F32)).astype(BF16)
+        inner = jnp.dot(normed, w_in_ref[layer], preferred_element_type=F32)
+        filler(4 * layer + 2)
+        inner = silu(inner).astype(BF16)
         update = jnp.dot(inner, w_out_ref[layer], preferred_element_type=F32)
+        filler(4 * layer + 3)
         return (residual.astype(F32) + update).astype(BF16)
 
     grown = own + 2 * HALO
@@ -254,15 +277,9 @@
     charges = jnp.concatenate([hi, mid, lo, jnp.zeros((5, own), F32)], axis=0).astype(BF16)
 
     charge_ref[...] = charges
-    left_ref[...] = atom_pieces(pos_ref)
-    head = cos_head_ref.shape[0] // tile
-    late = cos_ref.shape[0] // tile
     share = sums_ref.shape[2]
     per = 2 * tile // share
     dims = (((1,), (1,)), ((), ()))
-
-    def turn(step, out_ref):
-        phase(wave_ref[:, place(head + step, tile)], left_ref, out_ref)
 
     def added(step, cos_tile, sin_tile, odd):
         rows = []
@@ -273,15 +290,18 @@
         lanes = odd * (2 - per) * tile
         sums_ref[index, :, lanes : lanes + tile] = jnp.concatenate(rows, axis=0)
 
-    turn(0, even_ref)
-
-    @pl.loop(0, late // 4)
+    for step in range(filled - 1):
+        rows = place(step, tile)
+        added(head + step, cos_ref[rows, :], sin_ref[rows, :], step % 2)
+
+    @pl.loop(0, (late - filled) // 4)
     def _(block):
         for pair in range(2):
-            step = 4 * block + 2 * pair
+            early = 4 * block + 2 * pair
+            step = early + filled
             for n in range(2):
-                rows = place(step + n, tile)
-                added(step + n, cos_head_ref[rows, :], sin_head_ref[rows, :], n)
+                rows = place(early + n, tile)
+                added(early + n, cos_head_ref[rows, :], sin_head_ref[rows, :], n)
             turn(step + 1, odd_ref)
             added(head + step - 1, odd_tile_ref[0], odd_tile_ref[1], 1)
             evaluate(
@@ -300,6 +320,8 @@
                 chunk,
             )
 
+    rows = place(filled - 1, tile)
+    added(head + filled - 1, cos_ref[rows, :], sin_ref[rows, :], 1)
     added(head + late - 1, odd_tile_ref[0], odd_tile_ref[1], 1)
 
 
@@ -372,8 +394,8 @@
     before = shifted(last, 1)
     after = shifted(first, -1)
 
-    early = total // 2
     tile, chunk = 256, 32
+    early = (total - 8 * tile) // 2
     kept = pltpu.VMEM(w_in.shape, BF16)
     table = pltpu.VMEM((early, own), BF16)
     phases = [pltpu.VMEM((tile, own), F32)] * 2
@@ -436,7 +458,7 @@
         for x in (cos_head, sin_head, cos_late, sin_late)
     ]
     potential, field = pl.pallas_call(
-        functools.partial(response_kernel, tile=4096),
+        functools.partial(response_kernel, tile=1024),
         out_shape=(
             jax.ShapeDtypeStruct((1, own), F32),
             jax.ShapeDtypeStruct((3, own), F32),

time: 51 us -> 50.4 us (0.988)
  waiting for transfers between devices: 0.01 us -> 0.67 us
  Pallas kernels: 20.4 us -> 19.8 us
  blocking collectives: 23.4 us -> 22.8 us
    pallas_call x1, Pallas kernels: 6.6 us -> 5.78 us  [per_device(): pl.pallas_call(functools.partial(early_kernel, tile=tile, chunk=chunk, fa...]
    ppermute x2, waiting for transfers between devices: 0.01 us -> 0.67 us  [shifted(): return lax.ppermute(x, AXES, pairs)]
    all_to_all x1, blocking collectives: 14.2 us -> 13.6 us  [per_device(): swapped = lax.all_to_all(partial.astype(BF16), AXES, 0, 0, tiled=True)]
  transfers between devices with their start and end apart: 2 -> 2, of which waited for: 0 -> 1; matrix products, arithmetic and copies ran while one was open for 0% -> 0% of each run, Pallas kernels for 13% -> 12%
where the time goes in v13:
time: 50.4 us; the launch traced here: 50.1 us
  blocking collectives  22.8 us (45%)
  Pallas kernels  19.8 us (39%)
  starting transfers between devices  6.23 us (12%)
  between operations  0.68 us (1%)
  waiting for transfers between devices  0.67 us (1%)
    all_to_all x1, blocking collectives, per_device(): swapped = lax.all_to_all(partial.astype(BF16), AXES, 0, 0, tiled=True)  13.6 us
    all_to_all x1, blocking collectives, per_device(): sums = lax.all_to_all(spread, AXES, 0, 0, tiled=True)  9.19 us
    pallas_call x1, Pallas kernels, per_device(): pl.pallas_call(functools.partial(layer_kernel, tile=tile, chunk=chunk), o...  9.11 us
    ppermute x2, starting transfers between devices, shifted(): return lax.ppermute(x, AXES, pairs)  6.23 us
    pallas_call x1, Pallas kernels, per_device(): pl.pallas_call(functools.partial(early_kernel, tile=tile, chunk=chunk, fa...  5.78 us
    pallas_call x1, Pallas kernels, per_device(): pl.pallas_call(functools.partial(response_kernel, tile=1024), out_shape=(...  2.9 us
    pallas_call x1, Pallas kernels, per_device(): pl.pallas_call(pack_kernel, out_shape=(edge, edge, pltpu.VMEM(wave.shape,...  1.88 us
  transfers between devices with their start and end apart: 2, of which 1 were waited for; matrix products, arithmetic and copies ran while one was open for 0% of the time, Pallas kernels for 12%

profile of v13, /device:TPU:0, one launch (start us, length us, event | category | flops | bytes accessed | tf_op | source)
XLA Modules:
  0.0 50.1 jit_solution(12570377955714193177)
XLA Ops:
  0.6 1.9 %shard_map.103 = (bf16[128,384]{1,0:T(8,128)(2,1)S(1)}, bf16[128,384]{1,0:T(8,128)(2,1)S(1)}, f32[3,16384]{1,0:T(4,128)S(1)}, f32[3,256]{1,0:T(4,128)S(1)}) custom-call(bf16[256,256]{1,0:T(8,128)(2,1)} %feat_ref.1, f32[3,256]{1,0:T(4,128)} %pos_ref.1, s32[64,256]{1,0:T(8,128)} %bitcast.4, s32[1,256]{1,0:T(1,128)} %bitcast.5, f32[3,16384]{1,0:T(4,128)} %wave_ref.1), custom_call_target="tpu_custom_call" | custom-call | tf_op jit(solution)/shard_map/pallas_call | solution.py:387
  2.5 4.9 %collective-permute-start = (bf16[128,384]{1,0:T(8,128)(2,1)S(1)}, bf16[128,384]{1,0:T(8,128)(2,1)S(1)}, u32[]{:S(2)}, u32[]{:S(2)}) collective-permute-start(bf16[128,384]{1,0:T(8,128)(2,1)S(1)} %get-tuple-element.20.last_ref), channel_id=1, source_target_pairs={{0,1},{1,2},{2,3},{3,4},{4,5},{5,6},{6,7},{7,8},{8,9},{9,10},{10,1... | collective-permute-start | bytes 294920 | tf_op jit(solution)/shard_map/ppermute | solution.py:369
  7.5 1.3 %collective-permute-start.1 = (bf16[128,384]{1,0:T(8,128)(2,1)S(1)}, bf16[128,384]{1,0:T(8,128)(2,1)S(1)}, u32[]{:S(2)}, u32[]{:S(2)}) collective-permute-start(bf16[128,384]{1,0:T(8,128)(2,1)S(1)} %get-tuple-element.21.first_ref), channel_id=1, source_target_pairs={{1,0},{2,1},{3,2},{4,3},{5,4},{6,5},{7,6},{8,7},{9,8},{10,9},{11,1... | collective-permute-start | bytes 294920 | tf_op jit(solution)/shard_map/ppermute | solution.py:369
  8.8 5.8 %shard_map.104 = (bf16[7168,256]{1,0:T(8,128)(2,1)S(1)}, bf16[7168,256]{1,0:T(8,128)(2,1)S(1)}, f32[8,16384]{1,0:T(8,128)S(1)}, f32[256,128]{1,0:T(8,128)S(1)}, ...) custom-call(f32[3,256]{1,0:T(4,128)S(1)} %get-tuple-element.22.pos_ref, ...), custom_call_target="tpu_custom_call" | custom-call | flops 73400320 | bytes 7340032 | tf_op jit(solution)/shard_map/pallas_call | solution.py:403
  14.6 0.0 collective-permute-done.before_ref
  14.6 0.7 %collective-permute-done.1.after_ref = bf16[128,384]{1,0:T(8,128)(2,1)S(1)} collective-permute-done((bf16[128,384]{1,0:T(8,128)(2,1)S(1)}, bf16[128,384]{1,0:T(8,128)(2,1)S(1)}, u32[]{:S(2)}, u32[]{:S(2)}) %collective-permute-start.1) | collective-permute-done | bytes 98336 | tf_op jit(solution)/shard_map/ppermute | solution.py:369
  15.2 9.1 %shard_map.105 = (bf16[256,256]{1,0:T(8,128)(2,1)}, f32[32,2,512]{2,1,0:T(2,128)S(1)}, bf16[9216,256]{1,0:T(8,128)(2,1)S(1)}, bf16[9216,256]{1,0:T(8,128)(2,1)S(1)}) custom-call(bf16[128,384]{1,0:T(8,128)(2,1)S(1)} %collective-permute-done.before_ref, bf16[128,384]{1,0:T(8,128)(2,1)S(1)} %get-tuple-element.21.first_ref, ...), custom_call_target="tpu_custom_call" | custom-call | tf_op jit(solution)/shard_map/pallas_call | solution.py:424
  24.4 13.6 %all_to_all.10.parts_ref = bf16[32,2,512]{2,1,0:T(2,128)(2,1)S(1)} all-to-all(bf16[32,2,512]{2,1,0:T(2,128)(2,1)S(1)} %convert_element_type.3), channel_id=1, replica_groups=mesh['brick'=8,'kvec'=4] {'brick','kvec'}, dimensions={0} | all-to-all | bytes 131072 | tf_op jit(solution)/shard_map/all_to_all | solution.py:446
  38.0 0.1 shard_map.106
  38.0 9.2 %all_to_all.11.sums_ref = bf16[32,2,512]{2,1,0:T(2,128)(2,1)S(1)} all-to-all(bf16[32,2,512]{2,1,0:T(2,128)(2,1)S(1)} %shard_map.106), channel_id=1, replica_groups=mesh['brick'=8,'kvec'=4] {'brick','kvec'}, dimensions={0} | all-to-all | bytes 131072 | tf_op jit(solution)/shard_map/all_to_all | solution.py:454
  47.2 2.9 %shard_map.107 = (f32[1,256]{1,0:T(1,128)}, f32[3,256]{1,0:T(4,128)}) custom-call(bf16[32,2,512]{2,1,0:T(2,128)(2,1)S(1)} %all_to_all.11.sums_ref, f32[8,16384]{1,0:T(8,128)S(1)} %get-tuple-element.32.coef_ref, bf16[7168,256]{1,0:T(8,128)(2,1)S(1)} %get-tuple-element.28.cos_head_ref, bf16[7168,256]{1,0:T(8,128)(2,1)S(1)} %get-tuple-element.29.sin_head_ref, ...), custom_call_target="tpu_custom_call" | custom-call | tf_op jit(solution)/shard_map/pallas_call | solution.py:460
  (1 shorter events, 0.0 us)
Async XLA Ops:
  2.5 12.0 %collective-permute-start = (bf16[128,384]{1,0:T(8,128)(2,1)S(1)}, bf16[128,384]{1,0:T(8,128)(2,1)S(1)}, u32[]{:S(2)}, u32[]{:S(2)}) collective-permute-start(bf16[128,384]{1,0:T(8,128)(2,1)S(1)} %get-tuple-element.20.last_ref), channel_id=1, source_target_pairs={{0,1},{1,2},{2,3},{3,4},{4,5},{5,6},{6,7},{7,8},{8,9},{9,10},{10,1... | collective-permute-start | bytes 294920 | tf_op jit(solution)/shard_map/ppermute | solution.py:369
  7.5 7.8 %collective-permute-start.1 = (bf16[128,384]{1,0:T(8,128)(2,1)S(1)}, bf16[128,384]{1,0:T(8,128)(2,1)S(1)}, u32[]{:S(2)}, u32[]{:S(2)}) collective-permute-start(bf16[128,384]{1,0:T(8,128)(2,1)S(1)} %get-tuple-element.21.first_ref), channel_id=1, source_target_pairs={{1,0},{2,1},{3,2},{4,3},{5,4},{6,5},{7,6},{8,7},{9,8},{10,9},{11,1... | collective-permute-start | bytes 294920 | tf_op jit(solution)/shard_map/ppermute | solution.py:369

commit v14 on v13

--- a/solution.py
+++ b/solution.py
@@ -27,27 +27,38 @@
 
 
 def pack_kernel(
-    feat_ref, pos_ref, neigh_ref, counts_ref, wave_ref, first_ref, last_ref, waves_ref,
-    held_ref, sem,
+    feat_ref, pos_ref, neigh_ref, counts_ref, first_ref, last_ref, held_ref, slots_ref, used_ref,
+    sems,
 ):
     slots, own = neigh_ref.shape
     channels = feat_ref.shape[1]
-    copy = pltpu.make_async_copy(wave_ref, waves_ref, sem)
-    copy.start()
-    held_ref[...] = pos_ref[...]
+    half = own // 2
+    copies = [
+        pltpu.make_async_copy(source, target, sems.at[n])
+        for n, (source, target) in enumerate(
+            (
+                (neigh_ref, slots_ref),
+                (pos_ref, held_ref),
+                (counts_ref, used_ref),
+                (feat_ref.at[:half, :], first_ref.at[:, :channels]),
+                (feat_ref.at[half:, :], last_ref.at[:, :channels]),
+            )
+        )
+    ]
+    for copy in copies:
+        copy.start()
     rows = lax.broadcasted_iota(jnp.int32, (slots, own), 1)
     slot = lax.broadcasted_iota(jnp.int32, (slots, own), 0)
-    delta = (neigh_ref[...] - HALO - rows).astype(F32)
-    delta = jnp.where(slot < counts_ref[...], delta, 0.0)
+    for copy in copies:
+        copy.wait()
+    delta = (slots_ref[...] - HALO - rows).astype(F32)
+    delta = jnp.where(slot < used_ref[...], delta, 0.0)
     zero5 = jnp.zeros((5, own), F32)
-    coords = [jnp.concatenate([p, zero5], axis=0) for p in pieces(pos_ref[...])]
+    coords = [jnp.concatenate([p, zero5], axis=0) for p in pieces(held_ref[...])]
     rest = jnp.zeros((LANES - slots - 24, own), F32)
     extra = jnp.concatenate([delta] + coords + [rest], axis=0).astype(BF16)
-    half = own // 2
-    for ref, start in ((first_ref, 0), (last_ref, half)):
-        ref[:, :channels] = feat_ref[start : start + half, :]
-        ref[:, channels:] = extra[:, start : start + half]
-    copy.wait()
+    first_ref[:, channels:] = extra[:, :half]
+    last_ref[:, channels:] = extra[:, half:]
 
 
 HALF_SINE = (4.438831262995637, -7.228964613368321, 3.149392241482131)
@@ -122,14 +133,19 @@
 
 
 def early_kernel(
-    pos_ref, wave_ref, first_ref, last_ref, w_in_ref, w_out_ref, w_charge_ref, cos_ref, sin_ref,
-    coef_ref, hist_ref, w_in_out, w_out_out, w_charge_out, left_ref, even_ref, odd_ref, sems,
+    pos_ref, source_ref, first_ref, last_ref, w_in_ref, w_out_ref, w_charge_ref, cos_ref, sin_ref,
+    coef_ref, hist_ref, wave_ref, w_in_out, w_out_out, w_charge_out, left_ref, even_ref, odd_ref, sems,
     *, tile, chunk, factor,
 ):
     copies = [
         pltpu.make_async_copy(source, target, sems.at[n])
         for n, (source, target) in enumerate(
-            ((w_in_ref, w_in_out), (w_out_ref, w_out_out), (w_charge_ref, w_charge_out))
+            (
+                (source_ref, wave_ref),
+                (w_in_ref, w_in_out),
+                (w_out_ref, w_out_out),
+                (w_charge_ref, w_charge_out),
+            )
         )
     ]
     for copy in copies:
@@ -157,6 +173,7 @@
     def turn(step, out_ref):
         phase(wave_ref[:, place(step, tile)], left_ref, out_ref)
 
+    copies[0].wait()
     scale(0)
     turn(0, even_ref)
 
@@ -170,7 +187,7 @@
             turn(jnp.minimum(base + step + 2, head - 1), even_ref)
             evaluate(odd_ref, [into_table(cos_ref, sin_ref, base + step + 1, tile, chunk)], chunk)
 
-    for copy in copies:
+    for copy in copies[1:]:
         copy.wait()
 
 
@@ -182,7 +199,7 @@
     before_ref, first_ref, last_ref, after_ref, w_in_ref, w_out_ref, w_charge_ref, hist_ref,
     pos_ref, wave_ref, cos_head_ref, sin_head_ref, hidden_ref, sums_ref, cos_ref, sin_ref,
     feat_ref, mid_ref, matrix_ref, left_ref, charge_ref, even_ref, odd_ref, even_tile_ref,
-    odd_tile_ref, *, tile, chunk,
+    odd_tile_ref, final_ref, sem, *, tile, chunk,
 ):
     parts = (before_ref, first_ref, last_ref, after_ref)
     half = before_ref.shape[0]
@@ -265,7 +282,9 @@
     )
     mid_ref[grown:, :] = jnp.zeros((HALO, channels), BF16)
     final = advance(mid_ref, 1, range(1, blocks - 1), 1, mid_ref[HALO : HALO + own, :])
-    hidden_ref[...] = final
+    final_ref[...] = final
+    leave = pltpu.make_async_copy(final_ref, hidden_ref, sem)
+    leave.start()
     reader = jnp.concatenate(
         list(pieces(w_charge_ref[...])) + [jnp.zeros((5, channels), F32)], axis=0
     ).astype(BF16)
@@ -323,6 +342,7 @@
     rows = place(filled - 1, tile)
     added(head + filled - 1, cos_ref[rows, :], sin_ref[rows, :], 1)
     added(head + late - 1, odd_tile_ref[0], odd_tile_ref[1], 1)
+    leave.wait()
 
 
 def sum_kernel(parts_ref, out_ref):
@@ -379,18 +399,21 @@
     factor = 4.0 / math.sqrt(own * devices * total)
     dma = pltpu.SemaphoreType.DMA
     w_charge = w_charge.reshape(1, channels)
-    wave, w_in, w_out, w_charge = (
-        pltpu.with_memory_space_constraint(x, pltpu.HBM) for x in (wave, w_in, w_out, w_charge)
-    )
+    in_hbm = functools.partial(pltpu.with_memory_space_constraint, memory_space=pltpu.HBM)
+    wave, w_in, w_out, w_charge = (in_hbm(x) for x in (wave, w_in, w_out, w_charge))
 
     edge = pltpu.VMEM((half, width), BF16)
-    first, last, waves, held = pl.pallas_call(
+    first, last, held = pl.pallas_call(
         pack_kernel,
-        out_shape=(edge, edge, pltpu.VMEM(wave.shape, F32), pltpu.VMEM(positions.shape, F32)),
-        in_specs=[VMEM] * 4 + [HBM],
-        out_specs=(VMEM,) * 4,
-        scratch_shapes=[dma],
-    )(features, positions, neighbours.T, counts.reshape(1, own), wave)
+        out_shape=(edge, edge, pltpu.VMEM(positions.shape, F32)),
+        in_specs=[HBM] * 4,
+        out_specs=(VMEM,) * 3,
+        scratch_shapes=[
+            pltpu.VMEM(neighbours.shape[::-1], jnp.int32),
+            pltpu.VMEM((1, own), jnp.int32),
+            dma((5,)),
+        ],
+    )(*(in_hbm(x) for x in (features, positions, neighbours.T, counts.reshape(1, own))))
     before = shifted(last, 1)
     after = shifted(first, -1)
 
@@ -400,25 +423,26 @@
     table = pltpu.VMEM((early, own), BF16)
     phases = [pltpu.VMEM((tile, own), F32)] * 2
     grant = pltpu.CompilerParams(vmem_limit_bytes=16 << 20)
-    cos_head, sin_head, coef, hist, w_first, w_second, w_read = pl.pallas_call(
+    cos_head, sin_head, coef, hist, waves, w_first, w_second, w_read = pl.pallas_call(
         functools.partial(early_kernel, tile=tile, chunk=chunk, factor=factor),
         out_shape=(
             table,
             table,
             pltpu.VMEM((8, total), F32),
             pltpu.VMEM((own, LANES), F32),
+            pltpu.VMEM(wave.shape, F32),
             kept,
             kept,
             pltpu.VMEM((1, channels), F32),
         ),
-        in_specs=[VMEM] * 4 + [HBM] * 3,
-        out_specs=(VMEM,) * 7,
-        scratch_shapes=[pltpu.VMEM((32, own), BF16)] + phases + [dma((3,))],
+        in_specs=[VMEM, HBM, VMEM, VMEM] + [HBM] * 3,
+        out_specs=(VMEM,) * 8,
+        scratch_shapes=[pltpu.VMEM((32, own), BF16)] + phases + [dma((4,))],
         compiler_params=grant,
         cost_estimate=pl.CostEstimate(
             flops=own * early * 40, bytes_accessed=4 * own * early, transcendentals=0
         ),
-    )(held, waves, first, last, w_in, w_out, w_charge)
+    )(held, wave, first, last, w_in, w_out, w_charge)
 
     table = pltpu.VMEM((total - early, own), BF16)
     hidden, partial, cos_late, sin_late = pl.pallas_call(
@@ -430,7 +454,7 @@
             table,
         ),
         in_specs=[VMEM] * 12,
-        out_specs=(VMEM,) * 4,
+        out_specs=(HBM,) + (VMEM,) * 3,
         scratch_shapes=[
             pltpu.VMEM((4 * half + HALO, channels), BF16),
             pltpu.VMEM((own + 3 * HALO, channels), BF16),
@@ -439,7 +463,8 @@
             pltpu.VMEM((8, own), BF16),
         ]
         + phases
-        + [pltpu.VMEM((2, tile, own), BF16)] * 2,
+        + [pltpu.VMEM((2, tile, own), BF16)] * 2
+        + [pltpu.VMEM((own, channels), BF16), dma],
         compiler_params=grant,
     )(before, first, last, after, w_first, w_second, w_read, hist, held, waves, cos_head, sin_head)
 

time: 50.4 us -> 49.7 us (0.986)
  Pallas kernels: 19.8 us -> 19.1 us
  waiting for transfers between devices: 0.67 us -> 0.07 us
  blocking collectives: 22.8 us -> 23.4 us
    pallas_call x1, Pallas kernels: 1.88 us -> 1 us  [per_device(): pl.pallas_call(pack_kernel, out_shape=(edge, edge, pltpu.VMEM(positions.s...]
    ppermute x2, waiting for transfers between devices: 0.67 us -> 0.07 us  [shifted(): return lax.ppermute(x, AXES, pairs)]
    pallas_call x1, Pallas kernels: 5.78 us -> 6.38 us  [per_device(): pl.pallas_call(functools.partial(early_kernel, tile=tile, chunk=chunk, fa...]
    all_to_all x1, blocking collectives: 13.6 us -> 14.2 us  [per_device(): swapped = lax.all_to_all(partial.astype(BF16), AXES, 0, 0, tiled=True)]
  transfers between devices with their start and end apart: 2 -> 2, of which waited for: 1 -> 1; matrix products, arithmetic and copies ran while one was open for 0% -> 0% of each run, Pallas kernels for 12% -> 13%
where the time goes in v14:
time: 49.7 us; the launch traced here: 49.5 us
  blocking collectives  23.4 us (47%)
  Pallas kernels  19.1 us (38%)
  starting transfers between devices  6.23 us (13%)
  between operations  0.69 us (1%)
    all_to_all x1, blocking collectives, per_device(): swapped = lax.all_to_all(partial.astype(BF16), AXES, 0, 0, tiled=True)  14.2 us
    all_to_all x1, blocking collectives, per_device(): sums = lax.all_to_all(spread, AXES, 0, 0, tiled=True)  9.19 us
    pallas_call x1, Pallas kernels, per_device(): pl.pallas_call(functools.partial(layer_kernel, tile=tile, chunk=chunk), o...  8.71 us
    pallas_call x1, Pallas kernels, per_device(): pl.pallas_call(functools.partial(early_kernel, tile=tile, chunk=chunk, fa...  6.38 us
    ppermute x2, starting transfers between devices, shifted(): return lax.ppermute(x, AXES, pairs)  6.23 us
    pallas_call x1, Pallas kernels, per_device(): pl.pallas_call(functools.partial(response_kernel, tile=1024), out_shape=(...  2.9 us
    pallas_call x1, Pallas kernels, per_device(): pl.pallas_call(pack_kernel, out_shape=(edge, edge, pltpu.VMEM(positions.s...  1 us
  transfers between devices with their start and end apart: 2, of which 1 were waited for; matrix products, arithmetic and copies ran while one was open for 0% of the time, Pallas kernels for 13%

profile of v14, /device:TPU:0, one launch (start us, length us, event | category | flops | bytes accessed | tf_op | source)
XLA Modules:
  0.0 49.5 jit_solution(3030370792218901780)
XLA Ops:
  0.6 1.0 %shard_map.103 = (bf16[128,384]{1,0:T(8,128)(2,1)S(1)}, bf16[128,384]{1,0:T(8,128)(2,1)S(1)}, f32[3,256]{1,0:T(4,128)S(1)}) custom-call(bf16[256,256]{1,0:T(8,128)(2,1)} %feat_ref.1, f32[3,256]{1,0:T(4,128)} %pos_ref.1, s32[64,256]{1,0:T(8,128)} %bitcast.4, s32[1,256]{1,0:T(1,128)} %bitcast.5), custom_call_target="tpu_custom_call" | custom-call | tf_op jit(solution)/shard_map/pallas_call | solution.py:406
  1.6 4.9 %collective-permute-start = (bf16[128,384]{1,0:T(8,128)(2,1)S(1)}, bf16[128,384]{1,0:T(8,128)(2,1)S(1)}, u32[]{:S(2)}, u32[]{:S(2)}) collective-permute-start(bf16[128,384]{1,0:T(8,128)(2,1)S(1)} %get-tuple-element.20.last_ref), channel_id=1, source_target_pairs={{0,1},{1,2},{2,3},{3,4},{4,5},{5,6},{6,7},{7,8},{8,9},{9,10},{10,1... | collective-permute-start | bytes 294920 | tf_op jit(solution)/shard_map/ppermute | solution.py:389
  6.6 1.3 %collective-permute-start.1 = (bf16[128,384]{1,0:T(8,128)(2,1)S(1)}, bf16[128,384]{1,0:T(8,128)(2,1)S(1)}, u32[]{:S(2)}, u32[]{:S(2)}) collective-permute-start(bf16[128,384]{1,0:T(8,128)(2,1)S(1)} %get-tuple-element.21.first_ref), channel_id=1, source_target_pairs={{1,0},{2,1},{3,2},{4,3},{5,4},{6,5},{7,6},{8,7},{9,8},{10,9},{11,1... | collective-permute-start | bytes 294920 | tf_op jit(solution)/shard_map/ppermute | solution.py:389
  7.9 6.4 %shard_map.104 = (bf16[7168,256]{1,0:T(8,128)(2,1)S(1)}, bf16[7168,256]{1,0:T(8,128)(2,1)S(1)}, f32[8,16384]{1,0:T(8,128)S(1)}, f32[256,128]{1,0:T(8,128)S(1)}, ...) custom-call(f32[3,256]{1,0:T(4,128)S(1)} %get-tuple-element.22.pos_r, ...), custom_call_target="tpu_custom_call" | custom-call | flops 73400320 | bytes 7340032 | tf_op jit(solution)/shard_map/pallas_call | solution.py:426
  14.3 0.0 collective-permute-done.before_ref
  14.3 0.1 collective-permute-done.1.after_ref
  14.3 8.7 %shard_map.105 = (bf16[256,256]{1,0:T(8,128)(2,1)}, f32[32,2,512]{2,1,0:T(2,128)S(1)}, bf16[9216,256]{1,0:T(8,128)(2,1)S(1)}, bf16[9216,256]{1,0:T(8,128)(2,1)S(1)}) custom-call(bf16[128,384]{1,0:T(8,128)(2,1)S(1)} %collective-permute-done.before_ref, bf16[128,384]{1,0:T(8,128)(2,1)S(1)} %get-tuple-element.21.first_ref, ...), custom_call_target="tpu_custom_call" | custom-call | tf_op jit(solution)/shard_map/pallas_call | solution.py:448
  23.1 14.2 %all_to_all.10.parts_ref = bf16[32,2,512]{2,1,0:T(2,128)(2,1)S(1)} all-to-all(bf16[32,2,512]{2,1,0:T(2,128)(2,1)S(1)} %convert_element_type.3), channel_id=1, replica_groups=mesh['brick'=8,'kvec'=4] {'brick','kvec'}, dimensions={0} | all-to-all | bytes 131072 | tf_op jit(solution)/shard_map/all_to_all | solution.py:471
  37.3 0.1 shard_map.106
  37.4 9.2 %all_to_all.11.sums_ref = bf16[32,2,512]{2,1,0:T(2,128)(2,1)S(1)} all-to-all(bf16[32,2,512]{2,1,0:T(2,128)(2,1)S(1)} %shard_map.106), channel_id=1, replica_groups=mesh['brick'=8,'kvec'=4] {'brick','kvec'}, dimensions={0} | all-to-all | bytes 131072 | tf_op jit(solution)/shard_map/all_to_all | solution.py:479
  46.6 2.9 %shard_map.107 = (f32[1,256]{1,0:T(1,128)}, f32[3,256]{1,0:T(4,128)}) custom-call(bf16[32,2,512]{2,1,0:T(2,128)(2,1)S(1)} %all_to_all.11.sums_ref, f32[8,16384]{1,0:T(8,128)S(1)} %get-tuple-element.32.coef_ref, bf16[7168,256]{1,0:T(8,128)(2,1)S(1)} %get-tuple-element.28.cos_head_ref, bf16[7168,256]{1,0:T(8,128)(2,1)S(1)} %get-tuple-element.29.sin_head_ref, ...), custom_call_target="tpu_custom_call" | custom-call | tf_op jit(solution)/shard_map/pallas_call | solution.py:485
  (1 shorter events, 0.0 us)
Async XLA Ops:
  1.6 12.6 %collective-permute-start = (bf16[128,384]{1,0:T(8,128)(2,1)S(1)}, bf16[128,384]{1,0:T(8,128)(2,1)S(1)}, u32[]{:S(2)}, u32[]{:S(2)}) collective-permute-start(bf16[128,384]{1,0:T(8,128)(2,1)S(1)} %get-tuple-element.20.last_ref), channel_id=1, source_target_pairs={{0,1},{1,2},{2,3},{3,4},{4,5},{5,6},{6,7},{7,8},{8,9},{9,10},{10,1... | collective-permute-start | bytes 294920 | tf_op jit(solution)/shard_map/ppermute | solution.py:389
  6.6 7.8 %collective-permute-start.1 = (bf16[128,384]{1,0:T(8,128)(2,1)S(1)}, bf16[128,384]{1,0:T(8,128)(2,1)S(1)}, u32[]{:S(2)}, u32[]{:S(2)}) collective-permute-start(bf16[128,384]{1,0:T(8,128)(2,1)S(1)} %get-tuple-element.21.first_ref), channel_id=1, source_target_pairs={{1,0},{2,1},{3,2},{4,3},{5,4},{6,5},{7,6},{8,7},{9,8},{10,9},{11,1... | collective-permute-start | bytes 294920 | tf_op jit(solution)/shard_map/ppermute | solution.py:389

commit v15 on v14

--- a/solution.py
+++ b/solution.py
@@ -26,9 +26,18 @@
     return first, second, rest - second
 
 
+def even_device():
+    index = lax.axis_index("brick") * lax.axis_size("kvec") + lax.axis_index("kvec")
+    return index % 2 == 0
+
+
+def chosen(even, one, other):
+    return jnp.where(even, one.astype(F32), other.astype(F32)).astype(BF16)
+
+
 def pack_kernel(
-    feat_ref, pos_ref, neigh_ref, counts_ref, first_ref, last_ref, held_ref, slots_ref, used_ref,
-    sems,
+    feat_ref, pos_ref, neigh_ref, counts_ref, wave_ref, first_ref, last_ref, near_ref, far_ref,
+    held_ref, waves_ref, slots_ref, used_ref, sems,
 ):
     slots, own = neigh_ref.shape
     channels = feat_ref.shape[1]
@@ -42,6 +51,7 @@
                 (counts_ref, used_ref),
                 (feat_ref.at[:half, :], first_ref.at[:, :channels]),
                 (feat_ref.at[half:, :], last_ref.at[:, :channels]),
+                (wave_ref, waves_ref),
             )
         )
     ]
@@ -49,7 +59,7 @@
         copy.start()
     rows = lax.broadcasted_iota(jnp.int32, (slots, own), 1)
     slot = lax.broadcasted_iota(jnp.int32, (slots, own), 0)
-    for copy in copies:
+    for copy in copies[:-1]:
         copy.wait()
     delta = (slots_ref[...] - HALO - rows).astype(F32)
     delta = jnp.where(slot < used_ref[...], delta, 0.0)
@@ -59,6 +69,10 @@
     extra = jnp.concatenate([delta] + coords + [rest], axis=0).astype(BF16)
     first_ref[:, channels:] = extra[:, :half]
     last_ref[:, channels:] = extra[:, half:]
+    even = even_device()
+    near_ref[...] = chosen(even, last_ref[...], first_ref[...])
+    far_ref[...] = chosen(even, first_ref[...], last_ref[...])
+    copies[-1].wait()
 
 
 HALF_SINE = (4.438831262995637, -7.228964613368321, 3.149392241482131)
@@ -133,15 +147,14 @@
 
 
 def early_kernel(
-    pos_ref, source_ref, first_ref, last_ref, w_in_ref, w_out_ref, w_charge_ref, cos_ref, sin_ref,
-    coef_ref, hist_ref, wave_ref, w_in_out, w_out_out, w_charge_out, left_ref, even_ref, odd_ref, sems,
+    pos_ref, wave_ref, first_ref, last_ref, w_in_ref, w_out_ref, w_charge_ref, cos_ref, sin_ref,
+    coef_ref, hist_ref, w_in_out, w_out_out, w_charge_out, left_ref, even_ref, odd_ref, sems,
     *, tile, chunk, factor,
 ):
     copies = [
         pltpu.make_async_copy(source, target, sems.at[n])
         for n, (source, target) in enumerate(
             (
-                (source_ref, wave_ref),
                 (w_in_ref, w_in_out),
                 (w_out_ref, w_out_out),
                 (w_charge_ref, w_charge_out),
@@ -173,7 +186,6 @@
     def turn(step, out_ref):
         phase(wave_ref[:, place(step, tile)], left_ref, out_ref)
 
-    copies[0].wait()
     scale(0)
     turn(0, even_ref)
 
@@ -187,7 +199,7 @@
             turn(jnp.minimum(base + step + 2, head - 1), even_ref)
             evaluate(odd_ref, [into_table(cos_ref, sin_ref, base + step + 1, tile, chunk)], chunk)
 
-    for copy in copies[1:]:
+    for copy in copies:
         copy.wait()
 
 
@@ -196,11 +208,14 @@
 
 
 def layer_kernel(
-    before_ref, first_ref, last_ref, after_ref, w_in_ref, w_out_ref, w_charge_ref, hist_ref,
+    near_ref, first_ref, last_ref, far_ref, w_in_ref, w_out_ref, w_charge_ref, hist_ref,
     pos_ref, wave_ref, cos_head_ref, sin_head_ref, hidden_ref, sums_ref, cos_ref, sin_ref,
     feat_ref, mid_ref, matrix_ref, left_ref, charge_ref, even_ref, odd_ref, even_tile_ref,
-    odd_tile_ref, final_ref, sem, *, tile, chunk,
+    odd_tile_ref, final_ref, before_ref, after_ref, sem, *, tile, chunk,
 ):
+    even = even_device()
+    before_ref[...] = chosen(even, far_ref[...], near_ref[...])
+    after_ref[...] = chosen(even, near_ref[...], far_ref[...])
     parts = (before_ref, first_ref, last_ref, after_ref)
     half = before_ref.shape[0]
     channels = w_in_ref.shape[1]
@@ -383,10 +398,10 @@
     field_ref[...] = result[1:4]
 
 
-def shifted(x, step):
+def exchanged(x, start):
     devices = lax.axis_size(AXES)
-    pairs = [(i, i + step) for i in range(devices) if 0 <= i + step < devices]
-    return lax.ppermute(x, AXES, pairs)
+    pairs = [(i, i + 1) for i in range(start, devices - 1, 2)]
+    return lax.ppermute(x, AXES, pairs + [(j, i) for i, j in pairs])
 
 
 def per_device(features, positions, neighbours, counts, w_in, w_out, w_charge, wave):
@@ -403,19 +418,20 @@
     wave, w_in, w_out, w_charge = (in_hbm(x) for x in (wave, w_in, w_out, w_charge))
 
     edge = pltpu.VMEM((half, width), BF16)
-    first, last, held = pl.pallas_call(
+    first, last, near, far, held, waves = pl.pallas_call(
         pack_kernel,
-        out_shape=(edge, edge, pltpu.VMEM(positions.shape, F32)),
-        in_specs=[HBM] * 4,
-        out_specs=(VMEM,) * 3,
+        out_shape=(edge,) * 4
+        + (pltpu.VMEM(positions.shape, F32), pltpu.VMEM(wave.shape, F32)),
+        in_specs=[HBM] * 5,
+        out_specs=(VMEM,) * 6,
         scratch_shapes=[
             pltpu.VMEM(neighbours.shape[::-1], jnp.int32),
             pltpu.VMEM((1, own), jnp.int32),
-            dma((5,)),
+            dma((6,)),
         ],
-    )(*(in_hbm(x) for x in (features, positions, neighbours.T, counts.reshape(1, own))))
-    before = shifted(last, 1)
-    after = shifted(first, -1)
+    )(*(in_hbm(x) for x in (features, positions, neighbours.T, counts.reshape(1, own))), wave)
+    near = exchanged(near, 0)
+    far = exchanged(far, 1)
 
     tile, chunk = 256, 32
     early = (total - 8 * tile) // 2
@@ -423,26 +439,25 @@
     table = pltpu.VMEM((early, own), BF16)
     phases = [pltpu.VMEM((tile, own), F32)] * 2
     grant = pltpu.CompilerParams(vmem_limit_bytes=16 << 20)
-    cos_head, sin_head, coef, hist, waves, w_first, w_second, w_read = pl.pallas_call(
+    cos_head, sin_head, coef, hist, w_first, w_second, w_read = pl.pallas_call(
         functools.partial(early_kernel, tile=tile, chunk=chunk, factor=factor),
         out_shape=(
             table,
             table,
             pltpu.VMEM((8, total), F32),
             pltpu.VMEM((own, LANES), F32),
-            pltpu.VMEM(wave.shape, F32),
             kept,
             kept,
             pltpu.VMEM((1, channels), F32),
         ),
-        in_specs=[VMEM, HBM, VMEM, VMEM] + [HBM] * 3,
-        out_specs=(VMEM,) * 8,
-        scratch_shapes=[pltpu.VMEM((32, own), BF16)] + phases + [dma((4,))],
+        in_specs=[VMEM] * 4 + [HBM] * 3,
+        out_specs=(VMEM,) * 7,
+        scratch_shapes=[pltpu.VMEM((32, own), BF16)] + phases + [dma((3,))],
         compiler_params=grant,
         cost_estimate=pl.CostEstimate(
             flops=own * early * 40, bytes_accessed=4 * own * early, transcendentals=0
         ),
-    )(held, wave, first, last, w_in, w_out, w_charge)
+    )(held, waves, first, last, w_in, w_out, w_charge)
 
     table = pltpu.VMEM((total - early, own), BF16)
     hidden, partial, cos_late, sin_late = pl.pallas_call(
@@ -464,9 +479,11 @@
         ]
         + phases
         + [pltpu.VMEM((2, tile, own), BF16)] * 2
-        + [pltpu.VMEM((own, channels), BF16), dma],
+        + [pltpu.VMEM((own, channels), BF16)]
+        + [pltpu.VMEM((half, width), BF16)] * 2
+        + [dma],
         compiler_params=grant,
-    )(before, first, last, after, w_first, w_second, w_read, hist, held, waves, cos_head, sin_head)
+    )(near, first, last, far, w_first, w_second, w_read, hist, held, waves, cos_head, sin_head)
 
     swapped = lax.all_to_all(partial.astype(BF16), AXES, 0, 0, tiled=True)
     spread = pl.pallas_call(

time: 49.7 us -> 46.9 us (0.944)
  starting transfers between devices: 6.23 us -> 3.74 us
    ppermute x2, starting transfers between devices: 6.23 us -> 3.74 us  [exchanged(): return lax.ppermute(x, AXES, pairs + [(j, i) for i, j in pairs])]
    pallas_call x1, Pallas kernels: 6.38 us -> 5.78 us  [per_device(): pl.pallas_call(functools.partial(early_kernel, tile=tile, chunk=chunk, fa...]
  transfers between devices with their start and end apart: 2 -> 2, of which waited for: 1 -> 0; matrix products, arithmetic and copies ran while one was open for 0% -> 0% of each run, Pallas kernels for 13% -> 12%
where the time goes in v15:
time: 46.9 us; the launch traced here: 46.7 us
  blocking collectives  23.5 us (50%)
  Pallas kernels  18.7 us (40%)
  starting transfers between devices  3.74 us (8%)
  between operations  0.69 us (1%)
    all_to_all x1, blocking collectives, per_device(): swapped = lax.all_to_all(partial.astype(BF16), AXES, 0, 0, tiled=True)  14.3 us
    all_to_all x1, blocking collectives, per_device(): sums = lax.all_to_all(spread, AXES, 0, 0, tiled=True)  9.19 us
    pallas_call x1, Pallas kernels, per_device(): pl.pallas_call(functools.partial(layer_kernel, tile=tile, chunk=chunk), o...  8.77 us
    pallas_call x1, Pallas kernels, per_device(): pl.pallas_call(functools.partial(early_kernel, tile=tile, chunk=chunk, fa...  5.78 us
    ppermute x2, starting transfers between devices, exchanged(): return lax.ppermute(x, AXES, pairs + [(j, i) for i, j in pairs])  3.74 us
    pallas_call x1, Pallas kernels, per_device(): pl.pallas_call(functools.partial(response_kernel, tile=1024), out_shape=(...  2.9 us
    pallas_call x1, Pallas kernels, per_device(): pl.pallas_call(pack_kernel, out_shape=(edge,) * 4 + (pltpu.VMEM(positions...  1.14 us
  transfers between devices with their start and end apart: 2, of which 0 were waited for; matrix products, arithmetic and copies ran while one was open for 0% of the time, Pallas kernels for 12%

profile of v15, /device:TPU:0, one launch (start us, length us, event | category | flops | bytes accessed | tf_op | source)
XLA Modules:
  0.0 46.7 jit_solution(10731562713412272690)
XLA Ops:
  0.6 1.1 %shard_map.103 = (bf16[128,384]{1,0:T(8,128)(2,1)S(1)}, bf16[128,384]{1,0:T(8,128)(2,1)S(1)}, bf16[128,384]{1,0:T(8,128)(2,1)S(1)}, bf16[128,384]{1,0:T(8,128)(2...) custom-call(bf16[256,256]{1,0:T(8,128)(2,1)} %feat_ref.1, f32[3,256]{1,0:T(4,128)} %pos_ref.1, s32[64,256]{1,0:T(8,128)} %bitcast.4, ...), custom_call_target="tpu_custom_call" | custom-call | tf_op jit(solution)/shard_map/pallas_call | solution.py:421
  1.8 3.1 %collective-permute-start = (bf16[128,384]{1,0:T(8,128)(2,1)S(1)}, bf16[128,384]{1,0:T(8,128)(2,1)S(1)}, u32[]{:S(2)}, u32[]{:S(2)}) collective-permute-start(bf16[128,384]{1,0:T(8,128)(2,1)S(1)} %get-tuple-element.22), channel_id=1, source_target_pairs={{0,1},{2,3},{4,5},{6,7},{8,9},{10,11},{12,13},{14,15},{16,17},{18,... | collective-permute-start | bytes 294920 | tf_op jit(solution)/shard_map/ppermute | solution.py:404
  4.9 0.7 %collective-permute-start.1 = (bf16[128,384]{1,0:T(8,128)(2,1)S(1)}, bf16[128,384]{1,0:T(8,128)(2,1)S(1)}, u32[]{:S(2)}, u32[]{:S(2)}) collective-permute-start(bf16[128,384]{1,0:T(8,128)(2,1)S(1)} %get-tuple-element.25), channel_id=1, source_target_pairs={{1,2},{3,4},{5,6},{7,8},{9,10},{11,12},{13,14},{15,16},{17,18},{19... | collective-permute-start | bytes 294920 | tf_op jit(solution)/shard_map/ppermute | solution.py:404
  5.5 5.8 %shard_map.104 = (bf16[7168,256]{1,0:T(8,128)(2,1)S(1)}, bf16[7168,256]{1,0:T(8,128)(2,1)S(1)}, f32[8,16384]{1,0:T(8,128)S(1)}, f32[256,128]{1,0:T(8,128)S(1)}, ...) custom-call(f32[3,256]{1,0:T(4,128)S(1)} %get-tuple-element.26.pos_ref, ...), custom_call_target="tpu_custom_call" | custom-call | flops 73400320 | bytes 7340032 | tf_op jit(solution)/shard_map/pallas_call | solution.py:442
  11.3 0.0 collective-permute-done.near_ref
  11.3 0.0 collective-permute-done.1.far_ref
  11.3 8.8 %shard_map.105 = (bf16[256,256]{1,0:T(8,128)(2,1)}, f32[32,2,512]{2,1,0:T(2,128)S(1)}, bf16[9216,256]{1,0:T(8,128)(2,1)S(1)}, bf16[9216,256]{1,0:T(8,128)(2,1)S(1)}) custom-call(bf16[128,384]{1,0:T(8,128)(2,1)S(1)} %collective-permute-done.near_ref, bf16[128,384]{1,0:T(8,128)(2,1)S(1)} %get-tuple-element.23.first_ref, ...), custom_call_target="tpu_custom_call" | custom-call | tf_op jit(solution)/shard_map/pallas_call | solution.py:463
  20.2 14.3 %all_to_all.10.parts_ref = bf16[32,2,512]{2,1,0:T(2,128)(2,1)S(1)} all-to-all(bf16[32,2,512]{2,1,0:T(2,128)(2,1)S(1)} %convert_element_type.3), channel_id=1, replica_groups=mesh['brick'=8,'kvec'=4] {'brick','kvec'}, dimensions={0} | all-to-all | bytes 131072 | tf_op jit(solution)/shard_map/all_to_all | solution.py:488
  34.5 0.1 shard_map.106
  34.6 9.2 %all_to_all.11.sums_ref = bf16[32,2,512]{2,1,0:T(2,128)(2,1)S(1)} all-to-all(bf16[32,2,512]{2,1,0:T(2,128)(2,1)S(1)} %shard_map.106), channel_id=1, replica_groups=mesh['brick'=8,'kvec'=4] {'brick','kvec'}, dimensions={0} | all-to-all | bytes 131072 | tf_op jit(solution)/shard_map/all_to_all | solution.py:496
  43.8 2.9 %shard_map.107 = (f32[1,256]{1,0:T(1,128)}, f32[3,256]{1,0:T(4,128)}) custom-call(bf16[32,2,512]{2,1,0:T(2,128)(2,1)S(1)} %all_to_all.11.sums_ref, f32[8,16384]{1,0:T(8,128)S(1)} %get-tuple-element.36.coef_ref, bf16[7168,256]{1,0:T(8,128)(2,1)S(1)} %get-tuple-element.32.cos_head_ref, bf16[7168,256]{1,0:T(8,128)(2,1)S(1)} %get-tuple-element.33.sin_head_ref, ...), custom_call_target="tpu_custom_call" | custom-call | tf_op jit(solution)/shard_map/pallas_call | solution.py:502
  (1 shorter events, 0.0 us)
Async XLA Ops:
  1.8 9.5 %collective-permute-start = (bf16[128,384]{1,0:T(8,128)(2,1)S(1)}, bf16[128,384]{1,0:T(8,128)(2,1)S(1)}, u32[]{:S(2)}, u32[]{:S(2)}) collective-permute-start(bf16[128,384]{1,0:T(8,128)(2,1)S(1)} %get-tuple-element.22), channel_id=1, source_target_pairs={{0,1},{2,3},{4,5},{6,7},{8,9},{10,11},{12,13},{14,15},{16,17},{18,... | collective-permute-start | bytes 294920 | tf_op jit(solution)/shard_map/ppermute | solution.py:404
  4.9 6.5 %collective-permute-start.1 = (bf16[128,384]{1,0:T(8,128)(2,1)S(1)}, bf16[128,384]{1,0:T(8,128)(2,1)S(1)}, u32[]{:S(2)}, u32[]{:S(2)}) collective-permute-start(bf16[128,384]{1,0:T(8,128)(2,1)S(1)} %get-tuple-element.25), channel_id=1, source_target_pairs={{1,2},{3,4},{5,6},{7,8},{9,10},{11,12},{13,14},{15,16},{17,18},{19... | collective-permute-start | bytes 294920 | tf_op jit(solution)/shard_map/ppermute | solution.py:404

commit v16 on v15

--- a/solution.py
+++ b/solution.py
@@ -36,7 +36,7 @@
 
 
 def pack_kernel(
-    feat_ref, pos_ref, neigh_ref, counts_ref, wave_ref, first_ref, last_ref, near_ref, far_ref,
+    feat_ref, pos_ref, neigh_ref, counts_ref, wave_ref, first_ref, last_ref, near_ref,
     held_ref, waves_ref, slots_ref, used_ref, sems,
 ):
     slots, own = neigh_ref.shape
@@ -69,9 +69,7 @@
     extra = jnp.concatenate([delta] + coords + [rest], axis=0).astype(BF16)
     first_ref[:, channels:] = extra[:, :half]
     last_ref[:, channels:] = extra[:, half:]
-    even = even_device()
-    near_ref[...] = chosen(even, last_ref[...], first_ref[...])
-    far_ref[...] = chosen(even, first_ref[...], last_ref[...])
+    near_ref[...] = chosen(even_device(), last_ref[...], first_ref[...])
     copies[-1].wait()
 
 
@@ -146,28 +144,11 @@
     return hist.astype(F32).T
 
 
-def early_kernel(
-    pos_ref, wave_ref, first_ref, last_ref, w_in_ref, w_out_ref, w_charge_ref, cos_ref, sin_ref,
-    coef_ref, hist_ref, w_in_out, w_out_out, w_charge_out, left_ref, even_ref, odd_ref, sems,
-    *, tile, chunk, factor,
-):
-    copies = [
-        pltpu.make_async_copy(source, target, sems.at[n])
-        for n, (source, target) in enumerate(
-            (
-                (w_in_ref, w_in_out),
-                (w_out_ref, w_out_out),
-                (w_charge_ref, w_charge_out),
-            )
-        )
-    ]
-    for copy in copies:
-        copy.start()
-    left_ref[...] = atom_pieces(pos_ref)
-    channels = w_in_ref.shape[1]
+def prepare_kernel(wave_ref, first_ref, last_ref, far_ref, coef_ref, hist_ref, *, tile, factor):
+    channels = first_ref.shape[1] - LANES
+    far_ref[...] = chosen(even_device(), first_ref[...], last_ref[...])
     for n, ref in enumerate((first_ref, last_ref)):
         hist_ref[n * LANES : (n + 1) * LANES, :] = histogram(ref[:64, channels:].astype(F32))
-    head = cos_ref.shape[0] // tile
     group = 8
 
     def scale(step):
@@ -183,16 +164,39 @@
                 [one, w, one, w], axis=0
             )
 
+    @pl.loop(0, wave_ref.shape[1] // (2 * group * tile))
+    def _(block):
+        scale(2 * group * block)
+        scale(2 * group * block + group)
+
+
+def early_kernel(
+    pos_ref, wave_ref, w_in_ref, w_out_ref, w_charge_ref, cos_ref, sin_ref,
+    w_in_out, w_out_out, w_charge_out, left_ref, even_ref, odd_ref, sems,
+    *, tile, chunk,
+):
+    copies = [
+        pltpu.make_async_copy(source, target, sems.at[n])
+        for n, (source, target) in enumerate(
+            (
+                (w_in_ref, w_in_out),
+                (w_out_ref, w_out_out),
+                (w_charge_ref, w_charge_out),
+            )
+        )
+    ]
+    for copy in copies:
+        copy.start()
+    left_ref[...] = atom_pieces(pos_ref)
+    head = cos_ref.shape[0] // tile
     def turn(step, out_ref):
         phase(wave_ref[:, place(step, tile)], left_ref, out_ref)
 
-    scale(0)
     turn(0, even_ref)
 
     @pl.loop(0, head // 4)
     def _(block):
         base = 4 * block
-        scale(2 * base + group)
         for step in range(0, 4, 2):
             turn(base + step + 1, odd_ref)
             evaluate(even_ref, [into_table(cos_ref, sin_ref, base + step, tile, chunk)], chunk)
@@ -418,12 +422,12 @@
     wave, w_in, w_out, w_charge = (in_hbm(x) for x in (wave, w_in, w_out, w_charge))
 
     edge = pltpu.VMEM((half, width), BF16)
-    first, last, near, far, held, waves = pl.pallas_call(
+    first, last, near, held, waves = pl.pallas_call(
         pack_kernel,
-        out_shape=(edge,) * 4
+        out_shape=(edge,) * 3
         + (pltpu.VMEM(positions.shape, F32), pltpu.VMEM(wave.shape, F32)),
         in_specs=[HBM] * 5,
-        out_specs=(VMEM,) * 6,
+        out_specs=(VMEM,) * 5,
         scratch_shapes=[
             pltpu.VMEM(neighbours.shape[::-1], jnp.int32),
             pltpu.VMEM((1, own), jnp.int32),
@@ -431,6 +435,16 @@
         ],
     )(*(in_hbm(x) for x in (features, positions, neighbours.T, counts.reshape(1, own))), wave)
     near = exchanged(near, 0)
+    far, coef, hist = pl.pallas_call(
+        functools.partial(prepare_kernel, tile=256, factor=factor),
+        out_shape=(edge, pltpu.VMEM((8, total), F32), pltpu.VMEM((own, LANES), F32)),
+        in_specs=[VMEM] * 3,
+        out_specs=(VMEM,) * 3,
+        compiler_params=pltpu.CompilerParams(vmem_limit_bytes=4 << 20),
+        cost_estimate=pl.CostEstimate(
+            flops=own * total * 4, bytes_accessed=own * total, transcendentals=0
+        ),
+    )(waves, first, last)
     far = exchanged(far, 1)
 
     tile, chunk = 256, 32
@@ -439,25 +453,23 @@
     table = pltpu.VMEM((early, own), BF16)
     phases = [pltpu.VMEM((tile, own), F32)] * 2
     grant = pltpu.CompilerParams(vmem_limit_bytes=16 << 20)
-    cos_head, sin_head, coef, hist, w_first, w_second, w_read = pl.pallas_call(
-        functools.partial(early_kernel, tile=tile, chunk=chunk, factor=factor),
+    cos_head, sin_head, w_first, w_second, w_read = pl.pallas_call(
+        functools.partial(early_kernel, tile=tile, chunk=chunk),
         out_shape=(
             table,
             table,
-            pltpu.VMEM((8, total), F32),
-            pltpu.VMEM((own, LANES), F32),
             kept,
             kept,
             pltpu.VMEM((1, channels), F32),
         ),
-        in_specs=[VMEM] * 4 + [HBM] * 3,
-        out_specs=(VMEM,) * 7,
+        in_specs=[VMEM] * 2 + [HBM] * 3,
+        out_specs=(VMEM,) * 5,
         scratch_shapes=[pltpu.VMEM((32, own), BF16)] + phases + [dma((3,))],
         compiler_params=grant,
         cost_estimate=pl.CostEstimate(
             flops=own * early * 40, bytes_accessed=4 * own * early, transcendentals=0
         ),
-    )(held, waves, first, last, w_in, w_out, w_charge)
+    )(held, waves, w_in, w_out, w_charge)
 
     table = pltpu.VMEM((total - early, own), BF16)
     hidden, partial, cos_late, sin_late = pl.pallas_call(

time: 46.9 us -> 47.6 us (1.015)
    pallas_call x2 -> x3, Pallas kernels: 6.92 us -> 7.21 us  [the longest x1 5.27 us: per_device(): pl.pallas_call(functools.partial(early_kernel, tile=tile, chunk=chunk), o...]
  transfers between devices with their start and end apart: 2 -> 2, of which waited for: 0 -> 0; matrix products, arithmetic and copies ran while one was open for 0% -> 0% of each run, Pallas kernels for 12% -> 13%
where the time goes in v16:
time: 47.6 us; the launch traced here: 47.4 us
  blocking collectives  23.9 us (50%)
  Pallas kernels  19 us (40%)
  starting transfers between devices  3.76 us (8%)
  between operations  0.7 us (1%)
    all_to_all x1, blocking collectives, per_device(): swapped = lax.all_to_all(partial.astype(BF16), AXES, 0, 0, tiled=True)  14.7 us
    all_to_all x1, blocking collectives, per_device(): sums = lax.all_to_all(spread, AXES, 0, 0, tiled=True)  9.19 us
    pallas_call x1, Pallas kernels, per_device(): pl.pallas_call(functools.partial(layer_kernel, tile=tile, chunk=chunk), o...  8.77 us
    pallas_call x1, Pallas kernels, per_device(): pl.pallas_call(functools.partial(early_kernel, tile=tile, chunk=chunk), o...  5.27 us
    ppermute x2, starting transfers between devices, exchanged(): return lax.ppermute(x, AXES, pairs + [(j, i) for i, j in pairs])  3.76 us
    pallas_call x1, Pallas kernels, per_device(): pl.pallas_call(functools.partial(response_kernel, tile=1024), out_shape=(...  2.9 us
    pallas_call x1, Pallas kernels, per_device(): pl.pallas_call(pack_kernel, out_shape=(edge,) * 3 + (pltpu.VMEM(positions...  1.14 us
  transfers between devices with their start and end apart: 2, of which 0 were waited for; matrix products, arithmetic and copies ran while one was open for 0% of the time, Pallas kernels for 13%

profile of v16, /device:TPU:0, one launch (start us, length us, event | category | flops | bytes accessed | tf_op | source)
XLA Modules:
  0.0 47.4 jit_solution(5857632261961852460)
XLA Ops:
  0.6 1.1 %shard_map.103 = (bf16[128,384]{1,0:T(8,128)(2,1)S(1)}, bf16[128,384]{1,0:T(8,128)(2,1)S(1)}, bf16[128,384]{1,0:T(8,128)(2,1)S(1)}, f32[3,256]{1,0:T(4,128)S(1)}, f32[3,16384]{1,0:T(4,128)S(1)}) custom-call(bf16[256,256]{1,0:T(8,128)(2,1)} %feat_ref.1, f32[3,256]{1,0:T(4,128)} %pos_ref.1, s32[64,256]{1,0:T(8,128)} %bitcast.4, s32[1,256]{1,0:T(1,128)} %bitcast.5, ...), custom_call_target="tpu_custom_call" | custom-call | tf_op jit(solution)/shard_map/pallas_call | solution.py:425
  1.8 3.1 %collective-permute-start = (bf16[128,384]{1,0:T(8,128)(2,1)S(1)}, bf16[128,384]{1,0:T(8,128)(2,1)S(1)}, u32[]{:S(2)}, u32[]{:S(2)}) collective-permute-start(bf16[128,384]{1,0:T(8,128)(2,1)S(1)} %get-tuple-element.22), channel_id=1, source_target_pairs={{0,1},{2,3},{4,5},{6,7},{8,9},{10,11},{12,13},{14,15},{16,17},{18,... | collective-permute-start | bytes 294920 | tf_op jit(solution)/shard_map/ppermute | solution.py:408
  4.9 0.8 %shard_map.104 = (bf16[128,384]{1,0:T(8,128)(2,1)S(1)}, f32[8,16384]{1,0:T(8,128)S(1)}, f32[256,128]{1,0:T(8,128)S(1)}) custom-call(f32[3,16384]{1,0:T(4,128)S(1)} %get-tuple-element.25.wave_ref, bf16[128,384]{1,0:T(8,128)(2,1)S(1)} %get-tuple-element.23.first_ref, bf16[128,384]{1,0:T(8,128)(2,1)S(1)} %get-tuple-element.24.last_ref), custom_call_target="tpu_custom_call" | custom-call | flops 16777216 | bytes 4194304 | tf_op jit(solution)/shard_map/pallas_call | solution.py:438
  5.7 0.7 %collective-permute-start.1 = (bf16[128,384]{1,0:T(8,128)(2,1)S(1)}, bf16[128,384]{1,0:T(8,128)(2,1)S(1)}, u32[]{:S(2)}, u32[]{:S(2)}) collective-permute-start(bf16[128,384]{1,0:T(8,128)(2,1)S(1)} %get-tuple-element.26), channel_id=1, source_target_pairs={{1,2},{3,4},{5,6},{7,8},{9,10},{11,12},{13,14},{15,16},{17,18},{19... | collective-permute-start | bytes 294920 | tf_op jit(solution)/shard_map/ppermute | solution.py:408
  6.4 5.3 %shard_map.105 = (bf16[7168,256]{1,0:T(8,128)(2,1)S(1)}, bf16[7168,256]{1,0:T(8,128)(2,1)S(1)}, bf16[2,256,256]{2,1,0:T(8,128)(2,1)S(1)}, bf16[2,256,256]{2,1,0:T(8,128)(2,1)S(1)}, f32[1,256]{1,0:T(1,128)S(1)}) custom-call(f32[3,256]{1,0:T(4,128)S(1)} %get-tuple-element.27.pos_ref, f32[3,16384]{1,0:T(4,128)S(1)} %get-tuple-element.25.wave_ref, ...), custom_call_target="tpu_custom_call" | custom-call | flops 73400320 | bytes 7340032 | tf_op jit(solution)/shard_map/pallas_call | solution.py:456
  11.6 0.0 collective-permute-done.near_ref
  11.6 0.0 collective-permute-done.1.far_ref
  11.6 8.8 %shard_map.106 = (bf16[256,256]{1,0:T(8,128)(2,1)}, f32[32,2,512]{2,1,0:T(2,128)S(1)}, bf16[9216,256]{1,0:T(8,128)(2,1)S(1)}, bf16[9216,256]{1,0:T(8,128)(2,1)S(1)}) custom-call(bf16[128,384]{1,0:T(8,128)(2,1)S(1)} %collective-permute-done.near_ref, bf16[128,384]{1,0:T(8,128)(2,1)S(1)} %get-tuple-element.23.first_ref, ...), custom_call_target="tpu_custom_call" | custom-call | tf_op jit(solution)/shard_map/pallas_call | solution.py:475
  20.5 14.7 %all_to_all.10.parts_ref = bf16[32,2,512]{2,1,0:T(2,128)(2,1)S(1)} all-to-all(bf16[32,2,512]{2,1,0:T(2,128)(2,1)S(1)} %convert_element_type.3), channel_id=1, replica_groups=mesh['brick'=8,'kvec'=4] {'brick','kvec'}, dimensions={0} | all-to-all | bytes 131072 | tf_op jit(solution)/shard_map/all_to_all | solution.py:500
  35.2 0.1 shard_map.107
  35.3 9.2 %all_to_all.11.sums_ref = bf16[32,2,512]{2,1,0:T(2,128)(2,1)S(1)} all-to-all(bf16[32,2,512]{2,1,0:T(2,128)(2,1)S(1)} %shard_map.107), channel_id=1, replica_groups=mesh['brick'=8,'kvec'=4] {'brick','kvec'}, dimensions={0} | all-to-all | bytes 131072 | tf_op jit(solution)/shard_map/all_to_all | solution.py:508
  44.5 2.9 %shard_map.108 = (f32[1,256]{1,0:T(1,128)}, f32[3,256]{1,0:T(4,128)}) custom-call(bf16[32,2,512]{2,1,0:T(2,128)(2,1)S(1)} %all_to_all.11.sums_ref, f32[8,16384]{1,0:T(8,128)S(1)} %get-tuple-element.36.coef_ref, bf16[7168,256]{1,0:T(8,128)(2,1)S(1)} %get-tuple-element.32.cos_head_ref, bf16[7168,256]{1,0:T(8,128)(2,1)S(1)} %get-tuple-element.33.sin_head_ref, ...), custom_call_target="tpu_custom_call" | custom-call | tf_op jit(solution)/shard_map/pallas_call | solution.py:514
  (1 shorter events, 0.0 us)
Async XLA Ops:
  1.8 9.9 %collective-permute-start = (bf16[128,384]{1,0:T(8,128)(2,1)S(1)}, bf16[128,384]{1,0:T(8,128)(2,1)S(1)}, u32[]{:S(2)}, u32[]{:S(2)}) collective-permute-start(bf16[128,384]{1,0:T(8,128)(2,1)S(1)} %get-tuple-element.22), channel_id=1, source_target_pairs={{0,1},{2,3},{4,5},{6,7},{8,9},{10,11},{12,13},{14,15},{16,17},{18,... | collective-permute-start | bytes 294920 | tf_op jit(solution)/shard_map/ppermute | solution.py:408
  5.7 6.0 %collective-permute-start.1 = (bf16[128,384]{1,0:T(8,128)(2,1)S(1)}, bf16[128,384]{1,0:T(8,128)(2,1)S(1)}, u32[]{:S(2)}, u32[]{:S(2)}) collective-permute-start(bf16[128,384]{1,0:T(8,128)(2,1)S(1)} %get-tuple-element.26), channel_id=1, source_target_pairs={{1,2},{3,4},{5,6},{7,8},{9,10},{11,12},{13,14},{15,16},{17,18},{19... | collective-permute-start | bytes 294920 | tf_op jit(solution)/shard_map/ppermute | solution.py:408

commit v17 on v15

--- a/solution.py
+++ b/solution.py
@@ -214,8 +214,12 @@
     odd_tile_ref, final_ref, before_ref, after_ref, sem, *, tile, chunk,
 ):
     even = even_device()
-    before_ref[...] = chosen(even, far_ref[...], near_ref[...])
-    after_ref[...] = chosen(even, near_ref[...], far_ref[...])
+    index = lax.axis_index("brick") * lax.axis_size("kvec") + lax.axis_index("kvec")
+    last = lax.axis_size("brick") * lax.axis_size("kvec") - 1
+    absent = jnp.zeros(far_ref.shape, BF16)
+    far = chosen((index == 0) | (index == last), absent, far_ref[...])
+    before_ref[...] = chosen(even, far, near_ref[...])
+    after_ref[...] = chosen(even, near_ref[...], far)
     parts = (before_ref, first_ref, last_ref, after_ref)
     half = before_ref.shape[0]
     channels = w_in_ref.shape[1]
@@ -400,7 +404,7 @@
 
 def exchanged(x, start):
     devices = lax.axis_size(AXES)
-    pairs = [(i, i + 1) for i in range(start, devices - 1, 2)]
+    pairs = [(i, (i + 1) % devices) for i in range(start, devices, 2)]
     return lax.ppermute(x, AXES, pairs + [(j, i) for i, j in pairs])
 
 

time: 46.9 us -> 45 us (0.959)
  blocking collectives: 23.5 us -> 18.8 us
  starting transfers between devices: 3.74 us -> 6.61 us
    all_to_all x1, blocking collectives: 14.3 us -> 9.61 us  [per_device(): swapped = lax.all_to_all(partial.astype(BF16), AXES, 0, 0, tiled=True)]
    ppermute x2, starting transfers between devices: 3.74 us -> 6.61 us  [exchanged(): return lax.ppermute(x, AXES, pairs + [(j, i) for i, j in pairs])]
  transfers between devices with their start and end apart: 2 -> 2, of which waited for: 0 -> 0; matrix products, arithmetic and copies ran while one was open for 0% -> 0% of each run, Pallas kernels for 12% -> 13%
where the time goes in v17:
time: 45 us; the launch traced here: 44.8 us
  blocking collectives  18.8 us (42%)
  Pallas kernels  18.6 us (41%)
  starting transfers between devices  6.61 us (15%)
  between operations  0.68 us (2%)
    all_to_all x1, blocking collectives, per_device(): swapped = lax.all_to_all(partial.astype(BF16), AXES, 0, 0, tiled=True)  9.61 us
    all_to_all x1, blocking collectives, per_device(): sums = lax.all_to_all(spread, AXES, 0, 0, tiled=True)  9.19 us
    pallas_call x1, Pallas kernels, per_device(): pl.pallas_call(functools.partial(layer_kernel, tile=tile, chunk=chunk), o...  8.74 us
    ppermute x2, starting transfers between devices, exchanged(): return lax.ppermute(x, AXES, pairs + [(j, i) for i, j in pairs])  6.61 us
    pallas_call x1, Pallas kernels, per_device(): pl.pallas_call(functools.partial(early_kernel, tile=tile, chunk=chunk, fa...  5.78 us
    pallas_call x1, Pallas kernels, per_device(): pl.pallas_call(functools.partial(response_kernel, tile=1024), out_shape=(...  2.9 us
    pallas_call x1, Pallas kernels, per_device(): pl.pallas_call(pack_kernel, out_shape=(edge,) * 4 + (pltpu.VMEM(positions...  1.14 us
  transfers between devices with their start and end apart: 2, of which 0 were waited for; matrix products, arithmetic and copies ran while one was open for 0% of the time, Pallas kernels for 13%

profile of v17, /device:TPU:0, one launch (start us, length us, event | category | flops | bytes accessed | tf_op | source)
XLA Modules:
  0.0 44.8 jit_solution(2652840112445813683)
XLA Ops:
  0.6 1.1 %shard_map.103 = (bf16[128,384]{1,0:T(8,128)(2,1)S(1)}, bf16[128,384]{1,0:T(8,128)(2,1)S(1)}, bf16[128,384]{1,0:T(8,128)(2,1)S(1)}, bf16[128,384]{1,0:T(8,128)(2...) custom-call(bf16[256,256]{1,0:T(8,128)(2,1)} %feat_ref.1, f32[3,256]{1,0:T(4,128)} %pos_ref.1, s32[64,256]{1,0:T(8,128)} %bitcast.4, ...), custom_call_target="tpu_custom_call" | custom-call | tf_op jit(solution)/shard_map/pallas_call | solution.py:425
  1.8 3.1 %collective-permute-start = (bf16[128,384]{1,0:T(8,128)(2,1)S(1)}, bf16[128,384]{1,0:T(8,128)(2,1)S(1)}, u32[]{:S(2)}, u32[]{:S(2)}) collective-permute-start(bf16[128,384]{1,0:T(8,128)(2,1)S(1)} %get-tuple-element.22), channel_id=1, source_target_pairs={{0,1},{2,3},{4,5},{6,7},{8,9},{10,11},{12,13},{14,15},{16,17},{18,... | collective-permute-start | bytes 294920 | tf_op jit(solution)/shard_map/ppermute | solution.py:408
  4.9 3.5 %collective-permute-start.1 = (bf16[128,384]{1,0:T(8,128)(2,1)S(1)}, bf16[128,384]{1,0:T(8,128)(2,1)S(1)}, u32[]{:S(2)}, u32[]{:S(2)}) collective-permute-start(bf16[128,384]{1,0:T(8,128)(2,1)S(1)} %get-tuple-element.25), channel_id=1, source_target_pairs={{1,2},{3,4},{5,6},{7,8},{9,10},{11,12},{13,14},{15,16},{17,18},{19... | collective-permute-start | bytes 294920 | tf_op jit(solution)/shard_map/ppermute | solution.py:408
  8.4 5.8 %shard_map.104 = (bf16[7168,256]{1,0:T(8,128)(2,1)S(1)}, bf16[7168,256]{1,0:T(8,128)(2,1)S(1)}, f32[8,16384]{1,0:T(8,128)S(1)}, f32[256,128]{1,0:T(8,128)S(1)}, ...) custom-call(f32[3,256]{1,0:T(4,128)S(1)} %get-tuple-element.26.pos_ref, ...), custom_call_target="tpu_custom_call" | custom-call | flops 73400320 | bytes 7340032 | tf_op jit(solution)/shard_map/pallas_call | solution.py:446
  14.2 0.0 collective-permute-done.near_ref
  14.2 0.0 collective-permute-done.1.far_ref
  14.2 8.7 %shard_map.105 = (bf16[256,256]{1,0:T(8,128)(2,1)}, f32[32,2,512]{2,1,0:T(2,128)S(1)}, bf16[9216,256]{1,0:T(8,128)(2,1)S(1)}, bf16[9216,256]{1,0:T(8,128)(2,1)S(1)}) custom-call(bf16[128,384]{1,0:T(8,128)(2,1)S(1)} %collective-permute-done.near_ref, bf16[128,384]{1,0:T(8,128)(2,1)S(1)} %get-tuple-element.23.first_ref, ...), custom_call_target="tpu_custom_call" | custom-call | tf_op jit(solution)/shard_map/pallas_call | solution.py:467
  23.0 9.6 %all_to_all.10.parts_ref = bf16[32,2,512]{2,1,0:T(2,128)(2,1)S(1)} all-to-all(bf16[32,2,512]{2,1,0:T(2,128)(2,1)S(1)} %convert_element_type.3), channel_id=1, replica_groups=mesh['brick'=8,'kvec'=4] {'brick','kvec'}, dimensions={0} | all-to-all | bytes 131072 | tf_op jit(solution)/shard_map/all_to_all | solution.py:492
  32.6 0.1 shard_map.106
  32.7 9.2 %all_to_all.11.sums_ref = bf16[32,2,512]{2,1,0:T(2,128)(2,1)S(1)} all-to-all(bf16[32,2,512]{2,1,0:T(2,128)(2,1)S(1)} %shard_map.106), channel_id=1, replica_groups=mesh['brick'=8,'kvec'=4] {'brick','kvec'}, dimensions={0} | all-to-all | bytes 131072 | tf_op jit(solution)/shard_map/all_to_all | solution.py:500
  41.9 2.9 %shard_map.107 = (f32[1,256]{1,0:T(1,128)}, f32[3,256]{1,0:T(4,128)}) custom-call(bf16[32,2,512]{2,1,0:T(2,128)(2,1)S(1)} %all_to_all.11.sums_ref, f32[8,16384]{1,0:T(8,128)S(1)} %get-tuple-element.36.coef_ref, bf16[7168,256]{1,0:T(8,128)(2,1)S(1)} %get-tuple-element.32.cos_head_ref, bf16[7168,256]{1,0:T(8,128)(2,1)S(1)} %get-tuple-element.33.sin_head_ref, ...), custom_call_target="tpu_custom_call" | custom-call | tf_op jit(solution)/shard_map/pallas_call | solution.py:506
  (1 shorter events, 0.0 us)
Async XLA Ops:
  1.8 12.4 %collective-permute-start = (bf16[128,384]{1,0:T(8,128)(2,1)S(1)}, bf16[128,384]{1,0:T(8,128)(2,1)S(1)}, u32[]{:S(2)}, u32[]{:S(2)}) collective-permute-start(bf16[128,384]{1,0:T(8,128)(2,1)S(1)} %get-tuple-element.22), channel_id=1, source_target_pairs={{0,1},{2,3},{4,5},{6,7},{8,9},{10,11},{12,13},{14,15},{16,17},{18,... | collective-permute-start | bytes 294920 | tf_op jit(solution)/shard_map/ppermute | solution.py:408
  4.9 9.3 %collective-permute-start.1 = (bf16[128,384]{1,0:T(8,128)(2,1)S(1)}, bf16[128,384]{1,0:T(8,128)(2,1)S(1)}, u32[]{:S(2)}, u32[]{:S(2)}) collective-permute-start(bf16[128,384]{1,0:T(8,128)(2,1)S(1)} %get-tuple-element.25), channel_id=1, source_target_pairs={{1,2},{3,4},{5,6},{7,8},{9,10},{11,12},{13,14},{15,16},{17,18},{19... | collective-permute-start | bytes 294920 | tf_op jit(solution)/shard_map/ppermute | solution.py:408

commit v18 on v17

--- a/solution.py
+++ b/solution.py
@@ -434,8 +434,8 @@
             dma((6,)),
         ],
     )(*(in_hbm(x) for x in (features, positions, neighbours.T, counts.reshape(1, own))), wave)
+    far = exchanged(far, 1)
     near = exchanged(near, 0)
-    far = exchanged(far, 1)
 
     tile, chunk = 256, 32
     early = (total - 8 * tile) // 2

time: 45 us -> 45 us (level)
  no operation moved by 1% of the time
where the time goes in v18:
time: 45 us; the launch traced here: 44.8 us
  blocking collectives  18.8 us (42%)
  Pallas kernels  18.6 us (41%)
  starting transfers between devices  6.61 us (15%)
  between operations  0.68 us (2%)
    all_to_all x1, blocking collectives, per_device(): swapped = lax.all_to_all(partial.astype(BF16), AXES, 0, 0, tiled=True)  9.61 us
    all_to_all x1, blocking collectives, per_device(): sums = lax.all_to_all(spread, AXES, 0, 0, tiled=True)  9.19 us
    pallas_call x1, Pallas kernels, per_device(): pl.pallas_call(functools.partial(layer_kernel, tile=tile, chunk=chunk), o...  8.74 us
    ppermute x2, starting transfers between devices, exchanged(): return lax.ppermute(x, AXES, pairs + [(j, i) for i, j in pairs])  6.61 us
    pallas_call x1, Pallas kernels, per_device(): pl.pallas_call(functools.partial(early_kernel, tile=tile, chunk=chunk, fa...  5.78 us
    pallas_call x1, Pallas kernels, per_device(): pl.pallas_call(functools.partial(response_kernel, tile=1024), out_shape=(...  2.9 us
    pallas_call x1, Pallas kernels, per_device(): pl.pallas_call(pack_kernel, out_shape=(edge,) * 4 + (pltpu.VMEM(positions...  1.14 us
  transfers between devices with their start and end apart: 2, of which 0 were waited for; matrix products, arithmetic and copies ran while one was open for 0% of the time, Pallas kernels for 13%

profile of v18, /device:TPU:0, one launch (start us, length us, event | category | flops | bytes accessed | tf_op | source)
XLA Modules:
  0.0 44.8 jit_solution(2652840112445813683)
XLA Ops:
  0.6 1.1 %shard_map.103 = (bf16[128,384]{1,0:T(8,128)(2,1)S(1)}, bf16[128,384]{1,0:T(8,128)(2,1)S(1)}, bf16[128,384]{1,0:T(8,128)(2,1)S(1)}, bf16[128,384]{1,0:T(8,128)(2...) custom-call(bf16[256,256]{1,0:T(8,128)(2,1)} %feat_ref.1, f32[3,256]{1,0:T(4,128)} %pos_ref.1, s32[64,256]{1,0:T(8,128)} %bitcast.4, ...), custom_call_target="tpu_custom_call" | custom-call | tf_op jit(solution)/shard_map/pallas_call | solution.py:425
  1.8 3.1 %collective-permute-start = (bf16[128,384]{1,0:T(8,128)(2,1)S(1)}, bf16[128,384]{1,0:T(8,128)(2,1)S(1)}, u32[]{:S(2)}, u32[]{:S(2)}) collective-permute-start(bf16[128,384]{1,0:T(8,128)(2,1)S(1)} %get-tuple-element.22), channel_id=1, source_target_pairs={{0,1},{2,3},{4,5},{6,7},{8,9},{10,11},{12,13},{14,15},{16,17},{18,... | collective-permute-start | bytes 294920 | tf_op jit(solution)/shard_map/ppermute | solution.py:408
  4.9 3.5 %collective-permute-start.1 = (bf16[128,384]{1,0:T(8,128)(2,1)S(1)}, bf16[128,384]{1,0:T(8,128)(2,1)S(1)}, u32[]{:S(2)}, u32[]{:S(2)}) collective-permute-start(bf16[128,384]{1,0:T(8,128)(2,1)S(1)} %get-tuple-element.25), channel_id=1, source_target_pairs={{1,2},{3,4},{5,6},{7,8},{9,10},{11,12},{13,14},{15,16},{17,18},{19... | collective-permute-start | bytes 294920 | tf_op jit(solution)/shard_map/ppermute | solution.py:408
  8.4 5.8 %shard_map.104 = (bf16[7168,256]{1,0:T(8,128)(2,1)S(1)}, bf16[7168,256]{1,0:T(8,128)(2,1)S(1)}, f32[8,16384]{1,0:T(8,128)S(1)}, f32[256,128]{1,0:T(8,128)S(1)}, ...) custom-call(f32[3,256]{1,0:T(4,128)S(1)} %get-tuple-element.26.pos_ref, ...), custom_call_target="tpu_custom_call" | custom-call | flops 73400320 | bytes 7340032 | tf_op jit(solution)/shard_map/pallas_call | solution.py:446
  14.2 0.0 collective-permute-done.near_ref
  14.2 0.0 collective-permute-done.1.far_ref
  14.2 8.7 %shard_map.105 = (bf16[256,256]{1,0:T(8,128)(2,1)}, f32[32,2,512]{2,1,0:T(2,128)S(1)}, bf16[9216,256]{1,0:T(8,128)(2,1)S(1)}, bf16[9216,256]{1,0:T(8,128)(2,1)S(1)}) custom-call(bf16[128,384]{1,0:T(8,128)(2,1)S(1)} %collective-permute-done.near_ref, bf16[128,384]{1,0:T(8,128)(2,1)S(1)} %get-tuple-element.23.first_ref, ...), custom_call_target="tpu_custom_call" | custom-call | tf_op jit(solution)/shard_map/pallas_call | solution.py:467
  23.0 9.6 %all_to_all.10.parts_ref = bf16[32,2,512]{2,1,0:T(2,128)(2,1)S(1)} all-to-all(bf16[32,2,512]{2,1,0:T(2,128)(2,1)S(1)} %convert_element_type.3), channel_id=1, replica_groups=mesh['brick'=8,'kvec'=4] {'brick','kvec'}, dimensions={0} | all-to-all | bytes 131072 | tf_op jit(solution)/shard_map/all_to_all | solution.py:492
  32.6 0.1 shard_map.106
  32.7 9.2 %all_to_all.11.sums_ref = bf16[32,2,512]{2,1,0:T(2,128)(2,1)S(1)} all-to-all(bf16[32,2,512]{2,1,0:T(2,128)(2,1)S(1)} %shard_map.106), channel_id=1, replica_groups=mesh['brick'=8,'kvec'=4] {'brick','kvec'}, dimensions={0} | all-to-all | bytes 131072 | tf_op jit(solution)/shard_map/all_to_all | solution.py:500
  41.9 2.9 %shard_map.107 = (f32[1,256]{1,0:T(1,128)}, f32[3,256]{1,0:T(4,128)}) custom-call(bf16[32,2,512]{2,1,0:T(2,128)(2,1)S(1)} %all_to_all.11.sums_ref, f32[8,16384]{1,0:T(8,128)S(1)} %get-tuple-element.36.coef_ref, bf16[7168,256]{1,0:T(8,128)(2,1)S(1)} %get-tuple-element.32.cos_head_ref, bf16[7168,256]{1,0:T(8,128)(2,1)S(1)} %get-tuple-element.33.sin_head_ref, ...), custom_call_target="tpu_custom_call" | custom-call | tf_op jit(solution)/shard_map/pallas_call | solution.py:506
  (1 shorter events, 0.0 us)
Async XLA Ops:
  1.8 12.4 %collective-permute-start = (bf16[128,384]{1,0:T(8,128)(2,1)S(1)}, bf16[128,384]{1,0:T(8,128)(2,1)S(1)}, u32[]{:S(2)}, u32[]{:S(2)}) collective-permute-start(bf16[128,384]{1,0:T(8,128)(2,1)S(1)} %get-tuple-element.22), channel_id=1, source_target_pairs={{0,1},{2,3},{4,5},{6,7},{8,9},{10,11},{12,13},{14,15},{16,17},{18,... | collective-permute-start | bytes 294920 | tf_op jit(solution)/shard_map/ppermute | solution.py:408
  4.9 9.3 %collective-permute-start.1 = (bf16[128,384]{1,0:T(8,128)(2,1)S(1)}, bf16[128,384]{1,0:T(8,128)(2,1)S(1)}, u32[]{:S(2)}, u32[]{:S(2)}) collective-permute-start(bf16[128,384]{1,0:T(8,128)(2,1)S(1)} %get-tuple-element.25), channel_id=1, source_target_pairs={{1,2},{3,4},{5,6},{7,8},{9,10},{11,12},{13,14},{15,16},{17,18},{19... | collective-permute-start | bytes 294920 | tf_op jit(solution)/shard_map/ppermute | solution.py:408
